TPU v7x, 128 devices: a whole 4x4x4 slice. The times are simulated.
128 devices in a mesh: loop: 32 (over x, z, y_lo), feat: 4 (over y_hi, core).
Axes of the slice: x: 4, y: 4 (y_hi: 2, y_lo: 2; y = y_hi * 2 + y_lo), z: 4, core: 2. Of those that a mesh axis runs over, the one named last changes fastest.
Arguments:
- features: bfloat16 [262144, 128], P('loop', 'feat'), may hold values from -6 to 6
- band_blocks: bfloat16 [2048, 3, 128, 128], P('loop'), may hold values from 0 to 1.5, as said below
- off_blocks: bfloat16 [2048, 128, 128], P('loop'), may hold values from 0 to 1.5, as said below
- off_row: int32 [2048], P('loop'), may hold values from 0 to 63
- off_col: int32 [2048], P('loop'), may hold values from 0 to 63
- off_part: int32 [2048, 1], P('loop'), may hold values from 0 to 31; in each aligned block of 64 rows (0 to 63, 64 to 127, ...) at most 4 rows name the same one
- w_self: bfloat16 [128, 256], P('feat'), may hold values from -0.5 to 0.5
- w_neigh: bfloat16 [128, 256], P('feat'), may hold values from -4 to 4
- bias: float32 [256], P('feat'), may hold values from -3 to 3
- cotangent: bfloat16 [262144, 256], P('loop', 'feat'), may hold values from -6 to 6
Outputs:
- hidden: bfloat16 [262144, 256], P('loop', 'feat')
- grad_features: bfloat16 [262144, 128], P('loop', 'feat')
- weight_grads: float32 [2, 128, 256], P(None, 'feat')
- bias_grad: float32 [256], P('feat')
Inputs may be any that keep to these rules, and one draw needn't show every extreme that they name: `band_blocks`: nonnegative edge weights; zero or between 0.5 and 1.5. `off_blocks`: nonnegative edge weights; zero or between 0.5 and 1.5. `off_part`: off-band block g belongs to partition g // 64; among the blocks of one partition at most 4 have their columns in any one partition.
All inputs are finite; a program needn't handle non-finite values.
Results may differ from a plain program's by a relative error of at most 0.007.
Values may be sent and summed in bfloat16 or wider, within the bound.
No kernel may reach another device: no remote copies, remote signals or barrier semaphores. Data moves between devices by JAX's collectives and lax.ppermute only.
A program may use at most 128 MiB of HBM per device.

v0:
```python
import math

import jax
import jax.numpy as jnp
from jax import lax
from jax.sharding import PartitionSpec as P


def with_halo(block, sides, width):
    for axis, dim in sides:
        count = lax.axis_size(axis)
        forward = [(i, i + 1) for i in range(count - 1)]
        forward.append((count - 1, 0))
        backward = [(target, source) for source, target in forward]
        low = lax.ppermute(
            lax.slice_in_dim(block, block.shape[dim] - width, None, axis=dim), axis, forward
        )
        high = lax.ppermute(lax.slice_in_dim(block, 0, width, axis=dim), axis, backward)
        block = jnp.concatenate([low, block, high], axis=dim)
    return block


def per_device(
    features, band_blocks, off_blocks, off_row, off_col, off_part, w_self, w_neigh, bias, cotangent
):
    node_rows, feat_cols = features.shape
    block_size = band_blocks.shape[2]
    row_blocks = node_rows // block_size
    off_count = off_blocks.shape[0]
    loop_size = lax.axis_size("loop")
    capacity = max(2, 2 * off_count // loop_size)
    degree = 1.0 + jnp.sum(band_blocks, axis=(1, 3), dtype=jnp.float32)
    off_sums = jnp.sum(off_blocks, axis=2, dtype=jnp.float32)
    degree = degree.at[off_row].add(off_sums)
    inverse = 1.0 / degree
    owner_part = off_part[:, 0]
    owner_hits = (owner_part[:, None] == jnp.arange(loop_size, dtype=jnp.int32)[None, :]).astype(
        jnp.int32
    )
    slot_index = jnp.sum((jnp.cumsum(owner_hits, axis=0) - 1) * owner_hits, axis=1)
    padded = with_halo(features, (("loop", 0),), block_size)
    padded_blocks = padded.reshape(row_blocks + 2, block_size, feat_cols)
    stacked = jnp.stack([padded_blocks[:-2], padded_blocks[1:-1], padded_blocks[2:]], 1)
    aggregate = jnp.einsum(
        "bokj,bojf->bkf", band_blocks, stacked, preferred_element_type=jnp.float32
    )
    feature_blocks = features.reshape(row_blocks, block_size, feat_cols)
    request = jnp.zeros((loop_size, capacity), jnp.int32).at[owner_part, slot_index].set(off_col)
    asked_columns = lax.all_to_all(request, "loop", split_axis=0, concat_axis=0, tiled=True)
    answer = feature_blocks[asked_columns]
    returned = lax.all_to_all(answer, "loop", split_axis=0, concat_axis=0, tiled=True)
    panels = returned[owner_part, slot_index]
    off_terms = jnp.einsum("gkj,gjf->gkf", off_blocks, panels, preferred_element_type=jnp.float32)
    aggregate = aggregate.at[off_row].add(off_terms)
    mean_feat = (aggregate * inverse[:, :, None]).astype(jnp.bfloat16).reshape(node_rows, feat_cols)
    joined = jnp.concatenate([features, mean_feat], 1)
    joined_weights = jnp.concatenate([w_self, w_neigh], 0)
    partial_sums = jnp.dot(joined, joined_weights, preferred_element_type=jnp.float32)
    pre = lax.psum_scatter(partial_sums, "feat", scatter_dimension=1, tiled=True) + bias
    sigmoid_pre = jax.nn.sigmoid(pre)
    hidden = (pre * sigmoid_pre).astype(jnp.bfloat16)
    grad_pre = (
        cotangent.astype(jnp.float32) * sigmoid_pre * (1.0 + pre * (1.0 - sigmoid_pre))
    ).astype(jnp.bfloat16)
    grad_full = lax.all_gather(grad_pre, "feat", axis=1, tiled=True)
    grad_scale = 1.0 / math.sqrt(node_rows * loop_size)
    contract_rows = (((0,), (0,)), ((), ()))
    self_grad = lax.dot_general(
        features, grad_full, contract_rows, preferred_element_type=jnp.float32
    )
    neigh_grad = lax.dot_general(
        mean_feat, grad_full, contract_rows, preferred_element_type=jnp.float32
    )
    bias_local = jnp.sum(grad_pre, axis=0, dtype=jnp.float32)
    weight_grads, bias_grad = lax.psum(
        (jnp.stack([self_grad, neigh_grad]) * grad_scale, bias_local * grad_scale), "loop"
    )
    contract_cols = (((1,), (1,)), ((), ()))
    back_mean = (
        lax.dot_general(
            grad_full, w_neigh, contract_cols, preferred_element_type=jnp.float32
        ).reshape(row_blocks, block_size, feat_cols)
        * inverse[:, :, None]
    ).astype(jnp.bfloat16)
    self_part = lax.dot_general(
        grad_full, w_self, contract_cols, preferred_element_type=jnp.float32
    )
    terms = jnp.einsum("bokj,bkf->bojf", band_blocks, back_mean, preferred_element_type=jnp.float32)
    edge_terms = jnp.concatenate([terms[0, 0], terms[row_blocks - 1, 2]], 0)
    rim_terms = with_halo(edge_terms.astype(jnp.bfloat16), (("loop", 0),), block_size).astype(
        edge_terms.dtype
    )
    band_back = terms[:, 1]
    band_back = band_back.at[:-1].add(terms[1:, 0])
    band_back = band_back.at[1:].add(terms[:-1, 2])
    band_back = band_back.at[0].add(rim_terms[:block_size])
    band_back = band_back.at[row_blocks - 1].add(rim_terms[3 * block_size :])
    off_back = jnp.einsum(
        "gkj,gkf->gjf", off_blocks, back_mean[off_row], preferred_element_type=jnp.float32
    )
    outgoing = (
        jnp.zeros((loop_size, capacity, block_size, feat_cols), jnp.float32)
        .at[owner_part, slot_index]
        .set(off_back)
    )
    outgoing_cols = (
        jnp.zeros((loop_size, capacity), jnp.int32).at[owner_part, slot_index].set(off_col)
    )
    incoming, incoming_cols = (
        lax.all_to_all(outgoing, "loop", split_axis=0, concat_axis=0, tiled=True),
        lax.all_to_all(outgoing_cols, "loop", split_axis=0, concat_axis=0, tiled=True),
    )
    band_back = band_back.at[incoming_cols.reshape(-1)].add(
        incoming.reshape(-1, block_size, feat_cols)
    )
    grad_features = (self_part + band_back.reshape(node_rows, feat_cols)).astype(jnp.bfloat16)
    return (hidden, grad_features, weight_grads, bias_grad)


def solution(mesh):
    return jax.shard_map(
        per_device,
        mesh=mesh,
        in_specs=(
            P("loop", "feat"),
            P("loop", None, None, None),
            P("loop", None, None),
            P("loop"),
            P("loop"),
            P("loop", None),
            P("feat", None),
            P("feat", None),
            P("feat"),
            P("loop", "feat"),
        ),
        out_specs=(P("loop", "feat"), P("loop", "feat"), P(None, "feat", None), P("feat")),
        check_vma=False,
    )
```

profile of v0, /device:TPU:0, one launch (start us, length us, event | category | flops | bytes accessed | tf_op | source)
XLA Modules:
  0.0 529.1 jit_solution(13774646536607233449)
XLA Ops:
  7.9 1.7 collective-permute-start
  9.5 5.7 %collective-permute-start.1 = (bf16[128,32]{0,1:T(8,128)(2,1)S(1)}, bf16[128,32]{0,1:T(8,128)(2,1)S(1)}, u32[]{:S(2)}, u32[]{:S(2)}) collective-permute-start(bf16[128,32]{0,1:T(8,128)(2,1)S(1)} %get-tuple-element.62), channel_id=1, source_target_pairs={{4,0},{8,4},{12,8},{16,12},{20,16},{24,20},{28,24},{32,28},{36,32}... | collective-permute-start | bytes 24584 | tf_op jit(solution)/shard_map/ppermute | solution.py:18
  17.6 5.8 %scatter_fusion = s32[32,4]{0,1:T(4,128)S(1)} fusion(s32[32,4]{0,1:T(4,128)S(1)} %broadcast.143, s32[64]{0:T(128)S(1)} %get-tuple-element.54, s32[64]{0:T(128)} %param.22), kind=kCustom, calls=%fused_computation.3 | custom fusion | bytes 1280 | tf_op jit(solution)/shard_map/scatter | solution.py:48
  24.0 4.0 all-to-all-start
  29.1 3.9 convert_reduce_fusion
  33.1 3.0 all-to-all-done
  36.4 1.7 gather_fusion
  38.1 5.7 %all-to-all-start.1 = ((bf16[32,4,128,32]{2,3,1,0:T(8,128)(2,1)}), bf16[32,4,128,32]{2,3,1,0:T(8,128)(2,1)}, u32[]{:S(2)}, u32[]{:S(2)}) async-start(bf16[32,4,128,32]{2,3,1,0:T(8,128)(2,1)} %bitcast.8), calls=%async_computation.1 | async-start | bytes 2097152 | tf_op jit(solution)/shard_map/all_to_all | solution.py:51
  47.0 5.1 fusion.7
  52.1 8.5 %all-to-all-done.1 = bf16[32,4,128,32]{2,3,1,0:T(8,128)(2,1)} async-done(((bf16[32,4,128,32]{2,3,1,0:T(8,128)(2,1)}), bf16[32,4,128,32]{2,3,1,0:T(8,128)(2,1)}, u32[]{:S(2)}, u32[]{:S(2)}) %all-to-all-start.1) | async-done | bytes 1048608 | tf_op jit(solution)/shard_map/all_to_all | solution.py:51
  60.5 2.7 gather_fusion.1
  63.3 3.2 convolution_bitcast_fusion.2
  66.5 6.1 %scatter_fusion.1 = f32[64,128,32]{1,2,0:T(8,128)S(1)} fusion(f32[64,128,32]{1,2,0:T(8,128)S(1)} %fusion.7, s32[64]{0:T(128)S(1)} %compare_select_fusion.4, f32[64,128,32]{1,2,0:T(8,128)} %convolution_bitcast_fusion.2), kind=kCustom, calls=%fused_computation.4 | custom fusion | flops 262144 | bytes 3145984 | tf_op jit(solution)/shard_map/scatter-add | solution.py:54
  72.7 5.5 %fusion.11 = f32[8192,256]{0,1:T(8,128)} fusion(bf16[8192,32]{0,1:T(8,128)(2,1)S(1)} %copy_bitcast_fusion, bf16[8192,32]{0,1:T(8,128)(2,1)} %param.18, bf16[32,256]{1,0:T(8,128)(2,1)S(1)} %copy-done.7, bf16[32,256]{1,0:T(8,128)(2,1)S(1)} %copy-done.8), kind=kOutput, calls=%fused_computation.32 | convolution fusion | flops 270598144 | bytes 9469952 | tf_op jit(solution)/shard_map/dot_general | solution.py:58
  78.6 76.3 %reduce-scatter.2.cloned.1.call-done = f32[8192,64]{0,1:T(8,128)} async-done(((f32[8192,256]{0,1:T(8,128)}), f32[8192,64]{0,1:T(8,128)}) %reduce-scatter.2.cloned.1.call-update) | async-done | bytes 2097168 | tf_op jit(solution)/shard_map/reduce_scatter | solution.py:59
  154.8 4.4 convert_reduce_fusion.2
  160.7 82.9 %psum.15 = f32[64]{0:T(128)} all-reduce(f32[64]{0:T(128)S(1)} %broadcast_multiply_fusion), channel_id=1, replica_groups=mesh['loop'=32,'feat'=4] {'loop'}, use_global_device_ids=true, to_apply=%region_12.13 | all-reduce | flops 64 | bytes 512 | tf_op jit(solution)/shard_map/psum | solution.py:75
  243.6 3.7 convolution_bitcast_fusion.4
  247.3 1.4 convolution_bitcast_fusion.5
  249.3 3.0 convolution_bitcast_fusion.3
  253.2 1.7 convolution_bitcast_fusion.1
  254.9 1.6 broadcast_in_dim.5
  256.5 8.9 %scatter_fusion.3 = f32[32,4,128,32]{2,3,1,0:T(8,128)} fusion(f32[32,4,128,32]{2,3,1,0:T(8,128)} %broadcast_in_dim.5, s32[64]{0:T(128)S(1)} %get-tuple-element.54, f32[64,128,32]{1,2,0:T(8,128)S(1)} %copy-done.6), kind=kCustom, calls=%fused_computation.6 | custom fusion | bytes 3146240 | tf_op jit(solution)/shard_map/scatter | solution.py:104
  265.4 4.1 all-to-all-start.2
  269.5 4.0 fusion.38
  273.6 1.7 collective-permute-start.2
  275.3 4.6 collective-permute-start.3
  280.5 7.8 %collective-permute-done.2 = bf16[128,32]{0,1:T(8,128)(2,1)S(1)} collective-permute-done((bf16[128,32]{0,1:T(8,128)(2,1)S(1)}, bf16[128,32]{0,1:T(8,128)(2,1)S(1)}, u32[]{:S(2)}, u32[]{:S(2)}) %collective-permute-start.2) | collective-permute-done | bytes 8224 | tf_op jit(solution)/shard_map/ppermute | solution.py:15
  288.3 5.9 %scatter_fusion.4 = f32[64,128,32]{1,2,0:T(8,128)S(1)} fusion(f32[64,128,32]{1,2,0:T(8,128)S(1)} %fusion.28, s32[128]{0:T(128)S(1)} %fusion.32, f32[128,128,32]{1,2,0:T(8,128)S(1)} %bitcast.141), kind=kCustom, calls=%fused_computation.7 | custom fusion | flops 524288 | bytes 6291968 | tf_op jit(solution)/shard_map/scatter-add | solution.py:113
  294.2 3.8 fusion
  298.0 223.1 %all-reduce.2.cloned.1.call-done = f32[2,32,256]{2,1,0:T(8,128)} async-done(((f32[2,32,256]{2,1,0:T(8,128)}), f32[2,32,256]{2,1,0:T(8,128)}) %all-reduce.2.cloned.1.call-update) | async-done | bytes 65552 | tf_op jit(solution)/shard_map/psum | solution.py:75
  521.1 1.5 copy.88
  (74 shorter events, 12.2 us)
Async XLA Ops:
  7.9 38.0 %collective-permute-start = (bf16[128,32]{0,1:T(8,128)(2,1)S(1)}, bf16[128,32]{0,1:T(8,128)(2,1)S(1)}, u32[]{:S(2)}, u32[]{:S(2)}) collective-permute-start(bf16[128,32]{0,1:T(8,128)(2,1)S(1)} %get-tuple-element.61), channel_id=1, source_target_pairs={{0,4},{4,8},{8,12},{12,16},{16,20},{20,24},{24,28},{28,32},{32,36}... | collective-permute-start | bytes 24584 | tf_op jit(solution)/shard_map/ppermute | solution.py:15
  9.5 36.4 %collective-permute-start.1 = (bf16[128,32]{0,1:T(8,128)(2,1)S(1)}, bf16[128,32]{0,1:T(8,128)(2,1)S(1)}, u32[]{:S(2)}, u32[]{:S(2)}) collective-permute-start(bf16[128,32]{0,1:T(8,128)(2,1)S(1)} %get-tuple-element.62), channel_id=1, source_target_pairs={{4,0},{8,4},{12,8},{16,12},{20,16},{24,20},{28,24},{32,28},{36,32}... | collective-permute-start | bytes 24584 | tf_op jit(solution)/shard_map/ppermute | solution.py:18
  24.0 12.1 %all-to-all-start = ((s32[32,1,4]{2,1,0:T(1,128)}), s32[32,1,4]{2,1,0:T(1,128)S(1)}, u32[]{:S(2)}, u32[]{:S(2)}) async-start(s32[32,1,4]{2,1,0:T(1,128)} %copy.49), calls=%async_computation | async-start | bytes 32768 | tf_op jit(solution)/shard_map/all_to_all | solution.py:49
  29.1 4.0 copy-start.10
  38.1 5.7 %copy-start.1 = (bf16[64,128,128]{2,1,0:T(8,128)(2,1)S(1)}, bf16[64,128,128]{2,1,0:T(8,128)(2,1)}, u32[]{:S(2)}) copy-start(bf16[64,128,128]{2,1,0:T(8,128)(2,1)} %param.20) | copy-start | bytes 6291460
  38.1 7.3 %copy-start.4 = (bf16[8192,32]{0,1:T(8,128)(2,1)S(1)}, bf16[8192,32]{0,1:T(8,128)(2,1)}, u32[]{:S(2)}) copy-start(bf16[8192,32]{0,1:T(8,128)(2,1)} %param.18) | copy-start | bytes 1572868
  38.1 22.5 %all-to-all-start.1 = ((bf16[32,4,128,32]{2,3,1,0:T(8,128)(2,1)}), bf16[32,4,128,32]{2,3,1,0:T(8,128)(2,1)}, u32[]{:S(2)}, u32[]{:S(2)}) async-start(bf16[32,4,128,32]{2,3,1,0:T(8,128)(2,1)} %bitcast.8), calls=%async_computation.1 | async-start | bytes 2097152 | tf_op jit(solution)/shard_map/all_to_all | solution.py:51
  43.8 111.1 %reduce-scatter.2.cloned.1.call-start = ((), (), s32[]{:S(2)}) async-start(), calls=%async_computation.4 | async-start | bytes 10485760 | tf_op jit(solution)/shard_map/reduce_scatter | solution.py:59
  66.5 6.2 %copy-start.7 = (bf16[32,256]{1,0:T(8,128)(2,1)S(1)}, bf16[32,256]{1,0:T(8,128)(2,1)}, u32[]{:S(2)}) copy-start(bf16[32,256]{1,0:T(8,128)(2,1)} %param.25) | copy-start | bytes 49156
  66.5 6.2 %copy-start.8 = (bf16[32,256]{1,0:T(8,128)(2,1)S(1)}, bf16[32,256]{1,0:T(8,128)(2,1)}, u32[]{:S(2)}) copy-start(bf16[32,256]{1,0:T(8,128)(2,1)} %param.24) | copy-start | bytes 49156
  78.3 76.5 %copy-start.9 = (f32[64]{0:T(128)S(1)}, f32[64]{0:T(128)}, u32[]{:S(2)}) copy-start(f32[64]{0:T(128)} %param.26) | copy-start | bytes 772
  78.3 165.2 %all-gather.2.cloned.1.call-start = ((), (), s32[]{:S(2)}) async-start(), calls=%async_computation.5 | async-start | bytes 5242880 | tf_op jit(solution)/shard_map/all_gather | solution.py:65
  159.3 361.9 %all-reduce.2.cloned.1.call-start = ((), (), s32[]{:S(2)}) async-start(), calls=%async_computation.6 | async-start | bytes 131072 | tf_op jit(solution)/shard_map/psum | solution.py:75
  243.6 3.7 copy-start
  243.6 3.7 copy-start.5
  252.5 0.8 copy-start.2
  254.9 1.6 copy-start.6
  265.4 4.2 copy-start.3
  265.4 22.9 %all-to-all-start.2 = ((f32[32,4,128,32]{2,3,1,0:T(8,128)}), f32[32,4,128,32]{2,3,1,0:T(8,128)S(1)}, u32[]{:S(2)}, u32[]{:S(2)}) async-start(f32[32,4,128,32]{2,3,1,0:T(8,128)} %scatter_fusion.3), calls=%async_computation.3 | async-start | bytes 4194304 | tf_op jit(solution)/shard_map/all_to_all | solution.py:110
  273.6 14.7 %collective-permute-start.2 = (bf16[128,32]{0,1:T(8,128)(2,1)S(1)}, bf16[128,32]{0,1:T(8,128)(2,1)S(1)}, u32[]{:S(2)}, u32[]{:S(2)}) collective-permute-start(bf16[128,32]{0,1:T(8,128)(2,1)S(1)} %get-tuple-element.57), channel_id=1, source_target_pairs={{0,4},{4,8},{8,12},{12,16},{16,20},{20,24},{24,28},{28,32},{32,36}... | collective-permute-start | bytes 24584 | tf_op jit(solution)/shard_map/ppermute | solution.py:15
  275.3 12.9 %collective-permute-start.3 = (bf16[128,32]{0,1:T(8,128)(2,1)S(1)}, bf16[128,32]{0,1:T(8,128)(2,1)S(1)}, u32[]{:S(2)}, u32[]{:S(2)}) collective-permute-start(bf16[128,32]{0,1:T(8,128)(2,1)S(1)} %get-tuple-element.58), channel_id=1, source_target_pairs={{4,0},{8,4},{12,8},{16,12},{20,16},{24,20},{28,24},{32,28},{36,32}... | collective-permute-start | bytes 24584 | tf_op jit(solution)/shard_map/ppermute | solution.py:18
Sparse Core Ops, SparseCore 0:
  78.4 76.3 reduce-scatter.1
  159.4 38.9 all-gather.1
  249.4 271.6 all-reduce.1
where the time goes:
time: 530 us; the launch traced here: 529 us
  waiting for transfers between devices  319 us (60%)
  blocking collectives  82.9 us (16%)
  matrix products  31.4 us (6%)
  local copies, waits for them, and re-layouts  27.8 us (5%)
  starting transfers between devices  27.7 us (5%)
  other arithmetic  26.5 us (5%)
  between operations  14.1 us (3%)
    psum x1, waiting for transfers between devices, per_device(): lax.psum((jnp.stack([self_grad, neigh_grad]) * grad_scale, bias_local * g...  223 us
    psum x1, blocking collectives, per_device(): lax.psum((jnp.stack([self_grad, neigh_grad]) * grad_scale, bias_local * g...  82.9 us
    reduce_scatter x1, waiting for transfers between devices, per_device(): lax.psum_scatter(partial_sums, 'feat', scatter_dimension=1, tiled=True)  76.3 us
  transfers between devices with their start and end apart: 10, of which 5 were waited for; matrix products, arithmetic and copies ran while one was open for 10% of the time, Pallas kernels for 0%

commit v1 on v0

v1 whole, which is shorter than its diff:
```python
import math

import jax
import jax.numpy as jnp
from jax import lax
from jax.experimental import pallas as pl
from jax.experimental.pallas import tpu as pltpu
from jax.sharding import PartitionSpec as P

BF = jnp.bfloat16
F32 = jnp.float32
BLK = 128
ONES = 16
CAP = 4
NT = (((1,), (1,)), ((), ()))
TN = (((0,), (0,)), ((), ()))


def params(mib=40):
    return pltpu.CompilerParams(vmem_limit_bytes=mib * 1024 * 1024)


def full(shape):
    return pl.BlockSpec(shape, lambda *_: (0,) * len(shape))


def lanes(block, width=BLK):
    return pl.ds(pl.multiple_of(block * BLK, BLK), width)


def dot(a, b, dims=(((1,), (0,)), ((), ()))):
    return lax.dot_general(a, b, dims, preferred_element_type=F32)


def slots_kernel(part_ref, col_ref, key_ref, request_ref):
    part, col = part_ref[...], col_ref[...]
    count = part.shape[1]
    first = lax.broadcasted_iota(jnp.int32, (count, count), 0)
    second = lax.broadcasted_iota(jnp.int32, (count, count), 1)
    part_down = jnp.sum(jnp.where(first == second, part, 0), axis=1, keepdims=True)
    earlier = (part_down == part) & (first < second)
    slot = jnp.sum(earlier.astype(jnp.int32), axis=0, keepdims=True)
    key_ref[...] = part * CAP + slot
    shape = request_ref.shape
    wide = (shape[0], shape[1], count)
    owner = lax.broadcasted_iota(jnp.int32, wide, 0)
    lane = lax.broadcasted_iota(jnp.int32, shape, 2)
    hit = owner == part[None]
    table = jnp.zeros(shape, jnp.int32)
    for s in range(CAP):
        value = jnp.sum(
            jnp.where(hit & (slot[None] == s), col[None], 0), axis=2, keepdims=True
        )
        table = jnp.where(lane == s, value, table)
    request_ref[...] = table


def slots(part, col, loop_size):
    count = part.shape[1]
    return pl.pallas_call(
        slots_kernel,
        out_shape=(
            jax.ShapeDtypeStruct((1, count), jnp.int32),
            jax.ShapeDtypeStruct((loop_size, 8, BLK), jnp.int32),
        ),
        name="slots",
    )(part, col)


def answer_kernel(asked_ref, x_ref, out_ref, table, sem):
    copy = pltpu.make_async_copy(asked_ref.at[:, 0, :], table, sem)
    copy.start()
    copy.wait()

    def body(p, carry):
        for s in range(CAP):
            out_ref[p, s] = x_ref[:, lanes(table[p, s])]
        return carry

    lax.fori_loop(0, out_ref.shape[0], body, 0, unroll=4)


def answers(asked, x):
    loop_size, cols = asked.shape[0], x.shape[0]
    return pl.pallas_call(
        answer_kernel,
        in_specs=[pl.BlockSpec(memory_space=pl.ANY), pl.BlockSpec(memory_space=pltpu.VMEM)],
        out_shape=jax.ShapeDtypeStruct((loop_size, CAP, cols, BLK), BF),
        scratch_shapes=[pltpu.SMEM((loop_size, BLK), jnp.int32), pltpu.SemaphoreType.DMA],
        compiler_params=params(),
        name="answers",
    )(asked, x)


def band_kernel(x_ref, low_ref, high_ref, a_ref, out_ref, wide):
    step = pl.program_id(0)
    cols, rows = x_ref.shape

    @pl.when(step == 0)
    def _():
        wide[0:cols, 0:BLK] = low_ref[...]
        wide[0:cols, BLK : BLK + rows] = x_ref[...]
        wide[0:cols, BLK + rows :] = high_ref[...]
        wide[cols:, :] = jnp.ones((ONES, wide.shape[1]), BF)

    group = a_ref.shape[0]
    for r in range(group):
        left = wide[:, lanes(step * group + r, 3 * BLK)]
        right = jnp.concatenate([a_ref[r, 0], a_ref[r, 1], a_ref[r, 2]], axis=1)
        out_ref[:, r * BLK : (r + 1) * BLK] = dot(left, right, NT)


def band_forward(x, low, high, band):
    cols, rows = x.shape
    blocks, group = band.shape[0], 8
    return pl.pallas_call(
        band_kernel,
        grid=(blocks // group,),
        in_specs=[
            full((cols, rows)),
            full((cols, BLK)),
            full((cols, BLK)),
            pl.BlockSpec((group, 3, BLK, BLK), lambda i: (i, 0, 0, 0)),
        ],
        out_specs=pl.BlockSpec((cols + ONES, group * BLK), lambda i: (0, i)),
        out_shape=jax.ShapeDtypeStruct((cols + ONES, rows), F32),
        scratch_shapes=[pltpu.VMEM((cols + ONES, rows + 2 * BLK), BF)],
        compiler_params=params(),
        cost_estimate=pl.CostEstimate(
            flops=2 * 48 * 3 * BLK * rows, bytes_accessed=9 * 1024 * 1024, transcendentals=0
        ),
        name="band_forward",
    )(x, low, high, band)


def off_kernel(row_ref, key_ref, band_ref, panel_ref, a_ref, mean_ref, inverse_ref, total):
    step = pl.program_id(0)
    cols = panel_ref.shape[1]
    group = a_ref.shape[0]

    @pl.when(step == 0)
    def _():
        total[...] = band_ref[...]

    ones = jnp.ones((ONES, BLK), BF)
    for start in range(0, group, 8):
        terms = []
        for r in range(start, start + 8):
            left = jnp.concatenate([panel_ref[key_ref[0, step * group + r]], ones], axis=0)
            terms.append(dot(left, a_ref[r], NT))
        for r in range(start, start + 8):
            where = lanes(row_ref[step * group + r])
            total[:, where] = total[:, where] + terms[r - start]

    @pl.when(step == pl.num_programs(0) - 1)
    def _():
        width = 8 * BLK
        for start in range(0, total.shape[1], width):
            inverse = 1.0 / (1.0 + total[cols : cols + 1, start : start + width])
            inverse_ref[:, start : start + width] = inverse
            mean_ref[:, start : start + width] = (
                total[0:cols, start : start + width] * inverse
            ).astype(BF)


def off_forward(row, key, band_sum, panels, off):
    count, cols = off.shape[0], panels.shape[1]
    rows, group = band_sum.shape[1], 16
    return pl.pallas_call(
        off_kernel,
        grid_spec=pltpu.PrefetchScalarGridSpec(
            num_scalar_prefetch=2,
            grid=(count // group,),
            in_specs=[
                full(band_sum.shape),
                full(panels.shape),
                pl.BlockSpec((group, BLK, BLK), lambda i, *_: (i, 0, 0)),
            ],
            out_specs=[full((cols, rows)), full((1, rows))],
            scratch_shapes=[pltpu.VMEM(band_sum.shape, F32)],
        ),
        out_shape=(
            jax.ShapeDtypeStruct((cols, rows), BF),
            jax.ShapeDtypeStruct((1, rows), F32),
        ),
        compiler_params=params(),
        name="off_forward",
    )(row, key, band_sum, panels, off)


def weights_kernel(feat_ref, w0, w1, w2, w3, down_ref, bias_ref, back_ref):
    feat = feat_ref[0]
    pieces = [w0, w1, w2, w3]
    cols = w0.shape[0] // 2 - 4
    hidden = w0.shape[1]
    part = hidden // 4
    here = lax.broadcasted_iota(jnp.int32, (hidden, hidden), 0)
    there = lax.broadcasted_iota(jnp.int32, (hidden, hidden), 1)
    place = (jnp.bitwise_xor(there // part, feat)) * part + there % part
    chosen = jnp.where(here == place, 1.0, 0.0).astype(BF)
    tall = jnp.concatenate(
        [w[0:cols, :].astype(BF) for w in pieces]
        + [w[cols : 2 * cols, :].astype(BF) for w in pieces],
        axis=0,
    )
    down_ref[...] = (0.5 * dot(chosen, tall, (((0,), (1,)), ((), ())))).astype(BF)
    own = jnp.concatenate([w0[cols : 2 * cols, :].astype(BF), w0[0:cols, :].astype(BF)], axis=0)
    back_ref[...] = dot(own, chosen).astype(BF)
    eye = lax.broadcasted_iota(jnp.int32, (part, part), 0) == lax.broadcasted_iota(
        jnp.int32, (part, part), 1
    )
    for k, w in enumerate(pieces):
        line = w[2 * cols : 2 * cols + 1, 0:part]
        bias_ref[k * part : (k + 1) * part, :] = 0.5 * jnp.sum(
            jnp.where(eye, line, 0.0), axis=1, keepdims=True
        )


def weights(feat, packs):
    hidden = packs[0].shape[1]
    cols = packs[0].shape[0] // 2 - 4
    return pl.pallas_call(
        weights_kernel,
        in_specs=[pl.BlockSpec(memory_space=pltpu.SMEM)]
        + [pl.BlockSpec(memory_space=pltpu.VMEM)] * 4,
        out_shape=(
            jax.ShapeDtypeStruct((hidden, 8 * cols), BF),
            jax.ShapeDtypeStruct((hidden, 1), F32),
            jax.ShapeDtypeStruct((2 * cols, hidden), BF),
        ),
        name="weights",
    )(feat, *packs)


def dense_kernel(
    feat_ref, x0, x1, x2, x3, m0, m1, m2, m3, c0, c1, c2, c3, inverse_ref, down_ref, bias_ref,
    back_w_ref, hidden_ref, back_ref, self_ref, grads_ref, total,
):
    step = pl.program_id(0)
    cols, part = x0.shape[0], c0.shape[0]
    width = 2 * BLK

    @pl.when(step == 0)
    def _():
        total[...] = jnp.zeros_like(total)

    ones = jnp.ones((ONES, width), BF)

    def body(i, carry):
        at = pl.ds(pl.multiple_of(i * width, width), width)
        own = [x0[:, at], m0[:, at]]
        both = jnp.concatenate(
            [own[0], x1[:, at], x2[:, at], x3[:, at], own[1], m1[:, at], m2[:, at], m3[:, at]],
            axis=0,
        )
        half = dot(down_ref[...], both) + bias_ref[...]
        grads = []
        for k, c in enumerate((c0, c1, c2, c3)):
            u = half[k * part : (k + 1) * part]
            t = jnp.tanh(u)
            q = u * t
            if k == 0:
                hidden_ref[:, at] = (u + q).astype(BF)
            grads.append((c[:, at].astype(F32) * (0.5 + 0.5 * t) * (1.0 + u - q)).astype(BF))
        grad = jnp.concatenate(grads, axis=0)
        backs = dot(back_w_ref[...], grad)
        back_ref[:, at] = (backs[0:cols] * inverse_ref[:, at]).astype(BF)
        self_ref[:, at] = backs[cols:]
        total[...] += dot(jnp.concatenate(own + [ones], axis=0), grad, NT)
        return carry

    lax.fori_loop(0, x0.shape[1] // width, body, 0, unroll=2)

    @pl.when(step == pl.num_programs(0) - 1)
    def _():
        feat = feat_ref[0]
        sums = total[0 : 2 * cols, :]
        low, high = sums[:, 0:BLK], sums[:, BLK:]
        far = (feat & 2) != 0
        halves = [jnp.where(far, high, low), jnp.where(far, low, high)]
        halves = [jnp.where((feat & 1) != 0, pltpu.roll(h, part, 1), h) for h in halves]
        groups = 2 * cols // 8
        for r in range(groups):
            for h in range(2):
                grads_ref[2 * r + h] = halves[h][8 * r : 8 * r + 8]
        bias_tile = total[2 * cols : 2 * cols + 8, 0:BLK]
        for r in range(2 * groups, grads_ref.shape[0]):
            grads_ref[r] = bias_tile


def dense(feat, xs, ms, cs, inverse, down, bias, back_w, loop_size):
    cols, rows = xs[0].shape
    part = cs[0].shape[0]
    chunk = 1024
    along = lambda height: pl.BlockSpec((height, chunk), lambda i: (0, i))
    return pl.pallas_call(
        dense_kernel,
        grid=(rows // chunk,),
        in_specs=[pl.BlockSpec(memory_space=pltpu.SMEM)]
        + [along(cols)] * 8
        + [along(part)] * 4
        + [along(1), full(down.shape), full(bias.shape), full(back_w.shape)],
        out_specs=[along(part), along(cols), along(cols), full((loop_size, 8, BLK))],
        out_shape=(
            jax.ShapeDtypeStruct((part, rows), BF),
            jax.ShapeDtypeStruct((cols, rows), BF),
            jax.ShapeDtypeStruct((cols, rows), F32),
            jax.ShapeDtypeStruct((loop_size, 8, BLK), F32),
        ),
        scratch_shapes=[pltpu.VMEM((2 * cols + ONES, 4 * part), F32)],
        compiler_params=params(),
        name="dense",
    )(feat, *xs, *ms, *cs, inverse, down, bias, back_w)


def off_back_kernel(row_ref, key_ref, back_ref, a_ref, out_ref):
    step = pl.program_id(0)
    group = a_ref.shape[0]

    @pl.when(step == 0)
    def _():
        out_ref[...] = jnp.zeros_like(out_ref)

    for r in range(group):
        left = back_ref[:, lanes(row_ref[step * group + r])]
        out_ref[key_ref[0, step * group + r]] = dot(left, a_ref[r]).astype(BF)


def off_backward(row, key, back, off, slots_total):
    count, (cols, rows), group = off.shape[0], back.shape, 16
    return pl.pallas_call(
        off_back_kernel,
        grid_spec=pltpu.PrefetchScalarGridSpec(
            num_scalar_prefetch=2,
            grid=(count // group,),
            in_specs=[
                full((cols, rows)),
                pl.BlockSpec((group, BLK, BLK), lambda i, *_: (i, 0, 0)),
            ],
            out_specs=full((slots_total, cols, BLK)),
        ),
        out_shape=jax.ShapeDtypeStruct((slots_total, cols, BLK), BF),
        compiler_params=params(),
        name="off_backward",
    )(row, key, back, off)


def band_back_kernel(back_ref, self_ref, a_ref, out_ref, low_ref, high_ref, total):
    step = pl.program_id(0)
    group = a_ref.shape[0]
    cols, rows = self_ref.shape

    @pl.when(step == 0)
    def _():
        total[:, 0:BLK] = jnp.zeros((cols, BLK), F32)
        total[:, BLK : BLK + rows] = self_ref[...]
        total[:, BLK + rows :] = jnp.zeros((cols, BLK), F32)

    parts = []
    for r in range(group):
        left = back_ref[:, lanes(step * group + r)]
        right = jnp.concatenate([a_ref[r, 0], a_ref[r, 1], a_ref[r, 2]], axis=1)
        parts.append(dot(left, right))
    for c in range(group + 2):
        found = [
            parts[c - o][:, o * BLK : (o + 1) * BLK] for o in range(3) if 0 <= c - o < group
        ]
        at = lanes(step * group + c)
        total[:, at] = total[:, at] + sum(found[1:], found[0])

    @pl.when(step == pl.num_programs(0) - 1)
    def _():
        low_ref[...] = total[:, 0:BLK].astype(BF)
        out_ref[...] = total[:, BLK : BLK + rows]
        high_ref[...] = total[:, BLK + rows :].astype(BF)


def band_backward(back, self_part, band):
    cols, rows = back.shape
    blocks, group = band.shape[0], 8
    return pl.pallas_call(
        band_back_kernel,
        grid=(blocks // group,),
        in_specs=[
            full((cols, rows)),
            full((cols, rows)),
            pl.BlockSpec((group, 3, BLK, BLK), lambda i: (i, 0, 0, 0)),
        ],
        out_specs=[full((cols, rows)), full((cols, BLK)), full((cols, BLK))],
        out_shape=(
            jax.ShapeDtypeStruct((cols, rows), F32),
            jax.ShapeDtypeStruct((cols, BLK), BF),
            jax.ShapeDtypeStruct((cols, BLK), BF),
        ),
        scratch_shapes=[pltpu.VMEM((cols, rows + 2 * BLK), F32)],
        compiler_params=params(),
        cost_estimate=pl.CostEstimate(
            flops=2 * 32 * 3 * BLK * rows, bytes_accessed=9 * 1024 * 1024, transcendentals=0
        ),
        name="band_backward",
    )(back, self_part, band)


def collect_kernel(asked_ref, band_ref, low_ref, high_ref, in_ref, out_ref, total, table, sem):
    copy = pltpu.make_async_copy(asked_ref.at[:, 0, :], table, sem)
    copy.start()
    rows = band_ref.shape[1]
    total[...] = band_ref[...]
    total[:, 0:BLK] += low_ref[...].astype(F32)
    total[:, rows - BLK :] += high_ref[...].astype(F32)
    copy.wait()

    def body(p, carry):
        for s in range(CAP):
            at = lanes(table[p, s])
            total[:, at] = total[:, at] + in_ref[p, s].astype(F32)
        return carry

    lax.fori_loop(0, in_ref.shape[0], body, 0, unroll=4)
    out_ref[...] = total[...].astype(BF)


def collect(asked, band_sum, low, high, incoming):
    loop_size = asked.shape[0]
    vmem = pl.BlockSpec(memory_space=pltpu.VMEM)
    return pl.pallas_call(
        collect_kernel,
        in_specs=[pl.BlockSpec(memory_space=pl.ANY)] + [vmem] * 4,
        out_shape=jax.ShapeDtypeStruct(band_sum.shape, BF),
        scratch_shapes=[
            pltpu.VMEM(band_sum.shape, F32),
            pltpu.SMEM((loop_size, BLK), jnp.int32),
            pltpu.SemaphoreType.DMA,
        ],
        compiler_params=params(),
        name="collect",
    )(asked, band_sum, low, high, incoming)


def tile_sum_kernel(scale, in_ref, out_ref):
    total = jnp.sum(in_ref[...], axis=0) * scale
    for p in range(out_ref.shape[0]):
        out_ref[p] = total


def tile_sum(tiles, scale):
    return pl.pallas_call(
        lambda a, b: tile_sum_kernel(scale, a, b),
        out_shape=jax.ShapeDtypeStruct(tiles.shape, F32),
        name="tile_sum",
    )(tiles)


def tiles_kernel(in_ref, out_ref, bias_ref):
    groups = out_ref.shape[0] // 8
    for r in range(groups):
        for h in range(2):
            out_ref[8 * r : 8 * r + 8, h * BLK : (h + 1) * BLK] = in_ref[2 * r + h]
    bias_ref[...] = in_ref[2 * groups][0:1, 0 : bias_ref.shape[1]]


def tiles_apart(tiles, rows, hidden, part):
    return pl.pallas_call(
        tiles_kernel,
        out_shape=(
            jax.ShapeDtypeStruct((rows, hidden), F32),
            jax.ShapeDtypeStruct((1, part), F32),
        ),
        name="tiles_apart",
    )(tiles)


def per_device(
    features, band_blocks, off_blocks, off_row, off_col, off_part, w_self, w_neigh, bias, cotangent
):
    rows, cols = features.shape
    loop_size = lax.axis_size("loop")
    forward = [(i, (i + 1) % loop_size) for i in range(loop_size)]
    backward = [(b, a) for a, b in forward]
    swap = lambda x, k: lax.ppermute(x, "feat", [(i, i ^ k) for i in range(4)])
    spread = lambda x: lax.all_to_all(x, "loop", split_axis=0, concat_axis=0, tiled=True)

    def everywhere(x):
        far = swap(x, 2)
        return [x, swap(x, 1), far, swap(far, 1)]

    feat = lax.axis_index("feat").astype(jnp.int32).reshape(1)
    x, cot = features.T, cotangent.T
    key, request = slots(off_part.reshape(1, -1), off_col.reshape(1, -1), loop_size)
    asked = spread(request)

    pack = jnp.concatenate(
        [
            w_self.astype(F32),
            w_neigh.astype(F32),
            jnp.pad(bias.reshape(1, -1), ((0, 7), (0, w_self.shape[1] - bias.shape[0]))),
        ],
        axis=0,
    )
    down, bias_down, back_w = weights(feat, everywhere(pack))
    xs = everywhere(x)
    cs = everywhere(cot)

    low = lax.ppermute(x[:, rows - BLK :], "loop", forward)
    high = lax.ppermute(x[:, :BLK], "loop", backward)
    band_sum = band_forward(x, low, high, band_blocks)
    panels = spread(answers(asked, x))
    mean, inverse = off_forward(
        off_row, key, band_sum, panels.reshape(loop_size * CAP, cols, BLK), off_blocks
    )
    ms = everywhere(mean)
    hidden, back, self_part, tiles = dense(
        feat, xs, ms, cs, inverse, down, bias_down, back_w, loop_size
    )
    outgoing = off_backward(off_row, key, back, off_blocks, loop_size * CAP)
    incoming = spread(outgoing.reshape(loop_size, CAP, cols, BLK))
    back_sum, to_low, to_high = band_backward(back, self_part, band_blocks)
    from_low = lax.ppermute(to_high, "loop", forward)
    from_high = lax.ppermute(to_low, "loop", backward)

    sums = tile_sum(spread(tiles), 1.0 / math.sqrt(rows * loop_size))
    weight_grads, bias_grad = tiles_apart(
        spread(sums), 2 * cols, w_self.shape[1], bias.shape[0]
    )
    grad = collect(asked, back_sum, from_low, from_high, incoming)
    return (
        hidden.T,
        grad.T,
        weight_grads.reshape(2, cols, w_self.shape[1]),
        bias_grad.reshape(-1),
    )


def solution(mesh):
    return jax.shard_map(
        per_device,
        mesh=mesh,
        in_specs=(
            P("loop", "feat"),
            P("loop", None, None, None),
            P("loop", None, None),
            P("loop"),
            P("loop"),
            P("loop", None),
            P("feat", None),
            P("feat", None),
            P("feat"),
            P("loop", "feat"),
        ),
        out_specs=(P("loop", "feat"), P("loop", "feat"), P(None, "feat", None), P("feat")),
        check_vma=False,
    )
```

time: 530 us -> 167 us (0.32)
  waiting for transfers between devices: 319 us -> 52.4 us
  blocking collectives: 82.9 us -> 12.3 us
  Pallas kernels: 0 us -> 38.3 us
  matrix products: 31.4 us -> 0 us
  other arithmetic: 26.5 us -> 0.02 us
  starting transfers between devices: 27.7 us -> 45.2 us
  between operations: 14.1 us -> 0.91 us
  local copies, waits for them, and re-layouts: 27.8 us -> 16.8 us
    psum x1 -> x0, waiting for transfers between devices: 223 us -> none  [per_device(): lax.psum((jnp.stack([self_grad, neigh_grad]) * grad_scale, bias_local * g...]
    psum x1 -> x0, blocking collectives: 82.9 us -> none  [per_device(): lax.psum((jnp.stack([self_grad, neigh_grad]) * grad_scale, bias_local * g...]
    reduce_scatter x1 -> x0, waiting for transfers between devices: 76.3 us -> none  [per_device(): lax.psum_scatter(partial_sums, 'feat', scatter_dimension=1, tiled=True)]
    pallas_call x0 -> x11, Pallas kernels: none -> 38.3 us  [the longest x1 13.3 us: dense(): pl.pallas_call(dense_kernel, grid=(rows // chunk,), in_specs=[pl.BlockSpe...]
    ppermute x4 -> x16, waiting for transfers between devices: 7.79 us -> 41 us  [the longest x12 33.4 us: per_device(): swap = lambda x, k: lax.ppermute(x, 'feat', [(i, i ^ k) for i in range(4)])]
    dot_general x9 -> x0, matrix products: 31.4 us -> none  [the longest x1 5.55 us: per_device(): jnp.dot(joined, joined_weights, preferred_element_type=jnp.float32)]
    unnamed x26 -> x50, local copies, waits for them, and re-layouts: 1.98 us -> 16.8 us
    scatter x2 -> x0, local copies, waits for them, and re-layouts: 14.6 us -> none  [the longest x1 8.87 us: per_device(): outgoing = jnp.zeros((loop_size, capacity, block_size, feat_cols), jnp.fl...]
  transfers between devices with their start and end apart: 10 -> 20, of which waited for: 5 -> 9; matrix products, arithmetic and copies ran while one was open for 10% -> 0% of each run, Pallas kernels for 0% -> 12%
where the time goes in v1:
time: 167 us; the launch traced here: 166 us
  waiting for transfers between devices  52.4 us (31%)
  starting transfers between devices  45.2 us (27%)
  Pallas kernels  38.3 us (23%)
  local copies, waits for them, and re-layouts  16.8 us (10%)
  blocking collectives  12.3 us (7%)
    ppermute x12, waiting for transfers between devices, per_device(): swap = lambda x, k: lax.ppermute(x, 'feat', [(i, i ^ k) for i in range(4)])  33.4 us
    all_to_all x4, starting transfers between devices, per_device(): lax.all_to_all(x, 'loop', split_axis=0, concat_axis=0, tiled=True)  21.8 us
    unnamed x50, local copies, waits for them, and re-layouts  16.8 us
    pallas_call x1, Pallas kernels, dense(): pl.pallas_call(dense_kernel, grid=(rows // chunk,), in_specs=[pl.BlockSpe...  13.3 us
    all_to_all x1, blocking collectives, per_device(): lax.all_to_all(x, 'loop', split_axis=0, concat_axis=0, tiled=True)  12.3 us
    ppermute x12, starting transfers between devices, per_device(): swap = lambda x, k: lax.ppermute(x, 'feat', [(i, i ^ k) for i in range(4)])  11.7 us
    all_to_all x4, waiting for transfers between devices, per_device(): lax.all_to_all(x, 'loop', split_axis=0, concat_axis=0, tiled=True)  11.3 us
    ppermute x1, starting transfers between devices, per_device(): high = lax.ppermute(x[:, :BLK], 'loop', backward)  5.45 us
  transfers between devices with their start and end apart: 20, of which 9 were waited for; matrix products, arithmetic and copies ran while one was open for 0% of the time, Pallas kernels for 12%

profile of v1, /device:TPU:0, one launch (start us, length us, event | category | flops | bytes accessed | tf_op | source)
XLA Modules:
  0.0 166.0 jit_solution(10523646344950178259)
XLA Ops:
  0.7 1.8 %slots.1 = (s32[1,64]{1,0:T(1,128)}, s32[32,8,128]{2,1,0:T(8,128)}) custom-call(s32[1,64]{1,0:T(1,128)} %bitcast.22, s32[1,64]{1,0:T(1,128)} %bitcast.23), custom_call_target="tpu_custom_call" | custom-call | tf_op jit(solution)/shard_map/slots/pallas_call | solution.py:60
  2.5 9.3 %all-to-all-start = ((s32[32,8,128]{2,1,0:T(8,128)}), s32[32,8,128]{2,1,0:T(8,128)S(1)}, u32[]{:S(2)}, u32[]{:S(2)}) async-start(s32[32,8,128]{2,1,0:T(8,128)} %get-tuple-element.21), calls=%async_computation | async-start | bytes 262144 | tf_op jit(solution)/shard_map/all_to_all | solution.py:481
  11.7 3.0 %collective-permute-start.9 = (bf16[64,8192]{1,0:T(8,128)(2,1)}, bf16[64,8192]{1,0:T(8,128)(2,1)}, u32[]{:S(2)}, u32[]{:S(2)}) collective-permute-start(bf16[64,8192]{1,0:T(8,128)(2,1)} %bitcast.5.c0), channel_id=1, source_target_pairs={{0,2},{1,3},{2,0},{3,1},{4,6},{5,7},{6,4},{7,5},{8,10},{9,11},{10,... | collective-permute-start | bytes 3145736 | tf_op jit(solution)/shard_map/ppermute | solution.py:480
  14.7 5.5 %all-to-all-done.asked_ref = s32[32,8,128]{2,1,0:T(8,128)S(1)} async-done(((s32[32,8,128]{2,1,0:T(8,128)}), s32[32,8,128]{2,1,0:T(8,128)S(1)}, u32[]{:S(2)}, u32[]{:S(2)}) %all-to-all-start) | async-done | bytes 131104 | tf_op jit(solution)/shard_map/all_to_all | solution.py:481
  21.2 2.1 %answers.1 = bf16[32,4,32,128]{3,2,1,0:T(8,128)(2,1)} custom-call(s32[32,8,128]{2,1,0:T(8,128)S(1)} %all-to-all-done.asked_ref, bf16[32,8192]{1,0:T(8,128)(2,1)S(1)} %bitcast.12), custom_call_target="tpu_custom_call" | custom-call | tf_op jit(solution)/shard_map/answers/pallas_call | solution.py:85
  23.3 4.7 %all-to-all-start.1 = ((bf16[32,4,32,128]{3,2,1,0:T(8,128)(2,1)}), bf16[32,4,32,128]{3,2,1,0:T(8,128)(2,1)}, u32[]{:S(2)}, u32[]{:S(2)}) async-start(bf16[32,4,32,128]{3,2,1,0:T(8,128)(2,1)} %answers.1), calls=%async_computation.1 | async-start | bytes 2097152 | tf_op jit(solution)/shard_map/all_to_all | solution.py:481
  28.1 3.0 %collective-permute-start.12 = (f32[72,256]{1,0:T(8,128)S(1)}, f32[72,256]{1,0:T(8,128)S(1)}, u32[]{:S(2)}, u32[]{:S(2)}) collective-permute-start(f32[72,256]{1,0:T(8,128)S(1)} %select_maximum_fusion.w0), channel_id=1, source_target_pairs={{0,2},{1,3},{2,0},{3,1},{4,6},{5,7},{6,4},{7,5},{8,10},{9,11},{10,... | collective-permute-start | bytes 221192 | tf_op jit(solution)/shard_map/ppermute | solution.py:480
  31.1 21.1 %collective-permute-done.12.w2 = f32[72,256]{1,0:T(8,128)S(1)} collective-permute-done((f32[72,256]{1,0:T(8,128)S(1)}, f32[72,256]{1,0:T(8,128)S(1)}, u32[]{:S(2)}, u32[]{:S(2)}) %collective-permute-start.12) | collective-permute-done | bytes 73760 | tf_op jit(solution)/shard_map/ppermute | solution.py:480
  52.2 5.5 %collective-permute-start.4 = (bf16[32,128]{1,0:T(8,128)(2,1)S(1)}, bf16[32,128]{1,0:T(8,128)(2,1)S(1)}, u32[]{:S(2)}, u32[]{:S(2)}) collective-permute-start(bf16[32,128]{1,0:T(8,128)(2,1)S(1)} %get-tuple-element.36), channel_id=1, source_target_pairs={{4,0},{8,4},{12,8},{16,12},{20,16},{24,20},{28,24},{32,28},{36,32}... | collective-permute-start | bytes 24584 | tf_op jit(solution)/shard_map/ppermute | solution.py:505
  59.0 2.3 %collective-permute-start.1 = (bf16[32,8192]{1,0:T(8,128)(2,1)S(1)}, bf16[32,8192]{1,0:T(8,128)(2,1)S(1)}, u32[]{:S(2)}, u32[]{:S(2)}) collective-permute-start(bf16[32,8192]{1,0:T(8,128)(2,1)S(1)} %bitcast.14), channel_id=1, source_target_pairs={{0,2},{1,3},{2,0},{3,1},{4,6},{5,7},{6,4},{7,5},{8,10},{9,11},{10,... | collective-permute-start | bytes 1572872 | tf_op jit(solution)/shard_map/ppermute | solution.py:480
  61.4 4.3 %collective-permute-done.3.low_ref = bf16[32,128]{1,0:T(8,128)(2,1)S(1)} collective-permute-done((bf16[32,128]{1,0:T(8,128)(2,1)S(1)}, bf16[32,128]{1,0:T(8,128)(2,1)S(1)}, u32[]{:S(2)}, u32[]{:S(2)}) %collective-permute-start.3) | collective-permute-done | bytes 8224 | tf_op jit(solution)/shard_map/ppermute | solution.py:504
  65.6 2.8 %copy-done = bf16[64,3,128,128]{3,2,1,0:T(8,128)(2,1)S(1)} copy-done((bf16[64,3,128,128]{3,2,1,0:T(8,128)(2,1)S(1)}, bf16[64,3,128,128]{3,2,1,0:T(8,128)(2,1)}, u32[]{:S(2)}) %copy-start) | copy-done | bytes 6291480
  68.4 3.9 %band_forward.1.band_ref = f32[48,8192]{1,0:T(8,128)S(1)} custom-call(bf16[32,8192]{1,0:T(8,128)(2,1)S(1)} %bitcast.16, bf16[32,128]{1,0:T(8,128)(2,1)S(1)} %collective-permute-done.3.low_ref, bf16[32,128]{1,0:T(8,128)(2,1)S(1)} %collective-permute-done.4.high_ref, bf16[64,3,128,128]{3,2,1,0:T(8,128)(2,1)S(1)} %copy-done), custom_call_target="tpu_custom_call" | custom-call | flops 301989888 | bytes 9437184 | tf_op jit(solution)/shard_map/band_forward/pallas_call | solution.py:116
  73.6 1.4 copy-done.4
  75.0 4.7 %off_forward.1 = (bf16[32,8192]{1,0:T(8,128)(2,1)}, f32[1,8192]{1,0:T(1,128)S(1)}) custom-call(s32[64]{0:T(128)S(1)} %copy-done.16, s32[1,64]{1,0:T(1,128)S(1)} %copy-done.17, f32[48,8192]{1,0:T(8,128)S(1)} %copy-done.4, bf16[128,32,128]{2,1,0:T(8,128)(2,1)} %bitcast.4.panel_ref, bf16[64,128,128]{2,1,0:T(8,128)(2,1)S(1)} %copy-done.2), custom_call_target="tpu_custom_call" | custom-call | tf_op jit(solution)/shard_map/off_forward/pallas_call | solution.py:169
  80.2 2.3 %collective-permute-start.6 = (bf16[32,8192]{1,0:T(8,128)(2,1)}, bf16[32,8192]{1,0:T(8,128)(2,1)}, u32[]{:S(2)}, u32[]{:S(2)}) collective-permute-start(bf16[32,8192]{1,0:T(8,128)(2,1)} %get-tuple-element.22.m0), channel_id=1, source_target_pairs={{0,2},{1,3},{2,0},{3,1},{4,6},{5,7},{6,4},{7,5},{8,10},{9,11},{10,... | collective-permute-start | bytes 1572872 | tf_op jit(solution)/shard_map/ppermute | solution.py:480
  84.0 12.0 %collective-permute-done.6.m2 = bf16[32,8192]{1,0:T(8,128)(2,1)} collective-permute-done((bf16[32,8192]{1,0:T(8,128)(2,1)}, bf16[32,8192]{1,0:T(8,128)(2,1)}, u32[]{:S(2)}, u32[]{:S(2)}) %collective-permute-start.6) | collective-permute-done | bytes 524320 | tf_op jit(solution)/shard_map/ppermute | solution.py:480
  96.0 1.9 %weights.1 = (bf16[256,256]{1,0:T(8,128)(2,1)}, f32[256,1]{1,0:T(8,128)}, bf16[64,256]{1,0:T(8,128)(2,1)}) custom-call(s32[1]{0:T(128)} %bitcast.feat_ref, f32[72,256]{1,0:T(8,128)} %copy-done.19, f32[72,256]{1,0:T(8,128)} %copy-done.21, f32[72,256]{1,0:T(8,128)} %copy-done.20, f32[72,256]{1,0:T(8,128)} %collective-permute-done.13.w3), custom_call_target="tpu_custom_call" | custom-call | tf_op jit(solution)/shard_map/weights/pallas_call | solution.py:222
  101.8 13.3 %dense.1 = (bf16[64,8192]{1,0:T(8,128)(2,1)}, bf16[32,8192]{1,0:T(8,128)(2,1)S(1)}, f32[32,8192]{1,0:T(8,128)S(1)}, f32[32,8,128]{2,1,0:T(8,128)S(1)}) custom-call(s32[1]{0:T(128)} %bitcast.feat_ref, bf16[32,8192]{1,0:T(8,128)(2,1)S(1)} %bitcast.17, bf16[32,8192]{1,0:T(8,128)(2,1)} %collective-permute-done.x1, bf16[32,8192]{1,0:T(8,128)(2,1)S(1)} %copy-done.12, ...), custom_call_target="tpu_custom_call" | custom-call | tf_op jit(solution)/shard_map/dense/pallas_call | solution.py:296
  116.1 12.3 %all_to_all.25.a = f32[32,8,128]{2,1,0:T(8,128)} all-to-all(f32[32,8,128]{2,1,0:T(8,128)S(1)} %get-tuple-element.33), channel_id=1, replica_groups=mesh['loop'=32,'feat'=4] {'loop'}, dimensions={0} | all-to-all | bytes 262144 | tf_op jit(solution)/shard_map/all_to_all | solution.py:481
  128.5 1.6 tile_sum.1
  130.1 3.9 %all-to-all-start.4 = ((f32[32,8,128]{2,1,0:T(8,128)}), f32[32,8,128]{2,1,0:T(8,128)S(1)}, u32[]{:S(2)}, u32[]{:S(2)}) async-start(f32[32,8,128]{2,1,0:T(8,128)} %tile_sum.1), calls=%async_computation.4 | async-start | bytes 262144 | tf_op jit(solution)/shard_map/all_to_all | solution.py:481
  133.9 2.7 %off_backward.1 = bf16[128,32,128]{2,1,0:T(8,128)(2,1)} custom-call(s32[64]{0:T(128)S(1)} %copy-done.16, s32[1,64]{1,0:T(1,128)S(1)} %copy-done.17, bf16[32,8192]{1,0:T(8,128)(2,1)S(1)} %get-tuple-element.28.back_ref, bf16[64,128,128]{2,1,0:T(8,128)(2,1)S(1)} %copy-done.2), custom_call_target="tpu_custom_call" | custom-call | tf_op jit(solution)/shard_map/off_backward/pallas_call | solution.py:331
  136.6 5.8 %all-to-all-done.4.in_ref = f32[32,8,128]{2,1,0:T(8,128)S(1)} async-done(((f32[32,8,128]{2,1,0:T(8,128)}), f32[32,8,128]{2,1,0:T(8,128)S(1)}, u32[]{:S(2)}, u32[]{:S(2)}) %all-to-all-start.4) | async-done | bytes 131104 | tf_op jit(solution)/shard_map/all_to_all | solution.py:481
  142.4 4.0 %all-to-all-start.2 = ((bf16[32,4,32,128]{3,2,1,0:T(8,128)(2,1)}), bf16[32,4,32,128]{3,2,1,0:T(8,128)(2,1)S(1)}, u32[]{:S(2)}, u32[]{:S(2)}) async-start(bf16[32,4,32,128]{3,2,1,0:T(8,128)(2,1)} %bitcast.8), calls=%async_computation.2 | async-start | bytes 2097152 | tf_op jit(solution)/shard_map/all_to_all | solution.py:481
  146.4 2.8 %copy-done.1 = bf16[64,3,128,128]{3,2,1,0:T(8,128)(2,1)S(1)} copy-done((bf16[64,3,128,128]{3,2,1,0:T(8,128)(2,1)S(1)}, bf16[64,3,128,128]{3,2,1,0:T(8,128)(2,1)}, u32[]{:S(2)}) %copy-start.1) | copy-done | bytes 6291480
  149.2 2.4 %band_backward.1 = (f32[32,8192]{1,0:T(8,128)S(1)}, bf16[32,128]{1,0:T(8,128)(2,1)S(1)}, bf16[32,128]{1,0:T(8,128)(2,1)S(1)}) custom-call(bf16[32,8192]{1,0:T(8,128)(2,1)S(1)} %get-tuple-element.28.back_ref, f32[32,8192]{1,0:T(8,128)S(1)} %copy-done.8, bf16[64,3,128,128]{3,2,1,0:T(8,128)(2,1)S(1)} %copy-done.1), custom_call_target="tpu_custom_call" | custom-call | flops 201326592 | bytes 9437184 | tf_op jit(solution)/shard_map/band_backward/pallas_call | solution.py:381
  152.5 1.8 %collective-permute-start.14 = (bf16[32,128]{1,0:T(8,128)(2,1)S(1)}, bf16[32,128]{1,0:T(8,128)(2,1)S(1)}, u32[]{:S(2)}, u32[]{:S(2)}) collective-permute-start(bf16[32,128]{1,0:T(8,128)(2,1)S(1)} %get-tuple-element.31), channel_id=1, source_target_pairs={{0,4},{4,8},{8,12},{12,16},{16,20},{20,24},{24,28},{28,32},{32,36}... | collective-permute-start | bytes 24584 | tf_op jit(solution)/shard_map/ppermute | solution.py:518
  154.3 4.5 %collective-permute-start.15 = (bf16[32,128]{1,0:T(8,128)(2,1)S(1)}, bf16[32,128]{1,0:T(8,128)(2,1)S(1)}, u32[]{:S(2)}, u32[]{:S(2)}) collective-permute-start(bf16[32,128]{1,0:T(8,128)(2,1)S(1)} %get-tuple-element.32), channel_id=1, source_target_pairs={{4,0},{8,4},{12,8},{16,12},{20,16},{24,20},{28,24},{32,28},{36,32}... | collective-permute-start | bytes 24584 | tf_op jit(solution)/shard_map/ppermute | solution.py:519
  158.8 1.5 tiles_apart.1
  160.3 1.9 %collective-permute-done.14.low_ref = bf16[32,128]{1,0:T(8,128)(2,1)S(1)} collective-permute-done((bf16[32,128]{1,0:T(8,128)(2,1)S(1)}, bf16[32,128]{1,0:T(8,128)(2,1)S(1)}, u32[]{:S(2)}, u32[]{:S(2)}) %collective-permute-start.14) | collective-permute-done | bytes 8224 | tf_op jit(solution)/shard_map/ppermute | solution.py:518
  163.6 2.4 %collect.1 = bf16[32,8192]{1,0:T(8,128)(2,1)} custom-call(s32[32,8,128]{2,1,0:T(8,128)S(1)} %all-to-all-done.asked_ref, f32[32,8192]{1,0:T(8,128)S(1)} %copy-done.10, bf16[32,128]{1,0:T(8,128)(2,1)S(1)} %collective-permute-done.14.low_ref, bf16[32,128]{1,0:T(8,128)(2,1)S(1)} %collective-permute-done.15.high_ref, ...), custom_call_target="tpu_custom_call" | custom-call | tf_op jit(solution)/shard_map/collect/pallas_call | solution.py:426
  (74 shorter events, 12.8 us)
Async XLA Ops:
  0.6 27.4 %copy-start.22 = (bf16[32,256]{1,0:T(8,128)(2,1)S(1)}, bf16[32,256]{1,0:T(8,128)(2,1)}, u32[]{:S(2)}) copy-start(bf16[32,256]{1,0:T(8,128)(2,1)} %param.16) | copy-start | bytes 49156
  0.6 27.4 %copy-start.23 = (bf16[32,256]{1,0:T(8,128)(2,1)S(1)}, bf16[32,256]{1,0:T(8,128)(2,1)}, u32[]{:S(2)}) copy-start(bf16[32,256]{1,0:T(8,128)(2,1)} %param.17) | copy-start | bytes 49156
  0.7 27.4 %copy-start.24 = (f32[64]{0:T(128)S(1)}, f32[64]{0:T(128)}, u32[]{:S(2)}) copy-start(f32[64]{0:T(128)} %param.18) | copy-start | bytes 772
  2.5 17.7 %all-to-all-start = ((s32[32,8,128]{2,1,0:T(8,128)}), s32[32,8,128]{2,1,0:T(8,128)S(1)}, u32[]{:S(2)}, u32[]{:S(2)}) async-start(s32[32,8,128]{2,1,0:T(8,128)} %get-tuple-element.21), calls=%async_computation | async-start | bytes 262144 | tf_op jit(solution)/shard_map/all_to_all | solution.py:481
  11.7 70.8 %collective-permute-start.9 = (bf16[64,8192]{1,0:T(8,128)(2,1)}, bf16[64,8192]{1,0:T(8,128)(2,1)}, u32[]{:S(2)}, u32[]{:S(2)}) collective-permute-start(bf16[64,8192]{1,0:T(8,128)(2,1)} %bitcast.5.c0), channel_id=1, source_target_pairs={{0,2},{1,3},{2,0},{3,1},{4,6},{5,7},{6,4},{7,5},{8,10},{9,11},{10,... | collective-permute-start | bytes 3145736 | tf_op jit(solution)/shard_map/ppermute | solution.py:480
  21.2 31.0 %copy-start.6 = (bf16[8192,32]{0,1:T(8,128)(2,1)S(1)}, bf16[8192,32]{0,1:T(8,128)(2,1)}, u32[]{:S(2)}) copy-start(bf16[8192,32]{0,1:T(8,128)(2,1)} %param.10) | copy-start | bytes 1572868
  23.3 50.2 %all-to-all-start.1 = ((bf16[32,4,32,128]{3,2,1,0:T(8,128)(2,1)}), bf16[32,4,32,128]{3,2,1,0:T(8,128)(2,1)}, u32[]{:S(2)}, u32[]{:S(2)}) async-start(bf16[32,4,32,128]{3,2,1,0:T(8,128)(2,1)} %answers.1), calls=%async_computation.1 | async-start | bytes 2097152 | tf_op jit(solution)/shard_map/all_to_all | solution.py:481
  28.1 44.3 %copy-start.19 = (f32[72,256]{1,0:T(8,128)}, f32[72,256]{1,0:T(8,128)S(1)}, u32[]{:S(2)}) copy-start(f32[72,256]{1,0:T(8,128)S(1)} %select_maximum_fusion.w0) | copy-start | bytes 221188
  28.1 24.1 %collective-permute-start.12 = (f32[72,256]{1,0:T(8,128)S(1)}, f32[72,256]{1,0:T(8,128)S(1)}, u32[]{:S(2)}, u32[]{:S(2)}) collective-permute-start(f32[72,256]{1,0:T(8,128)S(1)} %select_maximum_fusion.w0), channel_id=1, source_target_pairs={{0,2},{1,3},{2,0},{3,1},{4,6},{5,7},{6,4},{7,5},{8,10},{9,11},{10,... | collective-permute-start | bytes 221192 | tf_op jit(solution)/shard_map/ppermute | solution.py:480
  31.1 48.6 %collective-permute-start.11 = (f32[72,256]{1,0:T(8,128)S(1)}, f32[72,256]{1,0:T(8,128)S(1)}, u32[]{:S(2)}, u32[]{:S(2)}) collective-permute-start(f32[72,256]{1,0:T(8,128)S(1)} %select_maximum_fusion.w0), channel_id=1, source_target_pairs={{0,1},{1,0},{2,3},{3,2},{4,5},{5,4},{6,7},{7,6},{8,9},{9,8},{10,11... | collective-permute-start | bytes 221192 | tf_op jit(solution)/shard_map/ppermute | solution.py:480
  52.2 20.2 %copy-start.20 = (f32[72,256]{1,0:T(8,128)}, f32[72,256]{1,0:T(8,128)S(1)}, u32[]{:S(2)}) copy-start(f32[72,256]{1,0:T(8,128)S(1)} %collective-permute-done.12.w2) | copy-start | bytes 221188
  52.2 28.0 %collective-permute-start.13 = (f32[72,256]{1,0:T(8,128)S(1)}, f32[72,256]{1,0:T(8,128)}, u32[]{:S(2)}, u32[]{:S(2)}) collective-permute-start(f32[72,256]{1,0:T(8,128)S(1)} %collective-permute-done.12.w2), channel_id=1, source_target_pairs={{0,1},{1,0},{2,3},{3,2},{4,5},{5,4},{6,7},{7,6},{8,9},{9,8},{10,11... | collective-permute-start | bytes 221192 | tf_op jit(solution)/shard_map/ppermute | solution.py:480
  52.2 6.8 %collective-permute-start.4 = (bf16[32,128]{1,0:T(8,128)(2,1)S(1)}, bf16[32,128]{1,0:T(8,128)(2,1)S(1)}, u32[]{:S(2)}, u32[]{:S(2)}) collective-permute-start(bf16[32,128]{1,0:T(8,128)(2,1)S(1)} %get-tuple-element.36), channel_id=1, source_target_pairs={{4,0},{8,4},{12,8},{16,12},{20,16},{24,20},{28,24},{32,28},{36,32}... | collective-permute-start | bytes 24584 | tf_op jit(solution)/shard_map/ppermute | solution.py:505
  57.7 15.9 %copy-start.16 = (s32[64]{0:T(128)S(1)}, s32[64]{0:T(128)}, u32[]{:S(2)}) copy-start(s32[64]{0:T(128)} %row_ref.3) | copy-start | bytes 772
  57.7 15.9 %copy-start.17 = (s32[1,64]{1,0:T(1,128)S(1)}, s32[1,64]{1,0:T(1,128)}, u32[]{:S(2)}) copy-start(s32[1,64]{1,0:T(1,128)} %get-tuple-element.20.key_ref) | copy-start | bytes 772
  57.7 8.0 %collective-permute-start.3 = (bf16[32,128]{1,0:T(8,128)(2,1)S(1)}, bf16[32,128]{1,0:T(8,128)(2,1)S(1)}, u32[]{:S(2)}, u32[]{:S(2)}) collective-permute-start(bf16[32,128]{1,0:T(8,128)(2,1)S(1)} %get-tuple-element.37), channel_id=1, source_target_pairs={{0,4},{4,8},{8,12},{12,16},{16,20},{20,24},{24,28},{28,32},{32,36}... | collective-permute-start | bytes 24584 | tf_op jit(solution)/shard_map/ppermute | solution.py:504
  59.0 23.5 %collective-permute-start.1 = (bf16[32,8192]{1,0:T(8,128)(2,1)S(1)}, bf16[32,8192]{1,0:T(8,128)(2,1)S(1)}, u32[]{:S(2)}, u32[]{:S(2)}) collective-permute-start(bf16[32,8192]{1,0:T(8,128)(2,1)S(1)} %bitcast.14), channel_id=1, source_target_pairs={{0,2},{1,3},{2,0},{3,1},{4,6},{5,7},{6,4},{7,5},{8,10},{9,11},{10,... | collective-permute-start | bytes 1572872 | tf_op jit(solution)/shard_map/ppermute | solution.py:480
  65.6 18.2 %collective-permute-start = (bf16[32,8192]{1,0:T(8,128)(2,1)S(1)}, bf16[32,8192]{1,0:T(8,128)(2,1)}, u32[]{:S(2)}, u32[]{:S(2)}) collective-permute-start(bf16[32,8192]{1,0:T(8,128)(2,1)S(1)} %bitcast.15), channel_id=1, source_target_pairs={{0,1},{1,0},{2,3},{3,2},{4,5},{5,4},{6,7},{7,6},{8,9},{9,8},{10,11... | collective-permute-start | bytes 1572872 | tf_op jit(solution)/shard_map/ppermute | solution.py:480
  68.4 5.1 %copy-start.2 = (bf16[64,128,128]{2,1,0:T(8,128)(2,1)S(1)}, bf16[64,128,128]{2,1,0:T(8,128)(2,1)}, u32[]{:S(2)}) copy-start(bf16[64,128,128]{2,1,0:T(8,128)(2,1)} %a_ref.7) | copy-start | bytes 6291460
  79.7 16.3 %copy-start.21 = (f32[72,256]{1,0:T(8,128)}, f32[72,256]{1,0:T(8,128)S(1)}, u32[]{:S(2)}) copy-start(f32[72,256]{1,0:T(8,128)S(1)} %collective-permute-done.11.w1) | copy-start | bytes 221188
  79.7 18.2 %collective-permute-start.8 = (bf16[64,8192]{1,0:T(8,128)(2,1)}, bf16[64,8192]{1,0:T(8,128)(2,1)}, u32[]{:S(2)}, u32[]{:S(2)}) collective-permute-start(bf16[64,8192]{1,0:T(8,128)(2,1)} %bitcast.5.c0), channel_id=1, source_target_pairs={{0,1},{1,0},{2,3},{3,2},{4,5},{5,4},{6,7},{7,6},{8,9},{9,8},{10,11... | collective-permute-start | bytes 3145736 | tf_op jit(solution)/shard_map/ppermute | solution.py:480
  80.2 15.7 %collective-permute-start.6 = (bf16[32,8192]{1,0:T(8,128)(2,1)}, bf16[32,8192]{1,0:T(8,128)(2,1)}, u32[]{:S(2)}, u32[]{:S(2)}) collective-permute-start(bf16[32,8192]{1,0:T(8,128)(2,1)} %get-tuple-element.22.m0), channel_id=1, source_target_pairs={{0,2},{1,3},{2,0},{3,1},{4,6},{5,7},{6,4},{7,5},{8,10},{9,11},{10,... | collective-permute-start | bytes 1572872 | tf_op jit(solution)/shard_map/ppermute | solution.py:480
  82.6 15.4 %collective-permute-start.10 = (bf16[64,8192]{1,0:T(8,128)(2,1)}, bf16[64,8192]{1,0:T(8,128)(2,1)}, u32[]{:S(2)}, u32[]{:S(2)}) collective-permute-start(bf16[64,8192]{1,0:T(8,128)(2,1)} %collective-permute-done.9.c2), channel_id=1, source_target_pairs={{0,1},{1,0},{2,3},{3,2},{4,5},{5,4},{6,7},{7,6},{8,9},{9,8},{10,11... | collective-permute-start | bytes 3145736 | tf_op jit(solution)/shard_map/ppermute | solution.py:480
  82.6 15.3 %collective-permute-start.2 = (bf16[32,8192]{1,0:T(8,128)(2,1)S(1)}, bf16[32,8192]{1,0:T(8,128)(2,1)}, u32[]{:S(2)}, u32[]{:S(2)}) collective-permute-start(bf16[32,8192]{1,0:T(8,128)(2,1)S(1)} %collective-permute-done.1.x2), channel_id=1, source_target_pairs={{0,1},{1,0},{2,3},{3,2},{4,5},{5,4},{6,7},{7,6},{8,9},{9,8},{10,11... | collective-permute-start | bytes 1572872 | tf_op jit(solution)/shard_map/ppermute | solution.py:480
  83.9 14.0 %collective-permute-start.5 = (bf16[32,8192]{1,0:T(8,128)(2,1)}, bf16[32,8192]{1,0:T(8,128)(2,1)}, u32[]{:S(2)}, u32[]{:S(2)}) collective-permute-start(bf16[32,8192]{1,0:T(8,128)(2,1)} %get-tuple-element.22.m0), channel_id=1, source_target_pairs={{0,1},{1,0},{2,3},{3,2},{4,5},{5,4},{6,7},{7,6},{8,9},{9,8},{10,11... | collective-permute-start | bytes 1572872 | tf_op jit(solution)/shard_map/ppermute | solution.py:480
  96.0 2.3 %collective-permute-start.7 = (bf16[32,8192]{1,0:T(8,128)(2,1)}, bf16[32,8192]{1,0:T(8,128)(2,1)}, u32[]{:S(2)}, u32[]{:S(2)}) collective-permute-start(bf16[32,8192]{1,0:T(8,128)(2,1)} %collective-permute-done.6.m2), channel_id=1, source_target_pairs={{0,1},{1,0},{2,3},{3,2},{4,5},{5,4},{6,7},{7,6},{8,9},{9,8},{10,11... | collective-permute-start | bytes 1572872 | tf_op jit(solution)/shard_map/ppermute | solution.py:480
  130.1 12.3 %all-to-all-start.4 = ((f32[32,8,128]{2,1,0:T(8,128)}), f32[32,8,128]{2,1,0:T(8,128)S(1)}, u32[]{:S(2)}, u32[]{:S(2)}) async-start(f32[32,8,128]{2,1,0:T(8,128)} %tile_sum.1), calls=%async_computation.4 | async-start | bytes 262144 | tf_op jit(solution)/shard_map/all_to_all | solution.py:481
  136.6 9.7 %copy-start.8 = (f32[32,8192]{1,0:T(8,128)S(1)}, f32[32,8192]{1,0:T(8,128)}, u32[]{:S(2)}) copy-start(f32[32,8192]{1,0:T(8,128)} %copy-done.7) | copy-start | bytes 3145732
  142.4 9.1 %copy-start.18 = (f32[32,8,128]{2,1,0:T(8,128)}, f32[32,8,128]{2,1,0:T(8,128)S(1)}, u32[]{:S(2)}) copy-start(f32[32,8,128]{2,1,0:T(8,128)S(1)} %all-to-all-done.4.in_ref) | copy-start | bytes 393220
  142.4 20.0 %all-to-all-start.2 = ((bf16[32,4,32,128]{3,2,1,0:T(8,128)(2,1)}), bf16[32,4,32,128]{3,2,1,0:T(8,128)(2,1)S(1)}, u32[]{:S(2)}, u32[]{:S(2)}) async-start(bf16[32,4,32,128]{3,2,1,0:T(8,128)(2,1)} %bitcast.8), calls=%async_computation.2 | async-start | bytes 2097152 | tf_op jit(solution)/shard_map/all_to_all | solution.py:481
  152.5 9.7 %collective-permute-start.14 = (bf16[32,128]{1,0:T(8,128)(2,1)S(1)}, bf16[32,128]{1,0:T(8,128)(2,1)S(1)}, u32[]{:S(2)}, u32[]{:S(2)}) collective-permute-start(bf16[32,128]{1,0:T(8,128)(2,1)S(1)} %get-tuple-element.31), channel_id=1, source_target_pairs={{0,4},{4,8},{8,12},{12,16},{16,20},{20,24},{24,28},{28,32},{32,36}... | collective-permute-start | bytes 24584 | tf_op jit(solution)/shard_map/ppermute | solution.py:518
  154.3 7.9 %collective-permute-start.15 = (bf16[32,128]{1,0:T(8,128)(2,1)S(1)}, bf16[32,128]{1,0:T(8,128)(2,1)S(1)}, u32[]{:S(2)}, u32[]{:S(2)}) collective-permute-start(bf16[32,128]{1,0:T(8,128)(2,1)S(1)} %get-tuple-element.32), channel_id=1, source_target_pairs={{4,0},{8,4},{12,8},{16,12},{20,16},{24,20},{28,24},{32,28},{36,32}... | collective-permute-start | bytes 24584 | tf_op jit(solution)/shard_map/ppermute | solution.py:519
  (13 other events, 16.8 us)

commit v2 on v0

v2 whole, which is shorter than its diff:
```python
import math

import jax
import jax.numpy as jnp
from jax import lax
from jax.experimental import pallas as pl
from jax.experimental.pallas import tpu as pltpu
from jax.sharding import PartitionSpec as P

BF = jnp.bfloat16
F32 = jnp.float32
I32 = jnp.int32
BLK = 128
ONES = 16
CAP = 4
SLOTS = CAP + 1
NN = (((1,), (0,)), ((), ()))
NT = (((1,), (1,)), ((), ()))
TT = (((0,), (1,)), ((), ()))
DMA = pltpu.SemaphoreType.DMA


def lanes(block, width=BLK):
    return pl.ds(pl.multiple_of(block * BLK, BLK), width)


def dot(a, b, dims=NN):
    return lax.dot_general(a, b, dims, preferred_element_type=F32)


def call(kernel, name, places, operands, results, scratch=(), aliases=None, flops=0, mib=16):
    spaces = {"v": pltpu.VMEM, "h": pltpu.HBM, "s": pltpu.SMEM, "a": pl.ANY, "w": pltpu.VMEM}
    ins, outs = places.split(">")
    held = [
        pltpu.with_memory_space_constraint(x, spaces[p]) if p in "vh" else x
        for p, x in zip(ins, operands, strict=True)
    ]
    nbytes = sum(math.prod(x.shape) * x.dtype.itemsize for x in operands)
    kinds = [
        pltpu.VMEM(shape, dtype) if p == "v" else jax.ShapeDtypeStruct(shape, dtype)
        for p, (shape, dtype) in zip(outs, results, strict=True)
    ]
    return pl.pallas_call(
        kernel,
        in_specs=[pl.BlockSpec(memory_space=spaces[p]) for p in ins],
        out_specs=[pl.BlockSpec(memory_space=spaces[p]) for p in outs],
        out_shape=kinds,
        scratch_shapes=list(scratch),
        input_output_aliases=aliases or {},
        compiler_params=pltpu.CompilerParams(vmem_limit_bytes=mib << 20),
        cost_estimate=pl.CostEstimate(flops=1, bytes_accessed=1, transcendentals=0),
        name=name,
    )(*held)


def near_rows(feat, k, rows):
    return pl.ds(pl.multiple_of(jnp.bitwise_xor(feat, k) * rows, BLK), rows)


def near_loop(me, shift, count):
    return lax.rem(me + shift + count, count)


def prepare_kernel(part_in, col_in, key_ref, request_ref, part_ref, col_ref, sems):
    copies = [
        pltpu.make_async_copy(part_in, part_ref, sems.at[0]),
        pltpu.make_async_copy(col_in, col_ref, sems.at[1]),
    ]
    for copy in copies:
        copy.start()
    for copy in copies:
        copy.wait()
    part, col = part_ref[...], col_ref[...]
    count = part.shape[1]
    first = lax.broadcasted_iota(I32, (count, count), 0)
    second = lax.broadcasted_iota(I32, (count, count), 1)
    part_down = jnp.sum(jnp.where(first == second, part, 0), axis=1, keepdims=True)
    earlier = (part_down == part) & (first < second)
    slot = jnp.sum(earlier.astype(I32), axis=0, keepdims=True)
    key_ref[...] = part * CAP + slot
    shape = request_ref.shape
    wide = (shape[0], shape[1], count)
    owner = lax.broadcasted_iota(I32, wide, 0)
    lane = lax.broadcasted_iota(I32, shape, 2)
    hit = owner == part[None]
    table = jnp.zeros(shape, I32)
    for s in range(CAP):
        value = jnp.sum(
            jnp.where(hit & (slot[None] == s), col[None], 0), axis=2, keepdims=True
        )
        table = jnp.where(lane == s, value, table)
    request_ref[...] = table


def prepare(part, col, loop_size):
    return call(
        prepare_kernel,
        "prepare",
        "hh>ww",
        (part, col),
        ((part.shape, I32), ((loop_size, 1, BLK), I32)),
        scratch=[pltpu.VMEM(part.shape, I32), pltpu.VMEM(col.shape, I32), DMA((2,))],
    )


def band_kernel(
    tie_ref, a_ref, off_ref, x_in, out_ref, off_held,
    band_ref, wide, total, sems, out_sems, more, x_sem,
):
    del tie_ref
    cols, rows = x_in.shape
    steps = sems.shape[0]
    group = a_ref.shape[0] // steps

    def copy(i):
        at = pl.ds(i * group, group)
        return pltpu.make_async_copy(a_ref.at[at], band_ref.at[at], sems.at[i])

    def send(i):
        at = lanes(i * group, group * BLK)
        return pltpu.make_async_copy(total.at[:, at], out_ref.at[:, at], out_sems.at[i])

    x_copy = pltpu.make_async_copy(x_in, wide.at[0:cols, BLK : BLK + rows], x_sem)
    x_copy.start()
    for i in range(steps):
        copy(i).start()
    late = pltpu.make_async_copy(off_ref, off_held, more)
    late.start()
    wide[0:cols, 0:BLK] = jnp.zeros((cols, BLK), BF)
    wide[0:cols, BLK + rows :] = jnp.zeros((cols, BLK), BF)
    wide[cols:, :] = jnp.ones((ONES, wide.shape[1]), BF)
    x_copy.wait()

    def body(i, carry):
        copy(i).wait()
        for r in range(group):
            b = i * group + r
            left = wide[:, lanes(b, 3 * BLK)]
            right = jnp.concatenate([band_ref[b, 0], band_ref[b, 1], band_ref[b, 2]], axis=1)
            total[:, lanes(b)] = dot(left, right, NT)
        send(i).start()
        return carry

    lax.fori_loop(0, steps, body, 0)
    for i in range(steps):
        send(i).wait()
    late.wait()


def band_forward(tie, band, off, x):
    cols, rows = x.shape
    return call(
        band_kernel,
        "band_forward",
        "shhh>hv",
        (tie, band, off, x),
        (((cols + ONES, rows), F32), (off.shape, BF)),
        scratch=[
            pltpu.VMEM(band.shape, BF),
            pltpu.VMEM((cols + ONES, rows + 2 * BLK), BF),
            pltpu.VMEM((cols + ONES, rows), F32),
            DMA((8,)),
            DMA((8,)),
            DMA,
            DMA,
        ],
        flops=2 * (cols + ONES) * 3 * BLK * rows,
    )


def pieces_kernel(
    place_ref, x_ref, cot_ref, self_in, neigh_in, bias_in, p0, p1, p2, p3,
    held, self_ref, neigh_ref, bias_ref, sems, out_sems, more,
):
    cols, part = x_ref.shape[0], cot_ref.shape[0]
    tall = cols + part
    copies, sends = [], []
    for k, piece in enumerate((p0, p1, p2, p3)):
        at = near_rows(place_ref[0], k, piece.shape[1])
        copies.append(
            pltpu.make_async_copy(x_ref.at[:, at], held.at[k, 0:cols], sems.at[2 * k])
        )
        copies.append(
            pltpu.make_async_copy(cot_ref.at[:, at], held.at[k, cols:tall], sems.at[2 * k + 1])
        )
        sends.append(pltpu.make_async_copy(held.at[k], piece, out_sems.at[k]))
    small = [
        pltpu.make_async_copy(a, b, more.at[i])
        for i, (a, b) in enumerate(
            ((self_in, self_ref), (neigh_in, neigh_ref), (bias_in, bias_ref))
        )
    ]
    for copy in small:
        copy.start()
    for k in (1, 2, 3, 0):
        copies[2 * k].start()
        copies[2 * k + 1].start()
    for copy in small:
        copy.wait()
    hidden = self_ref.shape[1]
    bias = bias_ref[...]
    high = bias.astype(BF)
    rest = bias - high.astype(F32)
    middle = rest.astype(BF)
    low = (rest - middle.astype(F32)).astype(BF)
    row = lax.broadcasted_iota(I32, (16, part), 0)
    lines = [jnp.broadcast_to(v.astype(F32), (16, part)) for v in (high, middle, low)]
    lines = jnp.where(row == 0, lines[0], jnp.where(row == 1, lines[1], lines[2]))
    lines = jnp.where(row < 3, lines, 0.0).astype(BF)
    for k in range(4):
        held[k, tall:, :] = jnp.zeros((16, held.shape[2]), BF)
        for g in range(cols // 16):
            rows = slice(16 * g, 16 * g + 16)
            held[k, tall:, 2 * g * hidden : (2 * g + 1) * hidden] = self_ref[rows, :]
            held[k, tall:, (2 * g + 1) * hidden : (2 * g + 2) * hidden] = neigh_ref[rows, :]
        held[k, tall:, cols // 8 * hidden : cols // 8 * hidden + part] = lines
    for k in (1, 2, 3, 0):
        copies[2 * k].wait()
        copies[2 * k + 1].wait()
        sends[k].start()
    for send in sends:
        send.wait()


def by_device(place, x, cot, w_self, w_neigh, bias):
    piece = (x.shape[0] + cot.shape[0] + 16, x.shape[1] // 4)
    return call(
        pieces_kernel,
        "by_device",
        "shhhhh>hhhh",
        (place, x, cot, w_self, w_neigh, bias),
        4 * ((piece, BF),),
        scratch=[
            pltpu.VMEM((4, *piece), BF),
            pltpu.VMEM(w_self.shape, BF),
            pltpu.VMEM(w_neigh.shape, BF),
            pltpu.VMEM(bias.shape, F32),
            DMA((8,)),
            DMA((4,)),
            DMA((3,)),
        ],
    )


def answer_kernel(place_ref, asked_ref, x_in, out_ref, x_ref, held, table, sem, x_sem, sems):
    copy = pltpu.make_async_copy(asked_ref.at[:, 0, :], table, sem)
    x_copy = pltpu.make_async_copy(x_in, x_ref, x_sem)
    copy.start()
    x_copy.start()
    count, steps = held.shape[0], sems.shape[0]
    group = count // steps
    above = near_loop(place_ref[1], 1, count)

    def send(j):
        at = pl.ds(j * group, group)
        return pltpu.make_async_copy(held.at[at], out_ref.at[at], sems.at[j])

    def body(p, carry):
        for s in range(CAP):
            held[p, s] = x_ref[:, lanes(table[p, s])]
        edge = jnp.where(p == above, x_ref.shape[1] // BLK - 1, 0)
        held[p, CAP] = x_ref[:, lanes(edge)]
        return carry

    copy.wait()
    x_copy.wait()
    for j in range(steps):
        lax.fori_loop(j * group, (j + 1) * group, body, 0, unroll=4)
        send(j).start()
    for j in range(steps):
        send(j).wait()


def answers(place, asked, x):
    shape = (asked.shape[0], SLOTS, x.shape[0], BLK)
    (out,) = call(
        answer_kernel,
        "answers",
        "sah>h",
        (place, asked, x),
        ((shape, BF),),
        scratch=[
            pltpu.VMEM(x.shape, BF),
            pltpu.VMEM(shape, BF),
            pltpu.SMEM((shape[0], BLK), I32),
            DMA,
            DMA,
            DMA((4,)),
        ],
    )
    return out


def off_kernel(
    place_ref, row_ref, key_ref, start_in, band_in, panel_in, a_ref,
    m0, m1, m2, m3, inverse_ref, total, edge_ref, panel_ref, sems,
):
    feat = place_ref[0]
    cols, rows = m0.shape[0], total.shape[1]
    count = a_ref.shape[0]
    pairs = [
        (panel_in, panel_ref), (start_in, total),
        (band_in.at[0, 0], edge_ref.at[0]), (band_in.at[band_in.shape[0] - 1, 2], edge_ref.at[1]),
    ]
    copies = [pltpu.make_async_copy(a, b, sems.at[i]) for i, (a, b) in enumerate(pairs)]
    for copy in copies:
        copy.start()
    for copy in copies:
        copy.wait()
    below, above = [near_loop(place_ref[1], d, panel_ref.shape[0]) for d in (-1, 1)]
    total[0:cols, 0:BLK] += dot(panel_ref[below, CAP], edge_ref[0], NT)
    total[0:cols, rows - BLK :] += dot(panel_ref[above, CAP], edge_ref[1], NT)
    ones = jnp.ones((ONES, BLK), BF)
    for start in range(0, count, 8):
        terms = []
        for r in range(start, start + 8):
            key = key_ref[0, r]
            left = jnp.concatenate([panel_ref[key // CAP, key % CAP], ones], axis=0)
            terms.append(dot(left, a_ref[r], NT))
        for r in range(start, start + 8):
            where = lanes(row_ref[r])
            total[:, where] = total[:, where] + terms[r - start]
    part = m0.shape[1]
    for k, mean_ref in enumerate((m1, m2, m3, m0)):
        at = near_rows(feat, (k + 1) % 4, part)
        inverse = 1.0 / (1.0 + total[cols : cols + 1, at])
        mean_ref[...] = (total[0:cols, at] * inverse).astype(BF)
        if k == 3:
            inverse_ref[...] = inverse


def off_forward(place, row, key, band_sum, band, panels, off):
    cols, rows = panels.shape[2], band_sum.shape[1]
    mean = ((cols, rows // 4), BF)
    return call(
        off_kernel,
        "off_forward",
        "ssshhhv>vvvvv",
        (place, row, key, band_sum, band, panels, off),
        4 * (mean,) + (((1, rows // 4), F32),),
        scratch=[
            pltpu.VMEM(band_sum.shape, F32),
            pltpu.VMEM((2, BLK, BLK), BF),
            pltpu.VMEM(panels.shape, BF),
            DMA((4,)),
        ],
        flops=2 * off.shape[0] * BLK * BLK * (cols + ONES),
    )


def weights_kernel(place_ref, p0, p1, p2, p3, down_ref, bias_ref, back_ref):
    feat = place_ref[0]
    hidden = down_ref.shape[0]
    cols, part = back_ref.shape[0] // 8, hidden // 4
    here = lax.broadcasted_iota(I32, (hidden, hidden), 0)
    there = lax.broadcasted_iota(I32, (hidden, hidden), 1)
    place = (jnp.bitwise_xor(there // part, feat)) * part + there % part
    chosen = jnp.where(here == place, 0.5, 0.0).astype(BF)
    eye = lax.broadcasted_iota(I32, (part, part), 0) == lax.broadcasted_iota(
        I32, (part, part), 1
    )
    own, neigh = [], []
    for k, p in enumerate((p0, p1, p2, p3)):
        rows = slice(cols + part, cols + part + 16)
        for g in range(cols // 16):
            own.append(p[rows, 2 * g * hidden : (2 * g + 1) * hidden])
            neigh.append(p[rows, (2 * g + 1) * hidden : (2 * g + 2) * hidden])
        start = cols // 8 * hidden
        lines = p[rows, start : start + BLK].astype(F32)[:, 0:part]
        line = (lines[0:1] + lines[1:2]) + lines[2:3]
        bias_ref[k * part : (k + 1) * part, :] = 0.5 * jnp.sum(
            jnp.where(eye, line, 0.0), axis=1, keepdims=True
        )
    down_ref[...] = dot(chosen, jnp.concatenate(own + neigh, axis=0), TT).astype(BF)
    back_ref[...] = dot(jnp.concatenate(neigh + own, axis=0), chosen).astype(BF)


def weights(place, pieces, cols, hidden):
    return call(
        weights_kernel,
        "weights",
        "svvvv>vvv",
        (place, *pieces),
        (((hidden, 8 * cols), BF), ((hidden, 1), F32), ((8 * cols, hidden), BF)),
    )


def dense_kernel(
    p0, p1, p2, p3, m0, m1, m2, m3, inverse_ref, down_ref, bias_ref, back_w_ref,
    b0, b1, b2, b3, grad_ref, h0, h1, h2, h3, helds, sems,
):
    cols, rows = m0.shape
    pieces = (p0, p1, p2, p3)
    part = h0.shape[0] - cols
    width = 2 * BLK

    def project(i):
        at = slice(i * width, (i + 1) * width)
        both = [p[0:cols, at] for p in pieces] + [m[:, at] for m in (m0, m1, m2, m3)]
        return dot(down_ref[...], jnp.concatenate(both, axis=0))

    def gradient(i, half):
        at = slice(i * width, (i + 1) * width)
        grads = []
        for k, p in enumerate(pieces):
            here = slice(k * part, (k + 1) * part)
            u = half[here] + bias_ref[here]
            t = jnp.tanh(u)
            s = 1.0 + t
            helds[k, 0:part, at] = (u * s).astype(BF)
            c = p[cols : cols + part, at].astype(F32)
            grads.append((c * s * (1.0 + u * (1.0 - t))).astype(BF))
        return jnp.concatenate(grads, axis=0)

    def products(i, grad):
        at = slice(i * width, (i + 1) * width)
        grad_ref[:, at] = grad
        both = dot(back_w_ref[...], grad)
        backs = both[0 : 4 * cols] * inverse_ref[:, at]
        for k, b in enumerate((b0, b1, b2, b3)):
            b[:, at] = backs[k * cols : (k + 1) * cols].astype(BF)
            own = both[(4 + k) * cols : (5 + k) * cols]
            helds[k, part:, at] = own.astype(BF)

    count = rows // width
    half, grad = project(0), None
    for i in range(count):
        later = project(i + 1) if i + 1 < count else None
        fresh = gradient(i, half)
        if grad is not None:
            products(i - 1, grad)
        half, grad = later, fresh
    products(count - 1, grad)
    sends = []
    for k, h in enumerate((h0, h1, h2, h3)):
        sends.append(pltpu.make_async_copy(helds.at[k], h, sems.at[k]))
        sends[-1].start()
    for send in sends:
        send.wait()


def dense(pieces, ms, inverse, down, bias, back_w):
    cols, rows = ms[0].shape
    hidden = down.shape[0]
    return call(
        dense_kernel,
        "dense",
        12 * "v" + ">vvvvvhhhh",
        (*pieces, *ms, inverse, down, bias, back_w),
        4 * (((cols, rows), BF),)
        + (((hidden, rows), BF),)
        + 4 * (((hidden // 4 + cols, rows), BF),),
        scratch=[pltpu.VMEM((4, hidden // 4 + cols, rows), BF), DMA((4,))],
        flops=2 * rows * hidden * 400,
    )


def after_kernel(feat_ref, p0, p1, p2, p3, m0, m1, m2, m3, grad_ref, g0, g1, g2, g3):
    cols, rows = m0.shape
    part = grad_ref.shape[0] // 4
    grad = grad_ref[...]
    left = [p[0:cols, :] for p in (p0, p1, p2, p3)] + [m[...] for m in (m0, m1, m2, m3)]
    left.append(jnp.ones((ONES, rows), BF))
    total = dot(jnp.concatenate(left, axis=0), grad, NT)
    feat = feat_ref[0]
    low, high = total[:, 0:BLK], total[:, BLK:]
    far = (feat & 2) != 0
    halves = [jnp.where(far, high, low), jnp.where(far, low, high)]
    halves = [jnp.where((feat & 1) != 0, pltpu.roll(h, part, 1), h) for h in halves]
    tall = 4 * cols
    for k, out in enumerate((g0, g1, g2, g3)):
        for h in range(2):
            at = slice(h * BLK, (h + 1) * BLK)
            out[0:cols, at] = halves[h][k * cols : (k + 1) * cols]
            out[cols : 2 * cols, at] = halves[h][tall + k * cols : tall + (k + 1) * cols]
        line = (low if k < 2 else high)[2 * tall : 2 * tall + 8]
        out[2 * cols :, 0:BLK] = pltpu.roll(line, part, 1) if k % 2 else line
        out[2 * cols :, BLK:] = jnp.zeros((8, BLK), F32)


def after(place, pieces, ms, grad):
    cols, _ = ms[0].shape
    return call(
        after_kernel,
        "after",
        "s" + 9 * "v" + ">wwww",
        (place, *pieces, *ms, grad),
        4 * (((2 * cols + 8, grad.shape[0]), F32),),
    )


def off_back_kernel(
    place_ref, row_ref, key_ref, b0, b1, b2, b3, a_ref, band_ref, out_ref, back_ref,
    held, edge_ref, sem, sems,
):
    count = band_ref.shape[0]
    edges = [
        pltpu.make_async_copy(band_ref.at[0, 0], edge_ref.at[0], sems.at[0]),
        pltpu.make_async_copy(band_ref.at[count - 1, 2], edge_ref.at[1], sems.at[1]),
    ]
    for edge in edges:
        edge.start()
    for k, b in enumerate((b0, b1, b2, b3)):
        back_ref[:, near_rows(place_ref[0], k, b.shape[1])] = b[...]
    held[...] = jnp.zeros_like(held)
    for r in range(a_ref.shape[0]):
        key = key_ref[0, r]
        left = back_ref[:, lanes(row_ref[r])]
        held[key // CAP, key % CAP] = dot(left, a_ref[r]).astype(BF)
    for edge in edges:
        edge.wait()
    below, above = [near_loop(place_ref[1], d, held.shape[0]) for d in (-1, 1)]
    rows = back_ref.shape[1]
    held[below, CAP] = dot(back_ref[:, 0:BLK], edge_ref[0]).astype(BF)
    held[above, CAP] = dot(back_ref[:, rows - BLK :], edge_ref[1]).astype(BF)
    copy = pltpu.make_async_copy(held, out_ref, sem)
    copy.start()
    copy.wait()


def off_backward(place, row, key, backs, off, band, loop_size):
    cols, part = backs[0].shape
    shape = (loop_size, SLOTS, cols, BLK)
    return call(
        off_back_kernel,
        "off_backward",
        "sssvvvvvh>hv",
        (place, row, key, *backs, off, band),
        ((shape, BF), ((cols, 4 * part), BF)),
        scratch=[pltpu.VMEM(shape, BF), pltpu.VMEM((2, BLK, BLK), BF), DMA, DMA((2,))],
    )


def band_back_kernel(back_ref, a_ref, total, held, sems):
    count, steps = a_ref.shape[0], sems.shape[0]
    group = count // steps
    copies = []
    for i in range(steps):
        at = pl.ds(i * group, group)
        copies.append(pltpu.make_async_copy(a_ref.at[at], held.at[at], sems.at[i]))
        copies[-1].start()
    carried = [None, None]
    for i in range(steps):
        copies[i].wait()
        for b in range(i * group, (i + 1) * group):
            right = jnp.concatenate([held[b, 0], held[b, 1], held[b, 2]], axis=1)
            term = dot(back_ref[:, b * BLK : (b + 1) * BLK], right)
            first, middle, last = [term[:, o * BLK : (o + 1) * BLK] for o in range(3)]
            if b > 0:
                total[:, (b - 1) * BLK : b * BLK] = carried[0] + first
            carried = [middle if b == 0 else carried[1] + middle, last]
    total[:, (count - 1) * BLK :] = carried[0]


def band_backward(back, band):
    cols, rows = back.shape
    (out,) = call(
        band_back_kernel,
        "band_backward",
        "vh>w",
        (back, band),
        (((cols, rows), F32),),
        scratch=[pltpu.VMEM(band.shape, BF), DMA((8,))],
    )
    return out


def collect_kernel(
    place_ref, asked_ref, start_ref, in_ref, h0, h1, h2, h3,
    out_ref, hidden_ref, total, held, selfs, table, sems,
):
    feat = place_ref[0]
    (cols, rows), part = total.shape, h0.shape[1]
    hidden = h0.shape[0] - cols
    copies = [
        pltpu.make_async_copy(asked_ref.at[:, 0, :], table, sems.at[0]),
        pltpu.make_async_copy(start_ref, total, sems.at[1]),
        pltpu.make_async_copy(in_ref, held, sems.at[2]),
    ]
    for k, h in enumerate((h0, h1, h2, h3)):
        copies.append(pltpu.make_async_copy(h.at[hidden:], selfs.at[k], sems.at[3 + k]))
    for k, h in enumerate((h0, h1, h2, h3)):
        at = near_rows(feat, k, part)
        copies.append(
            pltpu.make_async_copy(h.at[0:hidden], hidden_ref.at[:, at], sems.at[7 + k])
        )
    for copy in copies:
        copy.start()
    copies[1].wait()
    for k in range(4):
        copies[3 + k].wait()
        at = near_rows(feat, k, part)
        total[:, at] = total[:, at] + selfs[k].astype(F32)
    copies[0].wait()
    copies[2].wait()
    below, above = [near_loop(place_ref[1], d, held.shape[0]) for d in (-1, 1)]
    total[:, 0:BLK] += held[below, CAP].astype(F32)
    total[:, rows - BLK :] += held[above, CAP].astype(F32)

    def body(p, carry):
        for s in range(CAP):
            at = lanes(table[p, s])
            total[:, at] = total[:, at] + held[p, s].astype(F32)
        return carry

    lax.fori_loop(0, held.shape[0], body, 0, unroll=4)
    out_ref[...] = total[...].astype(BF)
    for copy in copies[7:]:
        copy.wait()


def collect(place, asked, band_sum, incoming, outs):
    cols, rows = band_sum.shape
    return call(
        collect_kernel,
        "collect",
        "saah" + 4 * "h" + ">ww",
        (place, asked, band_sum, incoming, *outs),
        ((band_sum.shape, BF), ((outs[0].shape[0] - cols, rows), BF)),
        scratch=[
            pltpu.VMEM(band_sum.shape, F32),
            pltpu.VMEM(incoming.shape, BF),
            pltpu.VMEM((4, cols, rows // 4), BF),
            pltpu.SMEM((asked.shape[0], BLK), I32),
            DMA((11,)),
        ],
    )


def finish_kernel(scale, own_ref, other_ref, out_ref, bias_ref):
    total = (own_ref[...] + other_ref[...]) * scale
    tall = out_ref.shape[0]
    out_ref[...] = total[0:tall]
    bias_ref[...] = total[tall : tall + 1, 0 : bias_ref.shape[1]]


def finish(own, other, part, scale):
    tall, wide = own.shape
    return call(
        lambda *refs: finish_kernel(scale, *refs),
        "finish",
        "ww>ww",
        (own, other),
        (((tall - 8, wide), F32), ((1, part), F32)),
    )


def per_device(
    features, band_blocks, off_blocks, off_row, off_col, off_part, w_self, w_neigh, bias, cotangent
):
    rows, cols = features.shape
    loop_size = lax.axis_size("loop")
    together = lax.optimization_barrier

    def swap(value, k, j=0):
        pairs = [(4 * i + f, 4 * (i ^ j) + (f ^ k)) for i in range(loop_size) for f in range(4)]
        return lax.ppermute(value, ("loop", "feat"), pairs)

    def swapped(values):
        return [values[0]] + [swap(values[k], k) for k in (1, 2, 3)]

    def spread(value):
        return lax.all_to_all(value, "loop", split_axis=0, concat_axis=0, tiled=True)

    place = jnp.stack([lax.axis_index("feat"), lax.axis_index("loop")]).astype(I32)
    x, cot = features.T, cotangent.T
    key, request = prepare(off_part.reshape(1, -1), off_col.reshape(1, -1), loop_size)
    request, place = together((request, place))
    asked = spread(request)
    pieces = by_device(place, x, cot, w_self, w_neigh, bias.reshape(1, -1))
    asked, then = together((asked, pieces[0]))[0], place
    pieces = swapped(pieces)
    ready = answers(place, asked, x)
    ready, then = together((ready, then))
    panels = spread(ready)
    band_sum, off = band_forward(then, band_blocks, off_blocks, x)
    *ms, inverse = off_forward(place, off_row, key, band_sum, band_blocks, panels, off)
    ms = swapped(ms)
    down, bias_down, back_w = weights(place, pieces, cols, w_self.shape[1])
    ms, down = together((ms, down))
    *rest, h0, h1, h2, h3 = dense(pieces, ms, inverse, down, bias_down, back_w)
    *backs, grad = rest
    backs = swapped(backs)
    terms = after(place, pieces, ms, grad)
    near = swapped(terms)
    o2 = swap(h2, 2)
    backs, h1, h3 = together((backs, h1, h3))
    outgoing, back = off_backward(place, off_row, key, backs, off, band_blocks, loop_size)
    grads = (near[0] + near[1]) + (near[2] + near[3])
    one, two, three = [swap(grads, 0, j) for j in (8, 16, 24)]
    outgoing, back, one, two, three, o2, h1, h3 = together(
        (outgoing, back, one, two, three, o2, h1, h3)
    )
    incoming = spread(outgoing)
    outs = [h0, swap(h1, 1), o2, swap(h3, 3)]
    back_sum = band_backward(back, band_blocks)
    one, two, three, back_sum = together((one, two, three, back_sum))
    grads = (grads + one) + (two + three)
    one, two, three = [swap(grads, 0, j) for j in (2, 4, 6)]
    grads = (grads + one) + (two + three)
    other = swap(grads, 0, 1)
    grad_features, hidden = collect(place, asked, back_sum, incoming, outs)
    weight_grads, bias_grad = finish(
        grads, other, bias.shape[0], 0.5 / math.sqrt(rows * loop_size)
    )
    return (
        hidden.T,
        grad_features.T,
        weight_grads.reshape(2, cols, w_self.shape[1]),
        bias_grad.reshape(-1),
    )


def solution(mesh):
    return jax.shard_map(
        per_device,
        mesh=mesh,
        in_specs=(
            P("loop", "feat"),
            P("loop", None, None, None),
            P("loop", None, None),
            P("loop"),
            P("loop"),
            P("loop", None),
            P("feat", None),
            P("feat", None),
            P("feat"),
            P("loop", "feat"),
        ),
        out_specs=(P("loop", "feat"), P("loop", "feat"), P(None, "feat", None), P("feat")),
        check_vma=False,
    )
```

time: 530 us -> 140 us (0.26)
  waiting for transfers between devices: 319 us -> 48.2 us
  blocking collectives: 82.9 us -> 0 us
  Pallas kernels: 0 us -> 36.4 us
  matrix products: 31.4 us -> 0 us
  other arithmetic: 26.5 us -> 0.14 us
  local copies, waits for them, and re-layouts: 27.8 us -> 3.6 us
  starting transfers between devices: 27.7 us -> 49.4 us
  between operations: 14.1 us -> 1.15 us
    psum x1 -> x0, waiting for transfers between devices: 223 us -> none  [per_device(): lax.psum((jnp.stack([self_grad, neigh_grad]) * grad_scale, bias_local * g...]
    psum x1 -> x0, blocking collectives: 82.9 us -> none  [per_device(): lax.psum((jnp.stack([self_grad, neigh_grad]) * grad_scale, bias_local * g...]
    reduce_scatter x1 -> x0, waiting for transfers between devices: 76.3 us -> none  [per_device(): lax.psum_scatter(partial_sums, 'feat', scatter_dimension=1, tiled=True)]
    pallas_call x0 -> x12, Pallas kernels: none -> 36.4 us  [call(): pl.pallas_call(kernel, in_specs=[pl.BlockSpec(memory_space=spaces[p]) for...]
    dot_general x9 -> x0, matrix products: 31.4 us -> none  [the longest x1 5.55 us: per_device(): jnp.dot(joined, joined_weights, preferred_element_type=jnp.float32)]
    ppermute x4 -> x22, waiting for transfers between devices: 7.79 us -> 35.9 us  [swap(): return lax.ppermute(value, ('loop', 'feat'), pairs)]
    scatter x2 -> x0, local copies, waits for them, and re-layouts: 14.6 us -> none  [the longest x1 8.87 us: per_device(): outgoing = jnp.zeros((loop_size, capacity, block_size, feat_cols), jnp.fl...]
    ppermute x4 -> x22, starting transfers between devices: 13.6 us -> 27.3 us  [swap(): return lax.ppermute(value, ('loop', 'feat'), pairs)]
  transfers between devices with their start and end apart: 10 -> 25, of which waited for: 5 -> 11; matrix products, arithmetic and copies ran while one was open for 10% -> 0% of each run, Pallas kernels for 0% -> 18%
where the time goes in v2:
time: 140 us; the launch traced here: 139 us
  starting transfers between devices  49.4 us (35%)
  waiting for transfers between devices  48.2 us (34%)
  Pallas kernels  36.4 us (26%)
  local copies, waits for them, and re-layouts  3.6 us (3%)
    pallas_call x12, Pallas kernels, call(): pl.pallas_call(kernel, in_specs=[pl.BlockSpec(memory_space=spaces[p]) for...  36.4 us
    ppermute x22, waiting for transfers between devices, swap(): return lax.ppermute(value, ('loop', 'feat'), pairs)  35.9 us
    ppermute x22, starting transfers between devices, swap(): return lax.ppermute(value, ('loop', 'feat'), pairs)  27.3 us
    all_to_all x3, starting transfers between devices, spread(): lax.all_to_all(value, 'loop', split_axis=0, concat_axis=0, tiled=True)  22.1 us
    all_to_all x3, waiting for transfers between devices, spread(): lax.all_to_all(value, 'loop', split_axis=0, concat_axis=0, tiled=True)  12.3 us
    unnamed x36, local copies, waits for them, and re-layouts  3.6 us
  transfers between devices with their start and end apart: 25, of which 11 were waited for; matrix products, arithmetic and copies ran while one was open for 0% of the time, Pallas kernels for 18%

profile of v2, /device:TPU:0, one launch (start us, length us, event | category | flops | bytes accessed | tf_op | source)
XLA Modules:
  0.0 138.9 jit_solution(2885408496274949544)
XLA Ops:
  0.7 1.8 %prepare.1 = (s32[1,64]{1,0:T(1,128)S(1)}, s32[32,1,128]{2,1,0:T(1,128)}) custom-call(s32[1,64]{1,0:T(1,128)} %bitcast.19, s32[1,64]{1,0:T(1,128)} %bitcast.20), custom_call_target="tpu_custom_call" | custom-call | flops 1 | bytes 1 | tf_op jit(solution)/shard_map/prepare/pallas_call | solution.py:43
  2.5 9.3 %all-to-all-start = ((s32[32,1,128]{2,1,0:T(1,128)}), s32[32,1,128]{2,1,0:T(1,128)S(1)}, u32[]{:S(2)}, u32[]{:S(2)}) async-start(s32[32,1,128]{2,1,0:T(1,128)} %get-tuple-element.69), calls=%async_computation | async-start | bytes 32768 | tf_op jit(solution)/shard_map/all_to_all | solution.py:663
  11.8 2.9 %by_device.1 = (bf16[112,2048]{1,0:T(8,128)(2,1)S(1)}, bf16[112,2048]{1,0:T(8,128)(2,1)}, bf16[112,2048]{1,0:T(8,128)(2,1)}, bf16[112,2048]{1,0:T(8,128)(2,1)}) custom-call(s32[2]{0:T(128)S(1)} %pad_add_fusion.place_ref.tie_ref.feat_ref, bf16[32,8192]{1,0:T(8,128)(2,1)} %bitcast.11, bf16[64,8192]{1,0:T(8,128)(2,1)} %bitcast.14, bf16[32,256]{1,0:T(8,128)(2,1)} %self_in.1, ...), custom_call_target="tpu_custom_call" | custom-call | flops 1 | bytes 1 | tf_op jit(solution)/shard_map/by_device/pallas_call | solution.py:43
  14.7 5.2 %all-to-all-done.asked_ref = s32[32,1,128]{2,1,0:T(1,128)S(1)} async-done(((s32[32,1,128]{2,1,0:T(1,128)}), s32[32,1,128]{2,1,0:T(1,128)S(1)}, u32[]{:S(2)}, u32[]{:S(2)}) %all-to-all-start) | async-done | bytes 16416 | tf_op jit(solution)/shard_map/all_to_all | solution.py:663
  19.9 2.8 %answers.1 = bf16[32,5,32,128]{3,2,1,0:T(8,128)(2,1)} custom-call(s32[2]{0:T(128)S(1)} %pad_add_fusion.place_ref.tie_ref.feat_ref, s32[32,1,128]{2,1,0:T(1,128)S(1)} %all-to-all-done.asked_ref, bf16[32,8192]{1,0:T(8,128)(2,1)} %bitcast.12), custom_call_target="tpu_custom_call" | custom-call | flops 1 | bytes 1 | tf_op jit(solution)/shard_map/answers/pallas_call | solution.py:43
  22.7 4.7 %all-to-all-start.1 = ((bf16[32,5,32,128]{3,2,1,0:T(8,128)(2,1)}), bf16[32,5,32,128]{3,2,1,0:T(8,128)(2,1)}, u32[]{:S(2)}, u32[]{:S(2)}) async-start(bf16[32,5,32,128]{3,2,1,0:T(8,128)(2,1)} %answers.1), calls=%async_computation.1 | async-start | bytes 2621440 | tf_op jit(solution)/shard_map/all_to_all | solution.py:663
  27.5 3.0 %collective-permute-start.1 = (bf16[112,2048]{1,0:T(8,128)(2,1)}, bf16[112,2048]{1,0:T(8,128)(2,1)S(1)}, u32[]{:S(2)}, u32[]{:S(2)}) collective-permute-start(bf16[112,2048]{1,0:T(8,128)(2,1)} %get-tuple-element.74), channel_id=1, source_target_pairs={{0,2},{1,3},{2,0},{3,1},{4,6},{5,7},{6,4},{7,5},{8,10},{9,11},{10,... | collective-permute-start | bytes 1376264 | tf_op jit(solution)/shard_map/ppermute | solution.py:657
  30.9 7.3 %band_forward.1 = (f32[48,8192]{1,0:T(8,128)S(1)}, bf16[64,128,128]{2,1,0:T(8,128)(2,1)S(1)}) custom-call(s32[2]{0:T(128)S(1)} %pad_add_fusion.place_ref.tie_ref.feat_ref, bf16[64,3,128,128]{3,2,1,0:T(8,128)(2,1)} %a_ref.3, bf16[64,128,128]{2,1,0:T(8,128)(2,1)} %off_ref.1, bf16[32,8192]{1,0:T(8,128)(2,1)} %bitcast.13), custom_call_target="tpu_custom_call" | custom-call | flops 1 | bytes 1 | tf_op jit(solution)/shard_map/band_forward/pallas_call | solution.py:43
  38.2 1.2 copy-done
  39.4 7.1 %all-to-all-done.1.panel_in = bf16[32,5,32,128]{3,2,1,0:T(8,128)(2,1)} async-done(((bf16[32,5,32,128]{3,2,1,0:T(8,128)(2,1)}), bf16[32,5,32,128]{3,2,1,0:T(8,128)(2,1)}, u32[]{:S(2)}, u32[]{:S(2)}) %all-to-all-start.1) | async-done | bytes 1310752 | tf_op jit(solution)/shard_map/all_to_all | solution.py:663
  46.5 4.1 %off_forward.1 = (bf16[32,2048]{1,0:T(8,128)(2,1)S(1)}, bf16[32,2048]{1,0:T(8,128)(2,1)S(1)}, bf16[32,2048]{1,0:T(8,128)(2,1)S(1)}, bf16[32,2048]{1,0:T(8,128)(2,1)S(1)}, f32[1,2048]{1,0:T(1,128)S(1)}) custom-call(s32[2]{0:T(128)S(1)} %pad_add_fusion.place_ref.tie_ref.feat_ref, s32[64]{0:T(128)S(1)} %copy-done.2, s32[1,64]{1,0:T(1,128)S(1)} %get-tuple-element.72.key_ref, ...), custom_call_target="tpu_custom_call" | custom-call | flops 1 | bytes 1 | tf_op jit(solution)/shard_map/off_forward/pallas_call | solution.py:43
  50.7 3.0 %collective-permute-start.4 = (bf16[32,2048]{1,0:T(8,128)(2,1)S(1)}, bf16[32,2048]{1,0:T(8,128)(2,1)S(1)}, u32[]{:S(2)}, u32[]{:S(2)}) collective-permute-start(bf16[32,2048]{1,0:T(8,128)(2,1)S(1)} %get-tuple-element.82), channel_id=1, source_target_pairs={{0,2},{1,3},{2,0},{3,1},{4,6},{5,7},{6,4},{7,5},{8,10},{9,11},{10,... | collective-permute-start | bytes 393224 | tf_op jit(solution)/shard_map/ppermute | solution.py:657
  54.0 1.1 collective-permute-done.1.p2
  55.1 6.5 %collective-permute-done.2.p3 = bf16[112,2048]{1,0:T(8,128)(2,1)} collective-permute-done((bf16[112,2048]{1,0:T(8,128)(2,1)}, bf16[112,2048]{1,0:T(8,128)(2,1)}, u32[]{:S(2)}, u32[]{:S(2)}) %collective-permute-start.2) | collective-permute-done | bytes 458784 | tf_op jit(solution)/shard_map/ppermute | solution.py:657
  61.7 1.3 weights.1
  63.0 4.5 %collective-permute-done.4.m2 = bf16[32,2048]{1,0:T(8,128)(2,1)S(1)} collective-permute-done((bf16[32,2048]{1,0:T(8,128)(2,1)S(1)}, bf16[32,2048]{1,0:T(8,128)(2,1)S(1)}, u32[]{:S(2)}, u32[]{:S(2)}) %collective-permute-start.4) | collective-permute-done | bytes 131104 | tf_op jit(solution)/shard_map/ppermute | solution.py:657
  67.5 3.2 %dense.1 = (bf16[32,2048]{1,0:T(8,128)(2,1)S(1)}, bf16[32,2048]{1,0:T(8,128)(2,1)S(1)}, bf16[32,2048]{1,0:T(8,128)(2,1)S(1)}, bf16[32,2048]{1,0:T(8,128)(2,1)S(1...) custom-call(bf16[112,2048]{1,0:T(8,128)(2,1)S(1)} %get-tuple-element, ...), custom_call_target="tpu_custom_call" | custom-call | flops 1 | bytes 1 | tf_op jit(solution)/shard_map/dense/pallas_call | solution.py:43
  72.4 1.6 %after.1 = (f32[72,256]{1,0:T(8,128)S(1)}, f32[72,256]{1,0:T(8,128)S(1)}, f32[72,256]{1,0:T(8,128)S(1)}, f32[72,256]{1,0:T(8,128)S(1)}) custom-call(s32[2]{0:T(128)S(1)} %pad_add_fusion.place_ref.tie_ref.feat_ref, bf16[112,2048]{1,0:T(8,128)(2,1)S(1)} %get-tuple-element.70.p0, bf16[112,2048]{1,0:T(8,128)(2,1)S(1)} %collective-permute-done.p1, ...), custom_call_target="tpu_custom_call" | custom-call | flops 1 | bytes 1 | tf_op jit(solution)/shard_map/after/pallas_call | solution.py:43
  74.7 2.9 %collective-permute-start.10 = (f32[72,256]{1,0:T(8,128)S(1)}, f32[72,256]{1,0:T(8,128)S(1)}, u32[]{:S(2)}, u32[]{:S(2)}) collective-permute-start(f32[72,256]{1,0:T(8,128)S(1)} %get-tuple-element.108), channel_id=1, source_target_pairs={{0,2},{1,3},{2,0},{3,1},{4,6},{5,7},{6,4},{7,5},{8,10},{9,11},{10,... | collective-permute-start | bytes 221192 | tf_op jit(solution)/shard_map/ppermute | solution.py:657
  78.3 2.9 %collective-permute-start.7 = (bf16[32,2048]{1,0:T(8,128)(2,1)S(1)}, bf16[32,2048]{1,0:T(8,128)(2,1)S(1)}, u32[]{:S(2)}, u32[]{:S(2)}) collective-permute-start(bf16[32,2048]{1,0:T(8,128)(2,1)S(1)} %get-tuple-element.95), channel_id=1, source_target_pairs={{0,2},{1,3},{2,0},{3,1},{4,6},{5,7},{6,4},{7,5},{8,10},{9,11},{10,... | collective-permute-start | bytes 393224 | tf_op jit(solution)/shard_map/ppermute | solution.py:657
  81.2 5.0 %collective-permute-done.10 = f32[72,256]{1,0:T(8,128)S(1)} collective-permute-done((f32[72,256]{1,0:T(8,128)S(1)}, f32[72,256]{1,0:T(8,128)S(1)}, u32[]{:S(2)}, u32[]{:S(2)}) %collective-permute-start.10) | collective-permute-done | bytes 73760 | tf_op jit(solution)/shard_map/ppermute | solution.py:657
  87.0 1.3 collective-permute-done.11
  88.4 2.1 %collective-permute-start.14 = (f32[72,256]{1,0:T(8,128)S(1)}, f32[72,256]{1,0:T(8,128)S(1)}, u32[]{:S(2)}, u32[]{:S(2)}) collective-permute-start(f32[72,256]{1,0:T(8,128)S(1)} %add_add_fusion.2), channel_id=1, source_target_pairs={{0,96},{1,97},{2,98},{3,99},{4,100},{5,101},{6,102},{7,103},{8,104... | collective-permute-start | bytes 221192 | tf_op jit(solution)/shard_map/ppermute | solution.py:657
  90.4 1.1 collective-permute-start.13
  93.3 3.3 %off_backward.1 = (bf16[32,5,32,128]{3,2,1,0:T(8,128)(2,1)}, bf16[32,8192]{1,0:T(8,128)(2,1)S(1)}) custom-call(s32[2]{0:T(128)S(1)} %pad_add_fusion.place_ref.tie_ref.feat_ref, s32[64]{0:T(128)S(1)} %copy-done.2, s32[1,64]{1,0:T(1,128)S(1)} %get-tuple-element.72.key_ref, bf16[32,2048]{1,0:T(8,128)(2,1)S(1)} %get-tuple-element.99.b0, ...), custom_call_target="tpu_custom_call" | custom-call | flops 1 | bytes 1 | tf_op jit(solution)/shard_map/off_backward/pallas_call | solution.py:43
  97.9 8.2 %all-to-all-start.2 = ((bf16[32,5,32,128]{3,2,1,0:T(8,128)(2,1)}), bf16[32,5,32,128]{3,2,1,0:T(8,128)(2,1)}, u32[]{:S(2)}, u32[]{:S(2)}) async-start(bf16[32,5,32,128]{3,2,1,0:T(8,128)(2,1)} %get-tuple-element.118), calls=%async_computation.2 | async-start | bytes 2621440 | tf_op jit(solution)/shard_map/all_to_all | solution.py:663
  106.2 1.9 %collective-permute-start.17 = (bf16[96,2048]{1,0:T(8,128)(2,1)S(1)}, bf16[96,2048]{1,0:T(8,128)(2,1)S(1)}, u32[]{:S(2)}, u32[]{:S(2)}) collective-permute-start(bf16[96,2048]{1,0:T(8,128)(2,1)S(1)} %copy-done.4), channel_id=1, source_target_pairs={{0,3},{1,2},{2,1},{3,0},{4,7},{5,6},{6,5},{7,4},{8,11},{9,10},{10,... | collective-permute-start | bytes 1179656 | tf_op jit(solution)/shard_map/ppermute | solution.py:657
  108.1 3.3 %band_backward.1.start_ref = f32[32,8192]{1,0:T(8,128)S(1)} custom-call(bf16[32,8192]{1,0:T(8,128)(2,1)S(1)} %get-tuple-element.116.back_ref, bf16[64,3,128,128]{3,2,1,0:T(8,128)(2,1)} %a_ref.3), custom_call_target="tpu_custom_call" | custom-call | flops 1 | bytes 1 | tf_op jit(solution)/shard_map/band_backward/pallas_call | solution.py:43
  111.5 3.0 %collective-permute-start.20 = (f32[72,256]{1,0:T(8,128)S(1)}, f32[72,256]{1,0:T(8,128)S(1)}, u32[]{:S(2)}, u32[]{:S(2)}) collective-permute-start(f32[72,256]{1,0:T(8,128)S(1)} %add_add_fusion.1), channel_id=1, source_target_pairs={{0,24},{1,25},{2,26},{3,27},{4,28},{5,29},{6,30},{7,31},{8,16},{9,... | collective-permute-start | bytes 221192 | tf_op jit(solution)/shard_map/ppermute | solution.py:657
  115.7 11.9 %collective-permute-done.20 = f32[72,256]{1,0:T(8,128)S(1)} collective-permute-done((f32[72,256]{1,0:T(8,128)S(1)}, f32[72,256]{1,0:T(8,128)S(1)}, u32[]{:S(2)}, u32[]{:S(2)}) %collective-permute-start.20) | collective-permute-done | bytes 73760 | tf_op jit(solution)/shard_map/ppermute | solution.py:657
  128.7 4.4 %collective-permute-done.21.refs_1_ = f32[72,256]{1,0:T(8,128)S(1)} collective-permute-done((f32[72,256]{1,0:T(8,128)S(1)}, f32[72,256]{1,0:T(8,128)S(1)}, u32[]{:S(2)}, u32[]{:S(2)}) %collective-permute-start.21) | collective-permute-done | bytes 73760 | tf_op jit(solution)/shard_map/ppermute | solution.py:657
  134.6 4.1 %collect.1 = (bf16[32,8192]{1,0:T(8,128)(2,1)}, bf16[64,8192]{1,0:T(8,128)(2,1)}) custom-call(s32[2]{0:T(128)S(1)} %pad_add_fusion.place_ref.tie_ref.feat_ref, s32[32,1,128]{2,1,0:T(1,128)S(1)} %all-to-all-done.asked_ref, f32[32,8192]{1,0:T(8,128)S(1)} %band_backward.1.start_ref, bf16[32,5,32,128]{3,2,1,0:T(8,128)(2,1)} %all-to-all-done.2.in_ref, ...), custom_call_target="tpu_custom_call" | custom-call | flops 1 | bytes 1 | tf_op jit(solution)/shard_map/collect/pallas_call | solution.py:43
  (70 shorter events, 11.8 us)
Async XLA Ops:
  2.5 17.4 %all-to-all-start = ((s32[32,1,128]{2,1,0:T(1,128)}), s32[32,1,128]{2,1,0:T(1,128)S(1)}, u32[]{:S(2)}, u32[]{:S(2)}) async-start(s32[32,1,128]{2,1,0:T(1,128)} %get-tuple-element.69), calls=%async_computation | async-start | bytes 32768 | tf_op jit(solution)/shard_map/all_to_all | solution.py:663
  22.7 23.7 %all-to-all-start.1 = ((bf16[32,5,32,128]{3,2,1,0:T(8,128)(2,1)}), bf16[32,5,32,128]{3,2,1,0:T(8,128)(2,1)}, u32[]{:S(2)}, u32[]{:S(2)}) async-start(bf16[32,5,32,128]{3,2,1,0:T(8,128)(2,1)} %answers.1), calls=%async_computation.1 | async-start | bytes 2621440 | tf_op jit(solution)/shard_map/all_to_all | solution.py:663
  27.4 26.2 %collective-permute-start = (bf16[112,2048]{1,0:T(8,128)(2,1)}, bf16[112,2048]{1,0:T(8,128)(2,1)S(1)}, u32[]{:S(2)}, u32[]{:S(2)}) collective-permute-start(bf16[112,2048]{1,0:T(8,128)(2,1)} %get-tuple-element.73), channel_id=1, source_target_pairs={{0,1},{1,0},{2,3},{3,2},{4,5},{5,4},{6,7},{7,6},{8,9},{9,8},{10,11... | collective-permute-start | bytes 1376264 | tf_op jit(solution)/shard_map/ppermute | solution.py:657
  27.5 27.6 %collective-permute-start.1 = (bf16[112,2048]{1,0:T(8,128)(2,1)}, bf16[112,2048]{1,0:T(8,128)(2,1)S(1)}, u32[]{:S(2)}, u32[]{:S(2)}) collective-permute-start(bf16[112,2048]{1,0:T(8,128)(2,1)} %get-tuple-element.74), channel_id=1, source_target_pairs={{0,2},{1,3},{2,0},{3,1},{4,6},{5,7},{6,4},{7,5},{8,10},{9,11},{10,... | collective-permute-start | bytes 1376264 | tf_op jit(solution)/shard_map/ppermute | solution.py:657
  30.5 16.0 %copy-start.2 = (s32[64]{0:T(128)S(1)}, s32[64]{0:T(128)}, u32[]{:S(2)}) copy-start(s32[64]{0:T(128)} %row_ref.3) | copy-start | bytes 772
  30.5 31.2 %collective-permute-start.2 = (bf16[112,2048]{1,0:T(8,128)(2,1)}, bf16[112,2048]{1,0:T(8,128)(2,1)}, u32[]{:S(2)}, u32[]{:S(2)}) collective-permute-start(bf16[112,2048]{1,0:T(8,128)(2,1)} %get-tuple-element.75), channel_id=1, source_target_pairs={{0,3},{1,2},{2,1},{3,0},{4,7},{5,6},{6,5},{7,4},{8,11},{9,10},{10,... | collective-permute-start | bytes 1376264 | tf_op jit(solution)/shard_map/ppermute | solution.py:657
  50.6 12.4 %collective-permute-start.3 = (bf16[32,2048]{1,0:T(8,128)(2,1)S(1)}, bf16[32,2048]{1,0:T(8,128)(2,1)S(1)}, u32[]{:S(2)}, u32[]{:S(2)}) collective-permute-start(bf16[32,2048]{1,0:T(8,128)(2,1)S(1)} %get-tuple-element.81), channel_id=1, source_target_pairs={{0,1},{1,0},{2,3},{3,2},{4,5},{5,4},{6,7},{7,6},{8,9},{9,8},{10,11... | collective-permute-start | bytes 393224 | tf_op jit(solution)/shard_map/ppermute | solution.py:657
  50.7 16.8 %collective-permute-start.4 = (bf16[32,2048]{1,0:T(8,128)(2,1)S(1)}, bf16[32,2048]{1,0:T(8,128)(2,1)S(1)}, u32[]{:S(2)}, u32[]{:S(2)}) collective-permute-start(bf16[32,2048]{1,0:T(8,128)(2,1)S(1)} %get-tuple-element.82), channel_id=1, source_target_pairs={{0,2},{1,3},{2,0},{3,1},{4,6},{5,7},{6,4},{7,5},{8,10},{9,11},{10,... | collective-permute-start | bytes 393224 | tf_op jit(solution)/shard_map/ppermute | solution.py:657
  53.6 13.8 %collective-permute-start.5 = (bf16[32,2048]{1,0:T(8,128)(2,1)S(1)}, bf16[32,2048]{1,0:T(8,128)(2,1)S(1)}, u32[]{:S(2)}, u32[]{:S(2)}) collective-permute-start(bf16[32,2048]{1,0:T(8,128)(2,1)S(1)} %get-tuple-element.83), channel_id=1, source_target_pairs={{0,3},{1,2},{2,1},{3,0},{4,7},{5,6},{6,5},{7,4},{8,11},{9,10},{10,... | collective-permute-start | bytes 393224 | tf_op jit(solution)/shard_map/ppermute | solution.py:657
  71.4 25.7 %collective-permute-start.15 = (bf16[96,2048]{1,0:T(8,128)(2,1)S(1)}, bf16[96,2048]{1,0:T(8,128)(2,1)S(1)}, u32[]{:S(2)}, u32[]{:S(2)}) collective-permute-start(bf16[96,2048]{1,0:T(8,128)(2,1)S(1)} %get-tuple-element.110), channel_id=1, source_target_pairs={{0,2},{1,3},{2,0},{3,1},{4,6},{5,7},{6,4},{7,5},{8,10},{9,11},{10,... | collective-permute-start | bytes 1179656 | tf_op jit(solution)/shard_map/ppermute | solution.py:657
  74.0 4.4 %collective-permute-start.9 = (f32[72,256]{1,0:T(8,128)S(1)}, f32[72,256]{1,0:T(8,128)S(1)}, u32[]{:S(2)}, u32[]{:S(2)}) collective-permute-start(f32[72,256]{1,0:T(8,128)S(1)} %get-tuple-element.107), channel_id=1, source_target_pairs={{0,1},{1,0},{2,3},{3,2},{4,5},{5,4},{6,7},{7,6},{8,9},{9,8},{10,11... | collective-permute-start | bytes 221192 | tf_op jit(solution)/shard_map/ppermute | solution.py:657
  74.7 11.6 %collective-permute-start.10 = (f32[72,256]{1,0:T(8,128)S(1)}, f32[72,256]{1,0:T(8,128)S(1)}, u32[]{:S(2)}, u32[]{:S(2)}) collective-permute-start(f32[72,256]{1,0:T(8,128)S(1)} %get-tuple-element.108), channel_id=1, source_target_pairs={{0,2},{1,3},{2,0},{3,1},{4,6},{5,7},{6,4},{7,5},{8,10},{9,11},{10,... | collective-permute-start | bytes 221192 | tf_op jit(solution)/shard_map/ppermute | solution.py:657
  77.6 10.7 %collective-permute-start.11 = (f32[72,256]{1,0:T(8,128)S(1)}, f32[72,256]{1,0:T(8,128)S(1)}, u32[]{:S(2)}, u32[]{:S(2)}) collective-permute-start(f32[72,256]{1,0:T(8,128)S(1)} %get-tuple-element.109), channel_id=1, source_target_pairs={{0,3},{1,2},{2,1},{3,0},{4,7},{5,6},{6,5},{7,4},{8,11},{9,10},{10,... | collective-permute-start | bytes 221192 | tf_op jit(solution)/shard_map/ppermute | solution.py:657
  77.6 12.8 %collective-permute-start.6 = (bf16[32,2048]{1,0:T(8,128)(2,1)S(1)}, bf16[32,2048]{1,0:T(8,128)(2,1)S(1)}, u32[]{:S(2)}, u32[]{:S(2)}) collective-permute-start(bf16[32,2048]{1,0:T(8,128)(2,1)S(1)} %get-tuple-element.94), channel_id=1, source_target_pairs={{0,1},{1,0},{2,3},{3,2},{4,5},{5,4},{6,7},{7,6},{8,9},{9,8},{10,11... | collective-permute-start | bytes 393224 | tf_op jit(solution)/shard_map/ppermute | solution.py:657
  78.3 13.2 %collective-permute-start.7 = (bf16[32,2048]{1,0:T(8,128)(2,1)S(1)}, bf16[32,2048]{1,0:T(8,128)(2,1)S(1)}, u32[]{:S(2)}, u32[]{:S(2)}) collective-permute-start(bf16[32,2048]{1,0:T(8,128)(2,1)S(1)} %get-tuple-element.95), channel_id=1, source_target_pairs={{0,2},{1,3},{2,0},{3,1},{4,6},{5,7},{6,4},{7,5},{8,10},{9,11},{10,... | collective-permute-start | bytes 393224 | tf_op jit(solution)/shard_map/ppermute | solution.py:657
  86.3 7.0 %collective-permute-start.8 = (bf16[32,2048]{1,0:T(8,128)(2,1)S(1)}, bf16[32,2048]{1,0:T(8,128)(2,1)S(1)}, u32[]{:S(2)}, u32[]{:S(2)}) collective-permute-start(bf16[32,2048]{1,0:T(8,128)(2,1)S(1)} %get-tuple-element.96), channel_id=1, source_target_pairs={{0,3},{1,2},{2,1},{3,0},{4,7},{5,6},{6,5},{7,4},{8,11},{9,10},{10,... | collective-permute-start | bytes 393224 | tf_op jit(solution)/shard_map/ppermute | solution.py:657
  88.4 8.3 %copy-start.10 = (f32[72,256]{1,0:T(8,128)}, f32[72,256]{1,0:T(8,128)S(1)}, u32[]{:S(2)}) copy-start(f32[72,256]{1,0:T(8,128)S(1)} %add_add_fusion.2) | copy-start | bytes 221188
  88.4 8.3 %collective-permute-start.14 = (f32[72,256]{1,0:T(8,128)S(1)}, f32[72,256]{1,0:T(8,128)S(1)}, u32[]{:S(2)}, u32[]{:S(2)}) collective-permute-start(f32[72,256]{1,0:T(8,128)S(1)} %add_add_fusion.2), channel_id=1, source_target_pairs={{0,96},{1,97},{2,98},{3,99},{4,100},{5,101},{6,102},{7,103},{8,104... | collective-permute-start | bytes 221192 | tf_op jit(solution)/shard_map/ppermute | solution.py:657
  90.4 6.6 %collective-permute-start.13 = (f32[72,256]{1,0:T(8,128)S(1)}, f32[72,256]{1,0:T(8,128)S(1)}, u32[]{:S(2)}, u32[]{:S(2)}) collective-permute-start(f32[72,256]{1,0:T(8,128)S(1)} %add_add_fusion.2), channel_id=1, source_target_pairs={{0,64},{1,65},{2,66},{3,67},{4,68},{5,69},{6,70},{7,71},{8,72},{9,... | collective-permute-start | bytes 221192 | tf_op jit(solution)/shard_map/ppermute | solution.py:657
  91.6 5.5 %collective-permute-start.12 = (f32[72,256]{1,0:T(8,128)S(1)}, f32[72,256]{1,0:T(8,128)S(1)}, u32[]{:S(2)}, u32[]{:S(2)}) collective-permute-start(f32[72,256]{1,0:T(8,128)S(1)} %add_add_fusion.2), channel_id=1, source_target_pairs={{0,32},{1,33},{2,34},{3,35},{4,36},{5,37},{6,38},{7,39},{8,40},{9,... | collective-permute-start | bytes 221192 | tf_op jit(solution)/shard_map/ppermute | solution.py:657
  96.6 9.4 %copy-start.6 = (bf16[96,2048]{1,0:T(8,128)(2,1)S(1)}, bf16[96,2048]{1,0:T(8,128)(2,1)}, u32[]{:S(2)}) copy-start(bf16[96,2048]{1,0:T(8,128)(2,1)} %copy-done.5) | copy-start | bytes 1179652
  96.6 9.6 %copy-start.4 = (bf16[96,2048]{1,0:T(8,128)(2,1)S(1)}, bf16[96,2048]{1,0:T(8,128)(2,1)}, u32[]{:S(2)}) copy-start(bf16[96,2048]{1,0:T(8,128)(2,1)} %copy-done.3) | copy-start | bytes 1179652
  97.9 35.9 %all-to-all-start.2 = ((bf16[32,5,32,128]{3,2,1,0:T(8,128)(2,1)}), bf16[32,5,32,128]{3,2,1,0:T(8,128)(2,1)}, u32[]{:S(2)}, u32[]{:S(2)}) async-start(bf16[32,5,32,128]{3,2,1,0:T(8,128)(2,1)} %get-tuple-element.118), calls=%async_computation.2 | async-start | bytes 2621440 | tf_op jit(solution)/shard_map/all_to_all | solution.py:663
  106.1 5.4 %copy-start.11 = (f32[72,256]{1,0:T(8,128)S(1)}, f32[72,256]{1,0:T(8,128)}, u32[]{:S(2)}) copy-start(f32[72,256]{1,0:T(8,128)} %copy-done.10) | copy-start | bytes 221188
  106.1 5.4 %copy-start.13 = (f32[72,256]{1,0:T(8,128)S(1)}, f32[72,256]{1,0:T(8,128)}, u32[]{:S(2)}) copy-start(f32[72,256]{1,0:T(8,128)} %copy-done.12) | copy-start | bytes 221188
  106.1 5.4 %copy-start.15 = (f32[72,256]{1,0:T(8,128)S(1)}, f32[72,256]{1,0:T(8,128)}, u32[]{:S(2)}) copy-start(f32[72,256]{1,0:T(8,128)} %copy-done.14) | copy-start | bytes 221188
  106.1 27.6 %collective-permute-start.16 = (bf16[96,2048]{1,0:T(8,128)(2,1)S(1)}, bf16[96,2048]{1,0:T(8,128)(2,1)S(1)}, u32[]{:S(2)}, u32[]{:S(2)}) collective-permute-start(bf16[96,2048]{1,0:T(8,128)(2,1)S(1)} %copy-done.6), channel_id=1, source_target_pairs={{0,1},{1,0},{2,3},{3,2},{4,5},{5,4},{6,7},{7,6},{8,9},{9,8},{10,11... | collective-permute-start | bytes 1179656 | tf_op jit(solution)/shard_map/ppermute | solution.py:657
  106.2 27.5 %collective-permute-start.17 = (bf16[96,2048]{1,0:T(8,128)(2,1)S(1)}, bf16[96,2048]{1,0:T(8,128)(2,1)S(1)}, u32[]{:S(2)}, u32[]{:S(2)}) collective-permute-start(bf16[96,2048]{1,0:T(8,128)(2,1)S(1)} %copy-done.4), channel_id=1, source_target_pairs={{0,3},{1,2},{2,1},{3,0},{4,7},{5,6},{6,5},{7,4},{8,11},{9,10},{10,... | collective-permute-start | bytes 1179656 | tf_op jit(solution)/shard_map/ppermute | solution.py:657
  111.5 16.1 %collective-permute-start.20 = (f32[72,256]{1,0:T(8,128)S(1)}, f32[72,256]{1,0:T(8,128)S(1)}, u32[]{:S(2)}, u32[]{:S(2)}) collective-permute-start(f32[72,256]{1,0:T(8,128)S(1)} %add_add_fusion.1), channel_id=1, source_target_pairs={{0,24},{1,25},{2,26},{3,27},{4,28},{5,29},{6,30},{7,31},{8,16},{9,... | collective-permute-start | bytes 221192 | tf_op jit(solution)/shard_map/ppermute | solution.py:657
  114.5 13.1 %collective-permute-start.19 = (f32[72,256]{1,0:T(8,128)S(1)}, f32[72,256]{1,0:T(8,128)S(1)}, u32[]{:S(2)}, u32[]{:S(2)}) collective-permute-start(f32[72,256]{1,0:T(8,128)S(1)} %add_add_fusion.1), channel_id=1, source_target_pairs={{0,16},{1,17},{2,18},{3,19},{4,20},{5,21},{6,22},{7,23},{8,24},{9,... | collective-permute-start | bytes 221192 | tf_op jit(solution)/shard_map/ppermute | solution.py:657
  115.4 12.2 %collective-permute-start.18 = (f32[72,256]{1,0:T(8,128)S(1)}, f32[72,256]{1,0:T(8,128)S(1)}, u32[]{:S(2)}, u32[]{:S(2)}) collective-permute-start(f32[72,256]{1,0:T(8,128)S(1)} %add_add_fusion.1), channel_id=1, source_target_pairs={{0,8},{1,9},{2,10},{3,11},{4,12},{5,13},{6,14},{7,15},{8,0},{9,1},... | collective-permute-start | bytes 221192 | tf_op jit(solution)/shard_map/ppermute | solution.py:657
  127.6 5.5 %collective-permute-start.21 = (f32[72,256]{1,0:T(8,128)S(1)}, f32[72,256]{1,0:T(8,128)S(1)}, u32[]{:S(2)}, u32[]{:S(2)}) collective-permute-start(f32[72,256]{1,0:T(8,128)S(1)} %add_add_fusion.refs_0_), channel_id=1, source_target_pairs={{0,4},{1,5},{2,6},{3,7},{4,0},{5,1},{6,2},{7,3},{8,12},{9,13},{10,... | collective-permute-start | bytes 221192 | tf_op jit(solution)/shard_map/ppermute | solution.py:657
  (11 other events, 17.6 us)

commit v3 on v2

--- a/solution.py
+++ b/solution.py
@@ -387,11 +387,11 @@
 
 def dense_kernel(
     p0, p1, p2, p3, m0, m1, m2, m3, inverse_ref, down_ref, bias_ref, back_w_ref,
-    b0, b1, b2, b3, grad_ref, h0, h1, h2, h3, helds, sems,
+    b0, b1, b2, b3, grad_ref, h0, h1, h2, h3, s0, s1, s2, s3, helds, selfs, sems,
 ):
     cols, rows = m0.shape
     pieces = (p0, p1, p2, p3)
-    part = h0.shape[0] - cols
+    part = h0.shape[0]
     width = 2 * BLK
 
     def project(i):
@@ -407,7 +407,7 @@
             u = half[here] + bias_ref[here]
             t = jnp.tanh(u)
             s = 1.0 + t
-            helds[k, 0:part, at] = (u * s).astype(BF)
+            helds[k, :, at] = (u * s).astype(BF)
             c = p[cols : cols + part, at].astype(F32)
             grads.append((c * s * (1.0 + u * (1.0 - t))).astype(BF))
         return jnp.concatenate(grads, axis=0)
@@ -420,7 +420,7 @@
         for k, b in enumerate((b0, b1, b2, b3)):
             b[:, at] = backs[k * cols : (k + 1) * cols].astype(BF)
             own = both[(4 + k) * cols : (5 + k) * cols]
-            helds[k, part:, at] = own.astype(BF)
+            selfs[k, :, at] = own.astype(BF)
 
     count = rows // width
     half, grad = project(0), None
@@ -430,11 +430,14 @@
         if grad is not None:
             products(i - 1, grad)
         half, grad = later, fresh
-    products(count - 1, grad)
     sends = []
     for k, h in enumerate((h0, h1, h2, h3)):
         sends.append(pltpu.make_async_copy(helds.at[k], h, sems.at[k]))
         sends[-1].start()
+    products(count - 1, grad)
+    for k, s in enumerate((s0, s1, s2, s3)):
+        sends.append(pltpu.make_async_copy(selfs.at[k], s, sems.at[4 + k]))
+        sends[-1].start()
     for send in sends:
         send.wait()
 
@@ -445,12 +448,17 @@
     return call(
         dense_kernel,
         "dense",
-        12 * "v" + ">vvvvvhhhh",
+        12 * "v" + ">vvvvvhhhhhhhh",
         (*pieces, *ms, inverse, down, bias, back_w),
         4 * (((cols, rows), BF),)
         + (((hidden, rows), BF),)
-        + 4 * (((hidden // 4 + cols, rows), BF),),
-        scratch=[pltpu.VMEM((4, hidden // 4 + cols, rows), BF), DMA((4,))],
+        + 4 * (((hidden // 4, rows), BF),)
+        + 4 * (((cols, rows), BF),),
+        scratch=[
+            pltpu.VMEM((4, hidden // 4, rows), BF),
+            pltpu.VMEM((4, cols, rows), BF),
+            DMA((8,)),
+        ],
         flops=2 * rows * hidden * 400,
     )
 
@@ -566,47 +574,64 @@
 
 
 def collect_kernel(
-    place_ref, asked_ref, start_ref, in_ref, h0, h1, h2, h3,
-    out_ref, hidden_ref, total, held, selfs, table, sems,
+    place_ref, asked_ref, start_ref, in_ref, h0, h1, h2, h3, s0, s1, s2, s3,
+    out_ref, hidden_out, total, second, held, selfs, hidden_ref, table, sems, in_sems, out_sems,
 ):
     feat = place_ref[0]
-    (cols, rows), part = total.shape, h0.shape[1]
-    hidden = h0.shape[0] - cols
+    steps = in_sems.shape[0]
+    group = held.shape[0] // steps
+
+    def arrive(j):
+        at = pl.ds(j * group, group)
+        return pltpu.make_async_copy(in_ref.at[at], held.at[at], in_sems.at[j])
+
+    rows, part = total.shape[1], h0.shape[1]
     copies = [
         pltpu.make_async_copy(asked_ref.at[:, 0, :], table, sems.at[0]),
         pltpu.make_async_copy(start_ref, total, sems.at[1]),
-        pltpu.make_async_copy(in_ref, held, sems.at[2]),
     ]
-    for k, h in enumerate((h0, h1, h2, h3)):
-        copies.append(pltpu.make_async_copy(h.at[hidden:], selfs.at[k], sems.at[3 + k]))
+    for k, s in enumerate((s0, s1, s2, s3)):
+        copies.append(pltpu.make_async_copy(s, selfs.at[k], sems.at[2 + k]))
     for k, h in enumerate((h0, h1, h2, h3)):
         at = near_rows(feat, k, part)
-        copies.append(
-            pltpu.make_async_copy(h.at[0:hidden], hidden_ref.at[:, at], sems.at[7 + k])
-        )
-    for copy in copies:
+        copies.append(pltpu.make_async_copy(h, hidden_ref.at[:, at], sems.at[6 + k]))
+    for copy in copies[:6]:
+        copy.start()
+    for j in range(steps):
+        arrive(j).start()
+    for copy in copies[6:]:
         copy.start()
     copies[1].wait()
     for k in range(4):
-        copies[3 + k].wait()
+        copies[2 + k].wait()
         at = near_rows(feat, k, part)
         total[:, at] = total[:, at] + selfs[k].astype(F32)
     copies[0].wait()
-    copies[2].wait()
+
+    def body(p, carry):
+        for s in range(CAP):
+            at = lanes(table[p, s])
+            sums = second if s % 2 else total
+            sums[:, at] = sums[:, at] + held[p, s].astype(F32)
+        return carry
+
+    second[...] = jnp.zeros_like(second)
+    sends = []
+    for j in range(steps):
+        arrive(j).wait()
+        lax.fori_loop(j * group, (j + 1) * group, body, 0, unroll=4)
+        copies[6 + j].wait()
+        at = near_rows(feat, j, part)
+        sends.append(
+            pltpu.make_async_copy(hidden_ref.at[:, at], hidden_out.at[:, at], out_sems.at[j])
+        )
+        sends[-1].start()
     below, above = [near_loop(place_ref[1], d, held.shape[0]) for d in (-1, 1)]
     total[:, 0:BLK] += held[below, CAP].astype(F32)
     total[:, rows - BLK :] += held[above, CAP].astype(F32)
-
-    def body(p, carry):
-        for s in range(CAP):
-            at = lanes(table[p, s])
-            total[:, at] = total[:, at] + held[p, s].astype(F32)
-        return carry
-
-    lax.fori_loop(0, held.shape[0], body, 0, unroll=4)
-    out_ref[...] = total[...].astype(BF)
-    for copy in copies[7:]:
-        copy.wait()
+    out_ref[...] = (total[...] + second[...]).astype(BF)
+    for send in sends:
+        send.wait()
 
 
 def collect(place, asked, band_sum, incoming, outs):
@@ -614,15 +639,19 @@
     return call(
         collect_kernel,
         "collect",
-        "saah" + 4 * "h" + ">ww",
+        "saah" + 8 * "h" + ">wh",
         (place, asked, band_sum, incoming, *outs),
-        ((band_sum.shape, BF), ((outs[0].shape[0] - cols, rows), BF)),
+        ((band_sum.shape, BF), ((outs[0].shape[0], rows), BF)),
         scratch=[
+            pltpu.VMEM(band_sum.shape, F32),
             pltpu.VMEM(band_sum.shape, F32),
             pltpu.VMEM(incoming.shape, BF),
             pltpu.VMEM((4, cols, rows // 4), BF),
+            pltpu.VMEM((outs[0].shape[0], rows), BF),
             pltpu.SMEM((asked.shape[0], BLK), I32),
-            DMA((11,)),
+            DMA((10,)),
+            DMA((4,)),
+            DMA((4,)),
         ],
     )
 
@@ -678,28 +707,30 @@
     ms = swapped(ms)
     down, bias_down, back_w = weights(place, pieces, cols, w_self.shape[1])
     ms, down = together((ms, down))
-    *rest, h0, h1, h2, h3 = dense(pieces, ms, inverse, down, bias_down, back_w)
+    *rest, h0, h1, h2, h3, s0, s1, s2, s3 = dense(pieces, ms, inverse, down, bias_down, back_w)
     *backs, grad = rest
     backs = swapped(backs)
     terms = after(place, pieces, ms, grad)
     near = swapped(terms)
-    o2 = swap(h2, 2)
-    backs, h1, h3 = together((backs, h1, h3))
+    selfs = swapped([s0, s1, s2, s3])
     outgoing, back = off_backward(place, off_row, key, backs, off, band_blocks, loop_size)
     grads = (near[0] + near[1]) + (near[2] + near[3])
     one, two, three = [swap(grads, 0, j) for j in (8, 16, 24)]
-    outgoing, back, one, two, three, o2, h1, h3 = together(
-        (outgoing, back, one, two, three, o2, h1, h3)
+    outs = [h0, h1, h2, h3]
+    outgoing, back, one, two, three, selfs, outs = together(
+        (outgoing, back, one, two, three, selfs, outs)
     )
     incoming = spread(outgoing)
-    outs = [h0, swap(h1, 1), o2, swap(h3, 3)]
+    outs = [outs[0], outs[1], swap(outs[2], 2), swap(outs[3], 3)]
     back_sum = band_backward(back, band_blocks)
-    one, two, three, back_sum = together((one, two, three, back_sum))
     grads = (grads + one) + (two + three)
     one, two, three = [swap(grads, 0, j) for j in (2, 4, 6)]
+    one, two, three, outs[1] = together((one, two, three, outs[1]))
+    outs[1] = swap(outs[1], 1)
     grads = (grads + one) + (two + three)
     other = swap(grads, 0, 1)
-    grad_features, hidden = collect(place, asked, back_sum, incoming, outs)
+    grad_features, hidden = collect(place, asked, back_sum, incoming, outs + selfs)
+    other, grad_features = together((other, grad_features))
     weight_grads, bias_grad = finish(
         grads, other, bias.shape[0], 0.5 / math.sqrt(rows * loop_size)
     )

time: 140 us -> 139 us (level)
  the two profiles are of different devices: /device:TPU:0 before, /device:TPU:1 now
where the time goes in v3:
time: 139 us
  starting transfers between devices  59.4 us (43%)
  Pallas kernels  36.9 us (27%)
  waiting for transfers between devices  35.9 us (26%)
  local copies, waits for them, and re-layouts  4.39 us (3%)
    ppermute x25, starting transfers between devices, swap(): return lax.ppermute(value, ('loop', 'feat'), pairs)  38.6 us
    pallas_call x12, Pallas kernels, call(): pl.pallas_call(kernel, in_specs=[pl.BlockSpec(memory_space=spaces[p]) for...  36.9 us
    ppermute x25, waiting for transfers between devices, swap(): return lax.ppermute(value, ('loop', 'feat'), pairs)  27.9 us
    all_to_all x3, starting transfers between devices, spread(): lax.all_to_all(value, 'loop', split_axis=0, concat_axis=0, tiled=True)  20.8 us
    all_to_all x3, waiting for transfers between devices, spread(): lax.all_to_all(value, 'loop', split_axis=0, concat_axis=0, tiled=True)  7.94 us
    unnamed x40, local copies, waits for them, and re-layouts  4.39 us
  transfers between devices with their start and end apart: 28, of which 10 were waited for; matrix products, arithmetic and copies ran while one was open for 1% of the time, Pallas kernels for 20%

profile of v3, /device:TPU:1, one launch (start us, length us, event | category | flops | bytes accessed | tf_op | source)
XLA Modules:
  0.0 138.6 jit_solution(10150502105823777427)
XLA Ops:
  0.7 1.8 %prepare.1 = (s32[1,64]{1,0:T(1,128)S(1)}, s32[32,1,128]{2,1,0:T(1,128)}) custom-call(s32[1,64]{1,0:T(1,128)} %bitcast.19, s32[1,64]{1,0:T(1,128)} %bitcast.20), custom_call_target="tpu_custom_call" | custom-call | flops 1 | bytes 1 | tf_op jit(solution)/shard_map/prepare/pallas_call | solution.py:43
  2.5 9.7 %all-to-all-start = ((s32[32,1,128]{2,1,0:T(1,128)}), s32[32,1,128]{2,1,0:T(1,128)S(1)}, u32[]{:S(2)}, u32[]{:S(2)}) async-start(s32[32,1,128]{2,1,0:T(1,128)} %get-tuple-element.74), calls=%async_computation | async-start | bytes 32768 | tf_op jit(solution)/shard_map/all_to_all | solution.py:692
  12.2 2.9 %by_device.1 = (bf16[112,2048]{1,0:T(8,128)(2,1)S(1)}, bf16[112,2048]{1,0:T(8,128)(2,1)}, bf16[112,2048]{1,0:T(8,128)(2,1)}, bf16[112,2048]{1,0:T(8,128)(2,1)}) custom-call(s32[2]{0:T(128)S(1)} %pad_add_fusion.place_ref.tie_ref.feat_ref, bf16[32,8192]{1,0:T(8,128)(2,1)} %bitcast.11, bf16[64,8192]{1,0:T(8,128)(2,1)} %bitcast.14, bf16[32,256]{1,0:T(8,128)(2,1)} %self_in.1, ...), custom_call_target="tpu_custom_call" | custom-call | flops 1 | bytes 1 | tf_op jit(solution)/shard_map/by_device/pallas_call | solution.py:43
  15.2 4.1 %all-to-all-done.asked_ref = s32[32,1,128]{2,1,0:T(1,128)S(1)} async-done(((s32[32,1,128]{2,1,0:T(1,128)}), s32[32,1,128]{2,1,0:T(1,128)S(1)}, u32[]{:S(2)}, u32[]{:S(2)}) %all-to-all-start) | async-done | bytes 16416 | tf_op jit(solution)/shard_map/all_to_all | solution.py:692
  19.2 2.8 %answers.1 = bf16[32,5,32,128]{3,2,1,0:T(8,128)(2,1)} custom-call(s32[2]{0:T(128)S(1)} %pad_add_fusion.place_ref.tie_ref.feat_ref, s32[32,1,128]{2,1,0:T(1,128)S(1)} %all-to-all-done.asked_ref, bf16[32,8192]{1,0:T(8,128)(2,1)} %bitcast.12), custom_call_target="tpu_custom_call" | custom-call | flops 1 | bytes 1 | tf_op jit(solution)/shard_map/answers/pallas_call | solution.py:43
  22.0 4.7 %all-to-all-start.1 = ((bf16[32,5,32,128]{3,2,1,0:T(8,128)(2,1)}), bf16[32,5,32,128]{3,2,1,0:T(8,128)(2,1)}, u32[]{:S(2)}, u32[]{:S(2)}) async-start(bf16[32,5,32,128]{3,2,1,0:T(8,128)(2,1)} %answers.1), calls=%async_computation.1 | async-start | bytes 2621440 | tf_op jit(solution)/shard_map/all_to_all | solution.py:692
  26.7 2.2 %collective-permute-start = (bf16[112,2048]{1,0:T(8,128)(2,1)}, bf16[112,2048]{1,0:T(8,128)(2,1)S(1)}, u32[]{:S(2)}, u32[]{:S(2)}) collective-permute-start(bf16[112,2048]{1,0:T(8,128)(2,1)} %get-tuple-element.78), channel_id=1, source_target_pairs={{0,1},{1,0},{2,3},{3,2},{4,5},{5,4},{6,7},{7,6},{8,9},{9,8},{10,11... | collective-permute-start | bytes 1376264 | tf_op jit(solution)/shard_map/ppermute | solution.py:686
  28.9 2.6 %collective-permute-start.1 = (bf16[112,2048]{1,0:T(8,128)(2,1)}, bf16[112,2048]{1,0:T(8,128)(2,1)S(1)}, u32[]{:S(2)}, u32[]{:S(2)}) collective-permute-start(bf16[112,2048]{1,0:T(8,128)(2,1)} %get-tuple-element.79), channel_id=1, source_target_pairs={{0,2},{1,3},{2,0},{3,1},{4,6},{5,7},{6,4},{7,5},{8,10},{9,11},{10,... | collective-permute-start | bytes 1376264 | tf_op jit(solution)/shard_map/ppermute | solution.py:686
  32.1 7.3 %band_forward.1 = (f32[48,8192]{1,0:T(8,128)S(1)}, bf16[64,128,128]{2,1,0:T(8,128)(2,1)S(1)}) custom-call(s32[2]{0:T(128)S(1)} %pad_add_fusion.place_ref.tie_ref.feat_ref, bf16[64,3,128,128]{3,2,1,0:T(8,128)(2,1)} %a_ref.3, bf16[64,128,128]{2,1,0:T(8,128)(2,1)} %off_ref.1, bf16[32,8192]{1,0:T(8,128)(2,1)} %bitcast.13), custom_call_target="tpu_custom_call" | custom-call | flops 1 | bytes 1 | tf_op jit(solution)/shard_map/band_forward/pallas_call | solution.py:43
  40.7 3.9 %all-to-all-done.1.panel_in = bf16[32,5,32,128]{3,2,1,0:T(8,128)(2,1)} async-done(((bf16[32,5,32,128]{3,2,1,0:T(8,128)(2,1)}), bf16[32,5,32,128]{3,2,1,0:T(8,128)(2,1)}, u32[]{:S(2)}, u32[]{:S(2)}) %all-to-all-start.1) | async-done | bytes 1310752 | tf_op jit(solution)/shard_map/all_to_all | solution.py:692
  44.6 4.1 %off_forward.1 = (bf16[32,2048]{1,0:T(8,128)(2,1)S(1)}, bf16[32,2048]{1,0:T(8,128)(2,1)S(1)}, bf16[32,2048]{1,0:T(8,128)(2,1)S(1)}, bf16[32,2048]{1,0:T(8,128)(2,1)S(1)}, f32[1,2048]{1,0:T(1,128)S(1)}) custom-call(s32[2]{0:T(128)S(1)} %pad_add_fusion.place_ref.tie_ref.feat_ref, s32[64]{0:T(128)S(1)} %copy-done.3, s32[1,64]{1,0:T(1,128)S(1)} %get-tuple-element.77.key_ref, ...), custom_call_target="tpu_custom_call" | custom-call | flops 1 | bytes 1 | tf_op jit(solution)/shard_map/off_forward/pallas_call | solution.py:43
  48.7 3.4 %collective-permute-start.3 = (bf16[32,2048]{1,0:T(8,128)(2,1)S(1)}, bf16[32,2048]{1,0:T(8,128)(2,1)S(1)}, u32[]{:S(2)}, u32[]{:S(2)}) collective-permute-start(bf16[32,2048]{1,0:T(8,128)(2,1)S(1)} %get-tuple-element.86), channel_id=1, source_target_pairs={{0,1},{1,0},{2,3},{3,2},{4,5},{5,4},{6,7},{7,6},{8,9},{9,8},{10,11... | collective-permute-start | bytes 393224 | tf_op jit(solution)/shard_map/ppermute | solution.py:686
  52.1 2.6 %collective-permute-start.4 = (bf16[32,2048]{1,0:T(8,128)(2,1)S(1)}, bf16[32,2048]{1,0:T(8,128)(2,1)S(1)}, u32[]{:S(2)}, u32[]{:S(2)}) collective-permute-start(bf16[32,2048]{1,0:T(8,128)(2,1)S(1)} %get-tuple-element.87), channel_id=1, source_target_pairs={{0,2},{1,3},{2,0},{3,1},{4,6},{5,7},{6,4},{7,5},{8,10},{9,11},{10,... | collective-permute-start | bytes 393224 | tf_op jit(solution)/shard_map/ppermute | solution.py:686
  55.3 10.7 %collective-permute-done.2.p3 = bf16[112,2048]{1,0:T(8,128)(2,1)} collective-permute-done((bf16[112,2048]{1,0:T(8,128)(2,1)}, bf16[112,2048]{1,0:T(8,128)(2,1)}, u32[]{:S(2)}, u32[]{:S(2)}) %collective-permute-start.2) | collective-permute-done | bytes 458784 | tf_op jit(solution)/shard_map/ppermute | solution.py:686
  67.3 2.3 %collective-permute-done.5.m3 = bf16[32,2048]{1,0:T(8,128)(2,1)S(1)} collective-permute-done((bf16[32,2048]{1,0:T(8,128)(2,1)S(1)}, bf16[32,2048]{1,0:T(8,128)(2,1)S(1)}, u32[]{:S(2)}, u32[]{:S(2)}) %collective-permute-start.5) | collective-permute-done | bytes 131104 | tf_op jit(solution)/shard_map/ppermute | solution.py:686
  69.6 3.5 %dense.1 = (bf16[32,2048]{1,0:T(8,128)(2,1)S(1)}, bf16[32,2048]{1,0:T(8,128)(2,1)S(1)}, bf16[32,2048]{1,0:T(8,128)(2,1)S(1)}, bf16[32,2048]{1,0:T(8,128)(2,1)S(1...) custom-call(bf16[112,2048]{1,0:T(8,128)(2,1)S(1)} %get-tuple-element, ...), custom_call_target="tpu_custom_call" | custom-call | flops 1 | bytes 1 | tf_op jit(solution)/shard_map/dense/pallas_call | solution.py:43
  74.5 1.8 %after.1 = (f32[72,256]{1,0:T(8,128)S(1)}, f32[72,256]{1,0:T(8,128)S(1)}, f32[72,256]{1,0:T(8,128)S(1)}, f32[72,256]{1,0:T(8,128)S(1)}) custom-call(s32[2]{0:T(128)S(1)} %pad_add_fusion.place_ref.tie_ref.feat_ref, bf16[112,2048]{1,0:T(8,128)(2,1)S(1)} %get-tuple-element.75.p0, bf16[112,2048]{1,0:T(8,128)(2,1)S(1)} %collective-permute-done.p1, ...), custom_call_target="tpu_custom_call" | custom-call | flops 1 | bytes 1 | tf_op jit(solution)/shard_map/after/pallas_call | solution.py:43
  77.0 3.0 %collective-permute-start.11 = (f32[72,256]{1,0:T(8,128)S(1)}, f32[72,256]{1,0:T(8,128)S(1)}, u32[]{:S(2)}, u32[]{:S(2)}) collective-permute-start(f32[72,256]{1,0:T(8,128)S(1)} %get-tuple-element.108), channel_id=1, source_target_pairs={{0,3},{1,2},{2,1},{3,0},{4,7},{5,6},{6,5},{7,4},{8,11},{9,10},{10,... | collective-permute-start | bytes 221192 | tf_op jit(solution)/shard_map/ppermute | solution.py:686
  80.4 2.8 %collective-permute-start.8 = (bf16[32,2048]{1,0:T(8,128)(2,1)S(1)}, bf16[32,2048]{1,0:T(8,128)(2,1)S(1)}, u32[]{:S(2)}, u32[]{:S(2)}) collective-permute-start(bf16[32,2048]{1,0:T(8,128)(2,1)S(1)} %get-tuple-element.101), channel_id=1, source_target_pairs={{0,3},{1,2},{2,1},{3,0},{4,7},{5,6},{6,5},{7,4},{8,11},{9,10},{10,... | collective-permute-start | bytes 393224 | tf_op jit(solution)/shard_map/ppermute | solution.py:686
  83.8 2.0 %collective-permute-start.16 = (bf16[32,2048]{1,0:T(8,128)(2,1)S(1)}, bf16[32,2048]{1,0:T(8,128)(2,1)S(1)}, u32[]{:S(2)}, u32[]{:S(2)}) collective-permute-start(bf16[32,2048]{1,0:T(8,128)(2,1)S(1)} %get-tuple-element.111), channel_id=1, source_target_pairs={{0,2},{1,3},{2,0},{3,1},{4,6},{5,7},{6,4},{7,5},{8,10},{9,11},{10,... | collective-permute-start | bytes 393224 | tf_op jit(solution)/shard_map/ppermute | solution.py:686
  87.0 2.4 %collective-permute-start.14 = (f32[72,256]{1,0:T(8,128)S(1)}, f32[72,256]{1,0:T(8,128)S(1)}, u32[]{:S(2)}, u32[]{:S(2)}) collective-permute-start(f32[72,256]{1,0:T(8,128)S(1)} %add_add_fusion.2), channel_id=1, source_target_pairs={{0,96},{1,97},{2,98},{3,99},{4,100},{5,101},{6,102},{7,103},{8,104... | collective-permute-start | bytes 221192 | tf_op jit(solution)/shard_map/ppermute | solution.py:686
  90.0 3.0 %collective-permute-start.13 = (f32[72,256]{1,0:T(8,128)S(1)}, f32[72,256]{1,0:T(8,128)S(1)}, u32[]{:S(2)}, u32[]{:S(2)}) collective-permute-start(f32[72,256]{1,0:T(8,128)S(1)} %add_add_fusion.2), channel_id=1, source_target_pairs={{0,64},{1,65},{2,66},{3,67},{4,68},{5,69},{6,70},{7,71},{8,72},{9,... | collective-permute-start | bytes 221192 | tf_op jit(solution)/shard_map/ppermute | solution.py:686
  93.0 3.3 %off_backward.1 = (bf16[32,5,32,128]{3,2,1,0:T(8,128)(2,1)}, bf16[32,8192]{1,0:T(8,128)(2,1)S(1)}) custom-call(s32[2]{0:T(128)S(1)} %pad_add_fusion.place_ref.tie_ref.feat_ref, s32[64]{0:T(128)S(1)} %copy-done.3, s32[1,64]{1,0:T(1,128)S(1)} %get-tuple-element.77.key_ref, bf16[32,2048]{1,0:T(8,128)(2,1)S(1)} %get-tuple-element.98.b0, ...), custom_call_target="tpu_custom_call" | custom-call | flops 1 | bytes 1 | tf_op jit(solution)/shard_map/off_backward/pallas_call | solution.py:43
  97.7 6.4 %all-to-all-start.2 = ((bf16[32,5,32,128]{3,2,1,0:T(8,128)(2,1)}), bf16[32,5,32,128]{3,2,1,0:T(8,128)(2,1)}, u32[]{:S(2)}, u32[]{:S(2)}) async-start(bf16[32,5,32,128]{3,2,1,0:T(8,128)(2,1)} %get-tuple-element.118), calls=%async_computation.2 | async-start | bytes 2621440 | tf_op jit(solution)/shard_map/all_to_all | solution.py:692
  105.0 2.5 %collective-permute-start.20 = (f32[72,256]{1,0:T(8,128)S(1)}, f32[72,256]{1,0:T(8,128)S(1)}, u32[]{:S(2)}, u32[]{:S(2)}) collective-permute-start(f32[72,256]{1,0:T(8,128)S(1)} %add_add_fusion.1), channel_id=1, source_target_pairs={{0,24},{1,25},{2,26},{3,27},{4,28},{5,29},{6,30},{7,31},{8,16},{9,... | collective-permute-start | bytes 221192 | tf_op jit(solution)/shard_map/ppermute | solution.py:686
  108.3 2.1 %collective-permute-start.22 = (bf16[64,2048]{1,0:T(8,128)(2,1)S(1)}, bf16[64,2048]{1,0:T(8,128)(2,1)S(1)}, u32[]{:S(2)}, u32[]{:S(2)}) collective-permute-start(bf16[64,2048]{1,0:T(8,128)(2,1)S(1)} %copy-done.9), channel_id=1, source_target_pairs={{0,2},{1,3},{2,0},{3,1},{4,6},{5,7},{6,4},{7,5},{8,10},{9,11},{10,... | collective-permute-start | bytes 786440 | tf_op jit(solution)/shard_map/ppermute | solution.py:686
  110.4 2.9 %collective-permute-start.23 = (bf16[64,2048]{1,0:T(8,128)(2,1)S(1)}, bf16[64,2048]{1,0:T(8,128)(2,1)S(1)}, u32[]{:S(2)}, u32[]{:S(2)}) collective-permute-start(bf16[64,2048]{1,0:T(8,128)(2,1)S(1)} %copy-done.7), channel_id=1, source_target_pairs={{0,3},{1,2},{2,1},{3,0},{4,7},{5,6},{6,5},{7,4},{8,11},{9,10},{10,... | collective-permute-start | bytes 786440 | tf_op jit(solution)/shard_map/ppermute | solution.py:686
  113.3 10.9 %collective-permute-done.20 = f32[72,256]{1,0:T(8,128)S(1)} collective-permute-done((f32[72,256]{1,0:T(8,128)S(1)}, f32[72,256]{1,0:T(8,128)S(1)}, u32[]{:S(2)}, u32[]{:S(2)}) %collective-permute-start.20) | collective-permute-done | bytes 73760 | tf_op jit(solution)/shard_map/ppermute | solution.py:686
  124.4 1.4 %collective-permute-start.21 = (bf16[64,2048]{1,0:T(8,128)(2,1)S(1)}, bf16[64,2048]{1,0:T(8,128)(2,1)}, u32[]{:S(2)}, u32[]{:S(2)}) collective-permute-start(bf16[64,2048]{1,0:T(8,128)(2,1)S(1)} %copy-done.5), channel_id=1, source_target_pairs={{0,1},{1,0},{2,3},{3,2},{4,5},{5,4},{6,7},{7,6},{8,9},{9,8},{10,11... | collective-permute-start | bytes 786440 | tf_op jit(solution)/shard_map/ppermute | solution.py:686
  126.8 3.3 %band_backward.1.start_ref = f32[32,8192]{1,0:T(8,128)S(1)} custom-call(bf16[32,8192]{1,0:T(8,128)(2,1)S(1)} %get-tuple-element.117.back_ref, bf16[64,3,128,128]{3,2,1,0:T(8,128)(2,1)} %a_ref.3), custom_call_target="tpu_custom_call" | custom-call | flops 1 | bytes 1 | tf_op jit(solution)/shard_map/band_backward/pallas_call | solution.py:43
  130.1 2.9 %collective-permute-done.23.h3 = bf16[64,2048]{1,0:T(8,128)(2,1)S(1)} collective-permute-done((bf16[64,2048]{1,0:T(8,128)(2,1)S(1)}, bf16[64,2048]{1,0:T(8,128)(2,1)S(1)}, u32[]{:S(2)}, u32[]{:S(2)}) %collective-permute-start.23) | collective-permute-done | bytes 262176 | tf_op jit(solution)/shard_map/ppermute | solution.py:686
  133.8 4.1 %collect.1 = (bf16[32,8192]{1,0:T(8,128)(2,1)}, bf16[64,8192]{1,0:T(8,128)(2,1)}) custom-call(s32[2]{0:T(128)S(1)} %pad_add_fusion.place_ref.tie_ref.feat_ref, s32[32,1,128]{2,1,0:T(1,128)S(1)} %all-to-all-done.asked_ref, f32[32,8192]{1,0:T(8,128)S(1)} %band_backward.1.start_ref, bf16[32,5,32,128]{3,2,1,0:T(8,128)(2,1)} %all-to-all-done.2.in_ref, ...), custom_call_target="tpu_custom_call" | custom-call | flops 1 | bytes 1 | tf_op jit(solution)/shard_map/collect/pallas_call | solution.py:43
  (80 shorter events, 14.1 us)
Async XLA Ops:
  2.5 16.8 %all-to-all-start = ((s32[32,1,128]{2,1,0:T(1,128)}), s32[32,1,128]{2,1,0:T(1,128)S(1)}, u32[]{:S(2)}, u32[]{:S(2)}) async-start(s32[32,1,128]{2,1,0:T(1,128)} %get-tuple-element.74), calls=%async_computation | async-start | bytes 32768 | tf_op jit(solution)/shard_map/all_to_all | solution.py:692
  22.0 22.5 %all-to-all-start.1 = ((bf16[32,5,32,128]{3,2,1,0:T(8,128)(2,1)}), bf16[32,5,32,128]{3,2,1,0:T(8,128)(2,1)}, u32[]{:S(2)}, u32[]{:S(2)}) async-start(bf16[32,5,32,128]{3,2,1,0:T(8,128)(2,1)} %answers.1), calls=%async_computation.1 | async-start | bytes 2621440 | tf_op jit(solution)/shard_map/all_to_all | solution.py:692
  26.7 28.0 %collective-permute-start = (bf16[112,2048]{1,0:T(8,128)(2,1)}, bf16[112,2048]{1,0:T(8,128)(2,1)S(1)}, u32[]{:S(2)}, u32[]{:S(2)}) collective-permute-start(bf16[112,2048]{1,0:T(8,128)(2,1)} %get-tuple-element.78), channel_id=1, source_target_pairs={{0,1},{1,0},{2,3},{3,2},{4,5},{5,4},{6,7},{7,6},{8,9},{9,8},{10,11... | collective-permute-start | bytes 1376264 | tf_op jit(solution)/shard_map/ppermute | solution.py:686
  28.9 26.4 %collective-permute-start.1 = (bf16[112,2048]{1,0:T(8,128)(2,1)}, bf16[112,2048]{1,0:T(8,128)(2,1)S(1)}, u32[]{:S(2)}, u32[]{:S(2)}) collective-permute-start(bf16[112,2048]{1,0:T(8,128)(2,1)} %get-tuple-element.79), channel_id=1, source_target_pairs={{0,2},{1,3},{2,0},{3,1},{4,6},{5,7},{6,4},{7,5},{8,10},{9,11},{10,... | collective-permute-start | bytes 1376264 | tf_op jit(solution)/shard_map/ppermute | solution.py:686
  31.6 13.0 %copy-start.3 = (s32[64]{0:T(128)S(1)}, s32[64]{0:T(128)}, u32[]{:S(2)}) copy-start(s32[64]{0:T(128)} %row_ref.3) | copy-start | bytes 772
  31.6 34.4 %collective-permute-start.2 = (bf16[112,2048]{1,0:T(8,128)(2,1)}, bf16[112,2048]{1,0:T(8,128)(2,1)}, u32[]{:S(2)}, u32[]{:S(2)}) collective-permute-start(bf16[112,2048]{1,0:T(8,128)(2,1)} %get-tuple-element.80), channel_id=1, source_target_pairs={{0,3},{1,2},{2,1},{3,0},{4,7},{5,6},{6,5},{7,4},{8,11},{9,10},{10,... | collective-permute-start | bytes 1376264 | tf_op jit(solution)/shard_map/ppermute | solution.py:686
  48.7 18.6 %collective-permute-start.3 = (bf16[32,2048]{1,0:T(8,128)(2,1)S(1)}, bf16[32,2048]{1,0:T(8,128)(2,1)S(1)}, u32[]{:S(2)}, u32[]{:S(2)}) collective-permute-start(bf16[32,2048]{1,0:T(8,128)(2,1)S(1)} %get-tuple-element.86), channel_id=1, source_target_pairs={{0,1},{1,0},{2,3},{3,2},{4,5},{5,4},{6,7},{7,6},{8,9},{9,8},{10,11... | collective-permute-start | bytes 393224 | tf_op jit(solution)/shard_map/ppermute | solution.py:686
  52.1 15.2 %collective-permute-start.4 = (bf16[32,2048]{1,0:T(8,128)(2,1)S(1)}, bf16[32,2048]{1,0:T(8,128)(2,1)S(1)}, u32[]{:S(2)}, u32[]{:S(2)}) collective-permute-start(bf16[32,2048]{1,0:T(8,128)(2,1)S(1)} %get-tuple-element.87), channel_id=1, source_target_pairs={{0,2},{1,3},{2,0},{3,1},{4,6},{5,7},{6,4},{7,5},{8,10},{9,11},{10,... | collective-permute-start | bytes 393224 | tf_op jit(solution)/shard_map/ppermute | solution.py:686
  54.7 14.9 %collective-permute-start.5 = (bf16[32,2048]{1,0:T(8,128)(2,1)S(1)}, bf16[32,2048]{1,0:T(8,128)(2,1)S(1)}, u32[]{:S(2)}, u32[]{:S(2)}) collective-permute-start(bf16[32,2048]{1,0:T(8,128)(2,1)S(1)} %get-tuple-element.88), channel_id=1, source_target_pairs={{0,3},{1,2},{2,1},{3,0},{4,7},{5,6},{6,5},{7,4},{8,11},{9,10},{10,... | collective-permute-start | bytes 393224 | tf_op jit(solution)/shard_map/ppermute | solution.py:686
  74.5 11.2 %collective-permute-start.6 = (bf16[32,2048]{1,0:T(8,128)(2,1)S(1)}, bf16[32,2048]{1,0:T(8,128)(2,1)S(1)}, u32[]{:S(2)}, u32[]{:S(2)}) collective-permute-start(bf16[32,2048]{1,0:T(8,128)(2,1)S(1)} %get-tuple-element.99), channel_id=1, source_target_pairs={{0,1},{1,0},{2,3},{3,2},{4,5},{5,4},{6,7},{7,6},{8,9},{9,8},{10,11... | collective-permute-start | bytes 393224 | tf_op jit(solution)/shard_map/ppermute | solution.py:686
  76.3 4.1 %collective-permute-start.9 = (f32[72,256]{1,0:T(8,128)S(1)}, f32[72,256]{1,0:T(8,128)S(1)}, u32[]{:S(2)}, u32[]{:S(2)}) collective-permute-start(f32[72,256]{1,0:T(8,128)S(1)} %get-tuple-element.106), channel_id=1, source_target_pairs={{0,1},{1,0},{2,3},{3,2},{4,5},{5,4},{6,7},{7,6},{8,9},{9,8},{10,11... | collective-permute-start | bytes 221192 | tf_op jit(solution)/shard_map/ppermute | solution.py:686
  76.7 6.5 %collective-permute-start.10 = (f32[72,256]{1,0:T(8,128)S(1)}, f32[72,256]{1,0:T(8,128)S(1)}, u32[]{:S(2)}, u32[]{:S(2)}) collective-permute-start(f32[72,256]{1,0:T(8,128)S(1)} %get-tuple-element.107), channel_id=1, source_target_pairs={{0,2},{1,3},{2,0},{3,1},{4,6},{5,7},{6,4},{7,5},{8,10},{9,11},{10,... | collective-permute-start | bytes 221192 | tf_op jit(solution)/shard_map/ppermute | solution.py:686
  77.0 6.7 %collective-permute-start.11 = (f32[72,256]{1,0:T(8,128)S(1)}, f32[72,256]{1,0:T(8,128)S(1)}, u32[]{:S(2)}, u32[]{:S(2)}) collective-permute-start(f32[72,256]{1,0:T(8,128)S(1)} %get-tuple-element.108), channel_id=1, source_target_pairs={{0,3},{1,2},{2,1},{3,0},{4,7},{5,6},{6,5},{7,4},{8,11},{9,10},{10,... | collective-permute-start | bytes 221192 | tf_op jit(solution)/shard_map/ppermute | solution.py:686
  80.1 6.9 %collective-permute-start.7 = (bf16[32,2048]{1,0:T(8,128)(2,1)S(1)}, bf16[32,2048]{1,0:T(8,128)(2,1)S(1)}, u32[]{:S(2)}, u32[]{:S(2)}) collective-permute-start(bf16[32,2048]{1,0:T(8,128)(2,1)S(1)} %get-tuple-element.100), channel_id=1, source_target_pairs={{0,2},{1,3},{2,0},{3,1},{4,6},{5,7},{6,4},{7,5},{8,10},{9,11},{10,... | collective-permute-start | bytes 393224 | tf_op jit(solution)/shard_map/ppermute | solution.py:686
  80.4 9.5 %collective-permute-start.8 = (bf16[32,2048]{1,0:T(8,128)(2,1)S(1)}, bf16[32,2048]{1,0:T(8,128)(2,1)S(1)}, u32[]{:S(2)}, u32[]{:S(2)}) collective-permute-start(bf16[32,2048]{1,0:T(8,128)(2,1)S(1)} %get-tuple-element.101), channel_id=1, source_target_pairs={{0,3},{1,2},{2,1},{3,0},{4,7},{5,6},{6,5},{7,4},{8,11},{9,10},{10,... | collective-permute-start | bytes 393224 | tf_op jit(solution)/shard_map/ppermute | solution.py:686
  83.2 9.8 %collective-permute-start.15 = (bf16[32,2048]{1,0:T(8,128)(2,1)S(1)}, bf16[32,2048]{1,0:T(8,128)(2,1)S(1)}, u32[]{:S(2)}, u32[]{:S(2)}) collective-permute-start(bf16[32,2048]{1,0:T(8,128)(2,1)S(1)} %get-tuple-element.110), channel_id=1, source_target_pairs={{0,1},{1,0},{2,3},{3,2},{4,5},{5,4},{6,7},{7,6},{8,9},{9,8},{10,11... | collective-permute-start | bytes 393224 | tf_op jit(solution)/shard_map/ppermute | solution.py:686
  83.8 12.6 %collective-permute-start.16 = (bf16[32,2048]{1,0:T(8,128)(2,1)S(1)}, bf16[32,2048]{1,0:T(8,128)(2,1)S(1)}, u32[]{:S(2)}, u32[]{:S(2)}) collective-permute-start(bf16[32,2048]{1,0:T(8,128)(2,1)S(1)} %get-tuple-element.111), channel_id=1, source_target_pairs={{0,2},{1,3},{2,0},{3,1},{4,6},{5,7},{6,4},{7,5},{8,10},{9,11},{10,... | collective-permute-start | bytes 393224 | tf_op jit(solution)/shard_map/ppermute | solution.py:686
  85.7 10.6 %collective-permute-start.17 = (bf16[32,2048]{1,0:T(8,128)(2,1)S(1)}, bf16[32,2048]{1,0:T(8,128)(2,1)S(1)}, u32[]{:S(2)}, u32[]{:S(2)}) collective-permute-start(bf16[32,2048]{1,0:T(8,128)(2,1)S(1)} %get-tuple-element.112), channel_id=1, source_target_pairs={{0,3},{1,2},{2,1},{3,0},{4,7},{5,6},{6,5},{7,4},{8,11},{9,10},{10,... | collective-permute-start | bytes 393224 | tf_op jit(solution)/shard_map/ppermute | solution.py:686
  87.0 9.4 %collective-permute-start.14 = (f32[72,256]{1,0:T(8,128)S(1)}, f32[72,256]{1,0:T(8,128)S(1)}, u32[]{:S(2)}, u32[]{:S(2)}) collective-permute-start(f32[72,256]{1,0:T(8,128)S(1)} %add_add_fusion.2), channel_id=1, source_target_pairs={{0,96},{1,97},{2,98},{3,99},{4,100},{5,101},{6,102},{7,103},{8,104... | collective-permute-start | bytes 221192 | tf_op jit(solution)/shard_map/ppermute | solution.py:686
  90.0 6.4 %collective-permute-start.13 = (f32[72,256]{1,0:T(8,128)S(1)}, f32[72,256]{1,0:T(8,128)S(1)}, u32[]{:S(2)}, u32[]{:S(2)}) collective-permute-start(f32[72,256]{1,0:T(8,128)S(1)} %add_add_fusion.2), channel_id=1, source_target_pairs={{0,64},{1,65},{2,66},{3,67},{4,68},{5,69},{6,70},{7,71},{8,72},{9,... | collective-permute-start | bytes 221192 | tf_op jit(solution)/shard_map/ppermute | solution.py:686
  93.0 3.6 %collective-permute-start.12 = (f32[72,256]{1,0:T(8,128)S(1)}, f32[72,256]{1,0:T(8,128)S(1)}, u32[]{:S(2)}, u32[]{:S(2)}) collective-permute-start(f32[72,256]{1,0:T(8,128)S(1)} %add_add_fusion.2), channel_id=1, source_target_pairs={{0,32},{1,33},{2,34},{3,35},{4,36},{5,37},{6,38},{7,39},{8,40},{9,... | collective-permute-start | bytes 221192 | tf_op jit(solution)/shard_map/ppermute | solution.py:686
  96.3 12.0 %copy-start.9 = (bf16[64,2048]{1,0:T(8,128)(2,1)S(1)}, bf16[64,2048]{1,0:T(8,128)(2,1)}, u32[]{:S(2)}) copy-start(bf16[64,2048]{1,0:T(8,128)(2,1)} %copy-done.8) | copy-start | bytes 786436
  96.3 14.1 %copy-start.7 = (bf16[64,2048]{1,0:T(8,128)(2,1)S(1)}, bf16[64,2048]{1,0:T(8,128)(2,1)}, u32[]{:S(2)}) copy-start(bf16[64,2048]{1,0:T(8,128)(2,1)} %copy-done.6) | copy-start | bytes 786436
  96.3 28.0 %copy-start.5 = (bf16[64,2048]{1,0:T(8,128)(2,1)S(1)}, bf16[64,2048]{1,0:T(8,128)(2,1)}, u32[]{:S(2)}) copy-start(bf16[64,2048]{1,0:T(8,128)(2,1)} %copy-done.4) | copy-start | bytes 786436
  97.7 35.4 %all-to-all-start.2 = ((bf16[32,5,32,128]{3,2,1,0:T(8,128)(2,1)}), bf16[32,5,32,128]{3,2,1,0:T(8,128)(2,1)}, u32[]{:S(2)}, u32[]{:S(2)}) async-start(bf16[32,5,32,128]{3,2,1,0:T(8,128)(2,1)} %get-tuple-element.118), calls=%async_computation.2 | async-start | bytes 2621440 | tf_op jit(solution)/shard_map/all_to_all | solution.py:692
  105.0 19.3 %collective-permute-start.20 = (f32[72,256]{1,0:T(8,128)S(1)}, f32[72,256]{1,0:T(8,128)S(1)}, u32[]{:S(2)}, u32[]{:S(2)}) collective-permute-start(f32[72,256]{1,0:T(8,128)S(1)} %add_add_fusion.1), channel_id=1, source_target_pairs={{0,24},{1,25},{2,26},{3,27},{4,28},{5,29},{6,30},{7,31},{8,16},{9,... | collective-permute-start | bytes 221192 | tf_op jit(solution)/shard_map/ppermute | solution.py:686
  107.4 16.8 %collective-permute-start.19 = (f32[72,256]{1,0:T(8,128)S(1)}, f32[72,256]{1,0:T(8,128)S(1)}, u32[]{:S(2)}, u32[]{:S(2)}) collective-permute-start(f32[72,256]{1,0:T(8,128)S(1)} %add_add_fusion.1), channel_id=1, source_target_pairs={{0,16},{1,17},{2,18},{3,19},{4,20},{5,21},{6,22},{7,23},{8,24},{9,... | collective-permute-start | bytes 221192 | tf_op jit(solution)/shard_map/ppermute | solution.py:686
  108.0 16.3 %collective-permute-start.18 = (f32[72,256]{1,0:T(8,128)S(1)}, f32[72,256]{1,0:T(8,128)S(1)}, u32[]{:S(2)}, u32[]{:S(2)}) collective-permute-start(f32[72,256]{1,0:T(8,128)S(1)} %add_add_fusion.1), channel_id=1, source_target_pairs={{0,8},{1,9},{2,10},{3,11},{4,12},{5,13},{6,14},{7,15},{8,0},{9,1},... | collective-permute-start | bytes 221192 | tf_op jit(solution)/shard_map/ppermute | solution.py:686
  108.3 21.8 %collective-permute-start.22 = (bf16[64,2048]{1,0:T(8,128)(2,1)S(1)}, bf16[64,2048]{1,0:T(8,128)(2,1)S(1)}, u32[]{:S(2)}, u32[]{:S(2)}) collective-permute-start(bf16[64,2048]{1,0:T(8,128)(2,1)S(1)} %copy-done.9), channel_id=1, source_target_pairs={{0,2},{1,3},{2,0},{3,1},{4,6},{5,7},{6,4},{7,5},{8,10},{9,11},{10,... | collective-permute-start | bytes 786440 | tf_op jit(solution)/shard_map/ppermute | solution.py:686
  110.4 22.7 %collective-permute-start.23 = (bf16[64,2048]{1,0:T(8,128)(2,1)S(1)}, bf16[64,2048]{1,0:T(8,128)(2,1)S(1)}, u32[]{:S(2)}, u32[]{:S(2)}) collective-permute-start(bf16[64,2048]{1,0:T(8,128)(2,1)S(1)} %copy-done.7), channel_id=1, source_target_pairs={{0,3},{1,2},{2,1},{3,0},{4,7},{5,6},{6,5},{7,4},{8,11},{9,10},{10,... | collective-permute-start | bytes 786440 | tf_op jit(solution)/shard_map/ppermute | solution.py:686
  124.4 8.7 %collective-permute-start.21 = (bf16[64,2048]{1,0:T(8,128)(2,1)S(1)}, bf16[64,2048]{1,0:T(8,128)(2,1)}, u32[]{:S(2)}, u32[]{:S(2)}) collective-permute-start(bf16[64,2048]{1,0:T(8,128)(2,1)S(1)} %copy-done.5), channel_id=1, source_target_pairs={{0,1},{1,0},{2,3},{3,2},{4,5},{5,4},{6,7},{7,6},{8,9},{9,8},{10,11... | collective-permute-start | bytes 786440 | tf_op jit(solution)/shard_map/ppermute | solution.py:686
  125.8 12.1 %collective-permute-start.24 = (f32[72,256]{1,0:T(8,128)S(1)}, f32[72,256]{1,0:T(8,128)S(1)}, u32[]{:S(2)}, u32[]{:S(2)}) collective-permute-start(f32[72,256]{1,0:T(8,128)S(1)} %add_add_fusion.refs_0_), channel_id=1, source_target_pairs={{0,4},{1,5},{2,6},{3,7},{4,0},{5,1},{6,2},{7,3},{8,12},{9,13},{10,... | collective-permute-start | bytes 221192 | tf_op jit(solution)/shard_map/ppermute | solution.py:686
  (16 other events, 31.9 us)

commit v4 on v3

--- a/solution.py
+++ b/solution.py
@@ -37,7 +37,7 @@
     ]
     nbytes = sum(math.prod(x.shape) * x.dtype.itemsize for x in operands)
     kinds = [
-        pltpu.VMEM(shape, dtype) if p == "v" else jax.ShapeDtypeStruct(shape, dtype)
+        {"v": pltpu.VMEM, "h": pltpu.HBM}.get(p, jax.ShapeDtypeStruct)(shape, dtype)
         for p, (shape, dtype) in zip(outs, results, strict=True)
     ]
     return pl.pallas_call(
@@ -173,15 +173,17 @@
     held, self_ref, neigh_ref, bias_ref, sems, out_sems, more,
 ):
     cols, part = x_ref.shape[0], cot_ref.shape[0]
-    tall = cols + part
+    tall, rows = cols + part, x_ref.shape[1] // 4
     copies, sends = [], []
     for k, piece in enumerate((p0, p1, p2, p3)):
-        at = near_rows(place_ref[0], k, piece.shape[1])
+        at = near_rows(place_ref[0], k, rows)
         copies.append(
-            pltpu.make_async_copy(x_ref.at[:, at], held.at[k, 0:cols], sems.at[2 * k])
+            pltpu.make_async_copy(x_ref.at[:, at], held.at[k, 0:cols, 0:rows], sems.at[2 * k])
         )
         copies.append(
-            pltpu.make_async_copy(cot_ref.at[:, at], held.at[k, cols:tall], sems.at[2 * k + 1])
+            pltpu.make_async_copy(
+                cot_ref.at[:, at], held.at[k, cols:tall, 0:rows], sems.at[2 * k + 1]
+            )
         )
         sends.append(pltpu.make_async_copy(held.at[k], piece, out_sems.at[k]))
     small = [
@@ -208,12 +210,10 @@
     lines = jnp.where(row == 0, lines[0], jnp.where(row == 1, lines[1], lines[2]))
     lines = jnp.where(row < 3, lines, 0.0).astype(BF)
     for k in range(4):
-        held[k, tall:, :] = jnp.zeros((16, held.shape[2]), BF)
-        for g in range(cols // 16):
-            rows = slice(16 * g, 16 * g + 16)
-            held[k, tall:, 2 * g * hidden : (2 * g + 1) * hidden] = self_ref[rows, :]
-            held[k, tall:, (2 * g + 1) * hidden : (2 * g + 2) * hidden] = neigh_ref[rows, :]
-        held[k, tall:, cols // 8 * hidden : cols // 8 * hidden + part] = lines
+        held[k, 0:cols, rows:] = self_ref[...]
+        held[k, cols : 2 * cols, rows:] = neigh_ref[...]
+        held[k, 2 * cols :, rows:] = jnp.zeros((tall - 2 * cols, hidden), BF)
+        held[k, 2 * cols : 2 * cols + 16, rows : rows + part] = lines
     for k in (1, 2, 3, 0):
         copies[2 * k].wait()
         copies[2 * k + 1].wait()
@@ -223,7 +223,7 @@
 
 
 def by_device(place, x, cot, w_self, w_neigh, bias):
-    piece = (x.shape[0] + cot.shape[0] + 16, x.shape[1] // 4)
+    piece = (x.shape[0] + cot.shape[0], x.shape[1] // 4 + w_self.shape[1])
     return call(
         pieces_kernel,
         "by_device",
@@ -361,12 +361,10 @@
     )
     own, neigh = [], []
     for k, p in enumerate((p0, p1, p2, p3)):
-        rows = slice(cols + part, cols + part + 16)
-        for g in range(cols // 16):
-            own.append(p[rows, 2 * g * hidden : (2 * g + 1) * hidden])
-            neigh.append(p[rows, (2 * g + 1) * hidden : (2 * g + 2) * hidden])
-        start = cols // 8 * hidden
-        lines = p[rows, start : start + BLK].astype(F32)[:, 0:part]
+        start = p.shape[1] - hidden
+        own.append(p[0:cols, start:])
+        neigh.append(p[cols : 2 * cols, start:])
+        lines = p[2 * cols : 2 * cols + 16, start : start + BLK].astype(F32)[:, 0:part]
         line = (lines[0:1] + lines[1:2]) + lines[2:3]
         bias_ref[k * part : (k + 1) * part, :] = 0.5 * jnp.sum(
             jnp.where(eye, line, 0.0), axis=1, keepdims=True
@@ -467,7 +465,7 @@
     cols, rows = m0.shape
     part = grad_ref.shape[0] // 4
     grad = grad_ref[...]
-    left = [p[0:cols, :] for p in (p0, p1, p2, p3)] + [m[...] for m in (m0, m1, m2, m3)]
+    left = [p[0:cols, 0:rows] for p in (p0, p1, p2, p3)] + [m[...] for m in (m0, m1, m2, m3)]
     left.append(jnp.ones((ONES, rows), BF))
     total = dot(jnp.concatenate(left, axis=0), grad, NT)
     feat = feat_ref[0]
@@ -712,21 +710,19 @@
     backs = swapped(backs)
     terms = after(place, pieces, ms, grad)
     near = swapped(terms)
-    selfs = swapped([s0, s1, s2, s3])
+    selfs = [s0, s1, swap(s2, 2), swap(s3, 3)]
     outgoing, back = off_backward(place, off_row, key, backs, off, band_blocks, loop_size)
     grads = (near[0] + near[1]) + (near[2] + near[3])
     one, two, three = [swap(grads, 0, j) for j in (8, 16, 24)]
     outs = [h0, h1, h2, h3]
-    outgoing, back, one, two, three, selfs, outs = together(
-        (outgoing, back, one, two, three, selfs, outs)
-    )
+    grads = (grads + one) + (two + three)
+    outgoing, back, grads, selfs, outs = together((outgoing, back, grads, selfs, outs))
     incoming = spread(outgoing)
     outs = [outs[0], outs[1], swap(outs[2], 2), swap(outs[3], 3)]
     back_sum = band_backward(back, band_blocks)
-    grads = (grads + one) + (two + three)
     one, two, three = [swap(grads, 0, j) for j in (2, 4, 6)]
-    one, two, three, outs[1] = together((one, two, three, outs[1]))
-    outs[1] = swap(outs[1], 1)
+    one, two, three, outs[1], selfs[1] = together((one, two, three, outs[1], selfs[1]))
+    outs[1], selfs[1] = swap(outs[1], 1), swap(selfs[1], 1)
     grads = (grads + one) + (two + three)
     other = swap(grads, 0, 1)
     grad_features, hidden = collect(place, asked, back_sum, incoming, outs + selfs)

time: 139 us -> 136 us (0.978)
  the two profiles are of different devices: /device:TPU:1 before, /device:TPU:0 now
where the time goes in v4:
time: 136 us; the launch traced here: 134 us
  starting transfers between devices  52.4 us (39%)
  waiting for transfers between devices  44.6 us (33%)
  Pallas kernels  35.1 us (26%)
    pallas_call x12, Pallas kernels, call(): pl.pallas_call(kernel, in_specs=[pl.BlockSpec(memory_space=spaces[p]) for...  35.1 us
    ppermute x25, waiting for transfers between devices, swap(): return lax.ppermute(value, ('loop', 'feat'), pairs)  31.6 us
    ppermute x25, starting transfers between devices, swap(): return lax.ppermute(value, ('loop', 'feat'), pairs)  30.5 us
    all_to_all x3, starting transfers between devices, spread(): lax.all_to_all(value, 'loop', split_axis=0, concat_axis=0, tiled=True)  21.9 us
    all_to_all x3, waiting for transfers between devices, spread(): lax.all_to_all(value, 'loop', split_axis=0, concat_axis=0, tiled=True)  13 us
  transfers between devices with their start and end apart: 28, of which 11 were waited for; matrix products, arithmetic and copies ran while one was open for 0% of the time, Pallas kernels for 20%

profile of v4, /device:TPU:0, one launch (start us, length us, event | category | flops | bytes accessed | tf_op | source)
XLA Modules:
  0.0 134.0 jit_solution(16787225276526412136)
XLA Ops:
  0.7 1.8 %prepare.1 = (s32[1,64]{1,0:T(1,128)S(1)}, s32[32,1,128]{2,1,0:T(1,128)}) custom-call(s32[1,64]{1,0:T(1,128)} %bitcast.19, s32[1,64]{1,0:T(1,128)} %bitcast.20), custom_call_target="tpu_custom_call" | custom-call | flops 1 | bytes 1 | tf_op jit(solution)/shard_map/prepare/pallas_call | solution.py:43
  2.5 9.3 %all-to-all-start = ((s32[32,1,128]{2,1,0:T(1,128)}), s32[32,1,128]{2,1,0:T(1,128)S(1)}, u32[]{:S(2)}, u32[]{:S(2)}) async-start(s32[32,1,128]{2,1,0:T(1,128)} %get-tuple-element.73), calls=%async_computation | async-start | bytes 32768 | tf_op jit(solution)/shard_map/all_to_all | solution.py:690
  11.8 3.1 %by_device.1 = (bf16[96,2304]{1,0:T(8,128)(2,1)}, bf16[96,2304]{1,0:T(8,128)(2,1)}, bf16[96,2304]{1,0:T(8,128)(2,1)}, bf16[96,2304]{1,0:T(8,128)(2,1)}) custom-call(s32[2]{0:T(128)S(1)} %pad_add_fusion.place_ref.tie_ref.feat_ref, bf16[32,8192]{1,0:T(8,128)(2,1)} %bitcast.11, bf16[64,8192]{1,0:T(8,128)(2,1)} %bitcast.14, bf16[32,256]{1,0:T(8,128)(2,1)} %self_in.1, ...), custom_call_target="tpu_custom_call" | custom-call | flops 1 | bytes 1 | tf_op jit(solution)/shard_map/by_device/pallas_call | solution.py:43
  14.8 5.1 %all-to-all-done.asked_ref = s32[32,1,128]{2,1,0:T(1,128)S(1)} async-done(((s32[32,1,128]{2,1,0:T(1,128)}), s32[32,1,128]{2,1,0:T(1,128)S(1)}, u32[]{:S(2)}, u32[]{:S(2)}) %all-to-all-start) | async-done | bytes 16416 | tf_op jit(solution)/shard_map/all_to_all | solution.py:690
  19.9 2.8 %answers.1 = bf16[32,5,32,128]{3,2,1,0:T(8,128)(2,1)} custom-call(s32[2]{0:T(128)S(1)} %pad_add_fusion.place_ref.tie_ref.feat_ref, s32[32,1,128]{2,1,0:T(1,128)S(1)} %all-to-all-done.asked_ref, bf16[32,8192]{1,0:T(8,128)(2,1)} %bitcast.12), custom_call_target="tpu_custom_call" | custom-call | flops 1 | bytes 1 | tf_op jit(solution)/shard_map/answers/pallas_call | solution.py:43
  22.7 4.7 %all-to-all-start.1 = ((bf16[32,5,32,128]{3,2,1,0:T(8,128)(2,1)}), bf16[32,5,32,128]{3,2,1,0:T(8,128)(2,1)}, u32[]{:S(2)}, u32[]{:S(2)}) async-start(bf16[32,5,32,128]{3,2,1,0:T(8,128)(2,1)} %answers.1), calls=%async_computation.1 | async-start | bytes 2621440 | tf_op jit(solution)/shard_map/all_to_all | solution.py:690
  27.5 3.0 %collective-permute-start.1 = (bf16[96,2304]{1,0:T(8,128)(2,1)}, bf16[96,2304]{1,0:T(8,128)(2,1)S(1)}, u32[]{:S(2)}, u32[]{:S(2)}) collective-permute-start(bf16[96,2304]{1,0:T(8,128)(2,1)} %get-tuple-element.78), channel_id=1, source_target_pairs={{0,2},{1,3},{2,0},{3,1},{4,6},{5,7},{6,4},{7,5},{8,10},{9,11},{10,... | collective-permute-start | bytes 1327112 | tf_op jit(solution)/shard_map/ppermute | solution.py:684
  30.9 7.6 %band_forward.1 = (f32[48,8192]{1,0:T(8,128)}, bf16[64,128,128]{2,1,0:T(8,128)(2,1)S(1)}) custom-call(s32[2]{0:T(128)S(1)} %pad_add_fusion.place_ref.tie_ref.feat_ref, bf16[64,3,128,128]{3,2,1,0:T(8,128)(2,1)} %a_ref.3, bf16[64,128,128]{2,1,0:T(8,128)(2,1)} %off_ref.1, bf16[32,8192]{1,0:T(8,128)(2,1)} %bitcast.13), custom_call_target="tpu_custom_call" | custom-call | flops 1 | bytes 1 | tf_op jit(solution)/shard_map/band_forward/pallas_call | solution.py:43
  38.5 7.9 %all-to-all-done.1.panel_in = bf16[32,5,32,128]{3,2,1,0:T(8,128)(2,1)} async-done(((bf16[32,5,32,128]{3,2,1,0:T(8,128)(2,1)}), bf16[32,5,32,128]{3,2,1,0:T(8,128)(2,1)}, u32[]{:S(2)}, u32[]{:S(2)}) %all-to-all-start.1) | async-done | bytes 1310752 | tf_op jit(solution)/shard_map/all_to_all | solution.py:690
  46.5 4.1 %off_forward.1 = (bf16[32,2048]{1,0:T(8,128)(2,1)S(1)}, bf16[32,2048]{1,0:T(8,128)(2,1)S(1)}, bf16[32,2048]{1,0:T(8,128)(2,1)S(1)}, bf16[32,2048]{1,0:T(8,128)(2,1)S(1)}, f32[1,2048]{1,0:T(1,128)S(1)}) custom-call(s32[2]{0:T(128)S(1)} %pad_add_fusion.place_ref.tie_ref.feat_ref, s32[64]{0:T(128)S(1)} %copy-done.1, s32[1,64]{1,0:T(1,128)S(1)} %get-tuple-element.76.key_ref, ...), custom_call_target="tpu_custom_call" | custom-call | flops 1 | bytes 1 | tf_op jit(solution)/shard_map/off_forward/pallas_call | solution.py:43
  50.7 3.0 %collective-permute-start.4 = (bf16[32,2048]{1,0:T(8,128)(2,1)S(1)}, bf16[32,2048]{1,0:T(8,128)(2,1)S(1)}, u32[]{:S(2)}, u32[]{:S(2)}) collective-permute-start(bf16[32,2048]{1,0:T(8,128)(2,1)S(1)} %get-tuple-element.86), channel_id=1, source_target_pairs={{0,2},{1,3},{2,0},{3,1},{4,6},{5,7},{6,4},{7,5},{8,10},{9,11},{10,... | collective-permute-start | bytes 393224 | tf_op jit(solution)/shard_map/ppermute | solution.py:684
  54.8 6.2 %collective-permute-done.2.p3 = bf16[96,2304]{1,0:T(8,128)(2,1)S(1)} collective-permute-done((bf16[96,2304]{1,0:T(8,128)(2,1)}, bf16[96,2304]{1,0:T(8,128)(2,1)S(1)}, u32[]{:S(2)}, u32[]{:S(2)}) %collective-permute-start.2) | collective-permute-done | bytes 442400 | tf_op jit(solution)/shard_map/ppermute | solution.py:684
  61.7 5.0 %collective-permute-done.4.m2 = bf16[32,2048]{1,0:T(8,128)(2,1)S(1)} collective-permute-done((bf16[32,2048]{1,0:T(8,128)(2,1)S(1)}, bf16[32,2048]{1,0:T(8,128)(2,1)S(1)}, u32[]{:S(2)}, u32[]{:S(2)}) %collective-permute-start.4) | collective-permute-done | bytes 131104 | tf_op jit(solution)/shard_map/ppermute | solution.py:684
  66.8 2.4 %dense.1 = (bf16[32,2048]{1,0:T(8,128)(2,1)S(1)}, bf16[32,2048]{1,0:T(8,128)(2,1)S(1)}, bf16[32,2048]{1,0:T(8,128)(2,1)S(1)}, bf16[32,2048]{1,0:T(8,128)(2,1)S(1...) custom-call(bf16[96,2304]{1,0:T(8,128)(2,1)S(1)} %copy-done, ...), custom_call_target="tpu_custom_call" | custom-call | flops 1 | bytes 1 | tf_op jit(solution)/shard_map/dense/pallas_call | solution.py:43
  69.2 1.1 after.1
  70.3 1.3 collective-permute-start.9
  72.2 2.3 %collective-permute-start.11 = (f32[72,256]{1,0:T(8,128)S(1)}, f32[72,256]{1,0:T(8,128)S(1)}, u32[]{:S(2)}, u32[]{:S(2)}) collective-permute-start(f32[72,256]{1,0:T(8,128)S(1)} %get-tuple-element.107), channel_id=1, source_target_pairs={{0,3},{1,2},{2,1},{3,0},{4,7},{5,6},{6,5},{7,4},{8,11},{9,10},{10,... | collective-permute-start | bytes 221192 | tf_op jit(solution)/shard_map/ppermute | solution.py:684
  75.9 2.2 %collective-permute-start.8 = (bf16[32,2048]{1,0:T(8,128)(2,1)S(1)}, bf16[32,2048]{1,0:T(8,128)(2,1)S(1)}, u32[]{:S(2)}, u32[]{:S(2)}) collective-permute-start(bf16[32,2048]{1,0:T(8,128)(2,1)S(1)} %get-tuple-element.100), channel_id=1, source_target_pairs={{0,3},{1,2},{2,1},{3,0},{4,7},{5,6},{6,5},{7,4},{8,11},{9,10},{10,... | collective-permute-start | bytes 393224 | tf_op jit(solution)/shard_map/ppermute | solution.py:684
  78.3 2.6 %collective-permute-start.14 = (f32[72,256]{1,0:T(8,128)S(1)}, f32[72,256]{1,0:T(8,128)S(1)}, u32[]{:S(2)}, u32[]{:S(2)}) collective-permute-start(f32[72,256]{1,0:T(8,128)S(1)} %add_add_fusion.2), channel_id=1, source_target_pairs={{0,96},{1,97},{2,98},{3,99},{4,100},{5,101},{6,102},{7,103},{8,104... | collective-permute-start | bytes 221192 | tf_op jit(solution)/shard_map/ppermute | solution.py:684
  81.0 1.2 collective-permute-start.13
  83.1 2.3 %collective-permute-start.15 = (bf16[32,2048]{1,0:T(8,128)(2,1)S(1)}, bf16[32,2048]{1,0:T(8,128)(2,1)S(1)}, u32[]{:S(2)}, u32[]{:S(2)}) collective-permute-start(bf16[32,2048]{1,0:T(8,128)(2,1)S(1)} %copy-done.11), channel_id=1, source_target_pairs={{0,2},{1,3},{2,0},{3,1},{4,6},{5,7},{6,4},{7,5},{8,10},{9,11},{10,... | collective-permute-start | bytes 393224 | tf_op jit(solution)/shard_map/ppermute | solution.py:684
  85.4 1.1 collective-permute-start.16
  86.5 3.3 %off_backward.1 = (bf16[32,5,32,128]{3,2,1,0:T(8,128)(2,1)}, bf16[32,8192]{1,0:T(8,128)(2,1)S(1)}) custom-call(s32[2]{0:T(128)S(1)} %pad_add_fusion.place_ref.tie_ref.feat_ref, s32[64]{0:T(128)S(1)} %copy-done.1, s32[1,64]{1,0:T(1,128)S(1)} %get-tuple-element.76.key_ref, bf16[32,2048]{1,0:T(8,128)(2,1)S(1)} %get-tuple-element.97.b0, ...), custom_call_target="tpu_custom_call" | custom-call | flops 1 | bytes 1 | tf_op jit(solution)/shard_map/off_backward/pallas_call | solution.py:43
  89.9 2.5 %collective-permute-done.16.s3 = bf16[32,2048]{1,0:T(8,128)(2,1)S(1)} collective-permute-done((bf16[32,2048]{1,0:T(8,128)(2,1)S(1)}, bf16[32,2048]{1,0:T(8,128)(2,1)S(1)}, u32[]{:S(2)}, u32[]{:S(2)}) %collective-permute-start.16) | collective-permute-done | bytes 131104 | tf_op jit(solution)/shard_map/ppermute | solution.py:684
  92.4 8.0 %all-to-all-start.2 = ((bf16[32,5,32,128]{3,2,1,0:T(8,128)(2,1)}), bf16[32,5,32,128]{3,2,1,0:T(8,128)(2,1)}, u32[]{:S(2)}, u32[]{:S(2)}) async-start(bf16[32,5,32,128]{3,2,1,0:T(8,128)(2,1)} %get-tuple-element.117), calls=%async_computation.2 | async-start | bytes 2621440 | tf_op jit(solution)/shard_map/all_to_all | solution.py:690
  100.4 3.0 %collective-permute-start.19 = (f32[72,256]{1,0:T(8,128)S(1)}, f32[72,256]{1,0:T(8,128)S(1)}, u32[]{:S(2)}, u32[]{:S(2)}) collective-permute-start(f32[72,256]{1,0:T(8,128)S(1)} %add_add_fusion.1), channel_id=1, source_target_pairs={{0,24},{1,25},{2,26},{3,27},{4,28},{5,29},{6,30},{7,31},{8,16},{9,... | collective-permute-start | bytes 221192 | tf_op jit(solution)/shard_map/ppermute | solution.py:684
  104.5 1.9 %collective-permute-start.21 = (bf16[64,2048]{1,0:T(8,128)(2,1)}, bf16[64,2048]{1,0:T(8,128)(2,1)S(1)}, u32[]{:S(2)}, u32[]{:S(2)}) collective-permute-start(bf16[64,2048]{1,0:T(8,128)(2,1)} %get-tuple-element.123), channel_id=1, source_target_pairs={{0,2},{1,3},{2,0},{3,1},{4,6},{5,7},{6,4},{7,5},{8,10},{9,11},{10,... | collective-permute-start | bytes 786440 | tf_op jit(solution)/shard_map/ppermute | solution.py:684
  106.5 14.4 %collective-permute-done.19 = f32[72,256]{1,0:T(8,128)S(1)} collective-permute-done((f32[72,256]{1,0:T(8,128)S(1)}, f32[72,256]{1,0:T(8,128)S(1)}, u32[]{:S(2)}, u32[]{:S(2)}) %collective-permute-start.19) | collective-permute-done | bytes 73760 | tf_op jit(solution)/shard_map/ppermute | solution.py:684
  121.6 1.5 %collective-permute-start.24 = (f32[72,256]{1,0:T(8,128)S(1)}, f32[72,256]{1,0:T(8,128)S(1)}, u32[]{:S(2)}, u32[]{:S(2)}) collective-permute-start(f32[72,256]{1,0:T(8,128)S(1)} %add_add_fusion.refs_0_), channel_id=1, source_target_pairs={{0,4},{1,5},{2,6},{3,7},{4,0},{5,1},{6,2},{7,3},{8,12},{9,13},{10,... | collective-permute-start | bytes 221192 | tf_op jit(solution)/shard_map/ppermute | solution.py:684
  123.1 3.3 %band_backward.1.start_ref = f32[32,8192]{1,0:T(8,128)S(1)} custom-call(bf16[32,8192]{1,0:T(8,128)(2,1)S(1)} %get-tuple-element.116.back_ref, bf16[64,3,128,128]{3,2,1,0:T(8,128)(2,1)} %a_ref.3), custom_call_target="tpu_custom_call" | custom-call | flops 1 | bytes 1 | tf_op jit(solution)/shard_map/band_backward/pallas_call | solution.py:43
  126.5 1.9 %collective-permute-done.22.h3 = bf16[64,2048]{1,0:T(8,128)(2,1)S(1)} collective-permute-done((bf16[64,2048]{1,0:T(8,128)(2,1)}, bf16[64,2048]{1,0:T(8,128)(2,1)S(1)}, u32[]{:S(2)}, u32[]{:S(2)}) %collective-permute-start.22) | collective-permute-done | bytes 262176 | tf_op jit(solution)/shard_map/ppermute | solution.py:684
  129.2 4.2 %collect.1 = (bf16[32,8192]{1,0:T(8,128)(2,1)}, bf16[64,8192]{1,0:T(8,128)(2,1)}) custom-call(s32[2]{0:T(128)S(1)} %pad_add_fusion.place_ref.tie_ref.feat_ref, s32[32,1,128]{2,1,0:T(1,128)S(1)} %all-to-all-done.asked_ref, f32[32,8192]{1,0:T(8,128)S(1)} %band_backward.1.start_ref, bf16[32,5,32,128]{3,2,1,0:T(8,128)(2,1)} %all-to-all-done.2.in_ref, ...), custom_call_target="tpu_custom_call" | custom-call | flops 1 | bytes 1 | tf_op jit(solution)/shard_map/collect/pallas_call | solution.py:43
  (64 shorter events, 8.9 us)
Async XLA Ops:
  2.5 17.4 %all-to-all-start = ((s32[32,1,128]{2,1,0:T(1,128)}), s32[32,1,128]{2,1,0:T(1,128)S(1)}, u32[]{:S(2)}, u32[]{:S(2)}) async-start(s32[32,1,128]{2,1,0:T(1,128)} %get-tuple-element.73), calls=%async_computation | async-start | bytes 32768 | tf_op jit(solution)/shard_map/all_to_all | solution.py:690
  22.7 23.8 %all-to-all-start.1 = ((bf16[32,5,32,128]{3,2,1,0:T(8,128)(2,1)}), bf16[32,5,32,128]{3,2,1,0:T(8,128)(2,1)}, u32[]{:S(2)}, u32[]{:S(2)}) async-start(bf16[32,5,32,128]{3,2,1,0:T(8,128)(2,1)} %answers.1), calls=%async_computation.1 | async-start | bytes 2621440 | tf_op jit(solution)/shard_map/all_to_all | solution.py:690
  27.4 26.2 %collective-permute-start = (bf16[96,2304]{1,0:T(8,128)(2,1)}, bf16[96,2304]{1,0:T(8,128)(2,1)S(1)}, u32[]{:S(2)}, u32[]{:S(2)}) collective-permute-start(bf16[96,2304]{1,0:T(8,128)(2,1)} %get-tuple-element.77), channel_id=1, source_target_pairs={{0,1},{1,0},{2,3},{3,2},{4,5},{5,4},{6,7},{7,6},{8,9},{9,8},{10,11... | collective-permute-start | bytes 1327112 | tf_op jit(solution)/shard_map/ppermute | solution.py:684
  27.5 27.3 %collective-permute-start.1 = (bf16[96,2304]{1,0:T(8,128)(2,1)}, bf16[96,2304]{1,0:T(8,128)(2,1)S(1)}, u32[]{:S(2)}, u32[]{:S(2)}) collective-permute-start(bf16[96,2304]{1,0:T(8,128)(2,1)} %get-tuple-element.78), channel_id=1, source_target_pairs={{0,2},{1,3},{2,0},{3,1},{4,6},{5,7},{6,4},{7,5},{8,10},{9,11},{10,... | collective-permute-start | bytes 1327112 | tf_op jit(solution)/shard_map/ppermute | solution.py:684
  30.5 30.4 %collective-permute-start.2 = (bf16[96,2304]{1,0:T(8,128)(2,1)}, bf16[96,2304]{1,0:T(8,128)(2,1)S(1)}, u32[]{:S(2)}, u32[]{:S(2)}) collective-permute-start(bf16[96,2304]{1,0:T(8,128)(2,1)} %get-tuple-element.79), channel_id=1, source_target_pairs={{0,3},{1,2},{2,1},{3,0},{4,7},{5,6},{6,5},{7,4},{8,11},{9,10},{10,... | collective-permute-start | bytes 1327112 | tf_op jit(solution)/shard_map/ppermute | solution.py:684
  50.6 11.2 %collective-permute-start.3 = (bf16[32,2048]{1,0:T(8,128)(2,1)S(1)}, bf16[32,2048]{1,0:T(8,128)(2,1)S(1)}, u32[]{:S(2)}, u32[]{:S(2)}) collective-permute-start(bf16[32,2048]{1,0:T(8,128)(2,1)S(1)} %get-tuple-element.85), channel_id=1, source_target_pairs={{0,1},{1,0},{2,3},{3,2},{4,5},{5,4},{6,7},{7,6},{8,9},{9,8},{10,11... | collective-permute-start | bytes 393224 | tf_op jit(solution)/shard_map/ppermute | solution.py:684
  50.7 16.1 %collective-permute-start.4 = (bf16[32,2048]{1,0:T(8,128)(2,1)S(1)}, bf16[32,2048]{1,0:T(8,128)(2,1)S(1)}, u32[]{:S(2)}, u32[]{:S(2)}) collective-permute-start(bf16[32,2048]{1,0:T(8,128)(2,1)S(1)} %get-tuple-element.86), channel_id=1, source_target_pairs={{0,2},{1,3},{2,0},{3,1},{4,6},{5,7},{6,4},{7,5},{8,10},{9,11},{10,... | collective-permute-start | bytes 393224 | tf_op jit(solution)/shard_map/ppermute | solution.py:684
  53.6 13.1 %collective-permute-start.5 = (bf16[32,2048]{1,0:T(8,128)(2,1)S(1)}, bf16[32,2048]{1,0:T(8,128)(2,1)S(1)}, u32[]{:S(2)}, u32[]{:S(2)}) collective-permute-start(bf16[32,2048]{1,0:T(8,128)(2,1)S(1)} %get-tuple-element.87), channel_id=1, source_target_pairs={{0,3},{1,2},{2,1},{3,0},{4,7},{5,6},{6,5},{7,4},{8,11},{9,10},{10,... | collective-permute-start | bytes 393224 | tf_op jit(solution)/shard_map/ppermute | solution.py:684
  70.3 5.6 %collective-permute-start.9 = (f32[72,256]{1,0:T(8,128)S(1)}, f32[72,256]{1,0:T(8,128)S(1)}, u32[]{:S(2)}, u32[]{:S(2)}) collective-permute-start(f32[72,256]{1,0:T(8,128)S(1)} %get-tuple-element.105), channel_id=1, source_target_pairs={{0,1},{1,0},{2,3},{3,2},{4,5},{5,4},{6,7},{7,6},{8,9},{9,8},{10,11... | collective-permute-start | bytes 221192 | tf_op jit(solution)/shard_map/ppermute | solution.py:684
  71.6 6.6 %collective-permute-start.10 = (f32[72,256]{1,0:T(8,128)S(1)}, f32[72,256]{1,0:T(8,128)S(1)}, u32[]{:S(2)}, u32[]{:S(2)}) collective-permute-start(f32[72,256]{1,0:T(8,128)S(1)} %get-tuple-element.106), channel_id=1, source_target_pairs={{0,2},{1,3},{2,0},{3,1},{4,6},{5,7},{6,4},{7,5},{8,10},{9,11},{10,... | collective-permute-start | bytes 221192 | tf_op jit(solution)/shard_map/ppermute | solution.py:684
  72.2 6.1 %collective-permute-start.11 = (f32[72,256]{1,0:T(8,128)S(1)}, f32[72,256]{1,0:T(8,128)S(1)}, u32[]{:S(2)}, u32[]{:S(2)}) collective-permute-start(f32[72,256]{1,0:T(8,128)S(1)} %get-tuple-element.107), channel_id=1, source_target_pairs={{0,3},{1,2},{2,1},{3,0},{4,7},{5,6},{6,5},{7,4},{8,11},{9,10},{10,... | collective-permute-start | bytes 221192 | tf_op jit(solution)/shard_map/ppermute | solution.py:684
  74.5 7.6 %collective-permute-start.6 = (bf16[32,2048]{1,0:T(8,128)(2,1)S(1)}, bf16[32,2048]{1,0:T(8,128)(2,1)S(1)}, u32[]{:S(2)}, u32[]{:S(2)}) collective-permute-start(bf16[32,2048]{1,0:T(8,128)(2,1)S(1)} %get-tuple-element.98), channel_id=1, source_target_pairs={{0,1},{1,0},{2,3},{3,2},{4,5},{5,4},{6,7},{7,6},{8,9},{9,8},{10,11... | collective-permute-start | bytes 393224 | tf_op jit(solution)/shard_map/ppermute | solution.py:684
  75.2 7.9 %collective-permute-start.7 = (bf16[32,2048]{1,0:T(8,128)(2,1)S(1)}, bf16[32,2048]{1,0:T(8,128)(2,1)S(1)}, u32[]{:S(2)}, u32[]{:S(2)}) collective-permute-start(bf16[32,2048]{1,0:T(8,128)(2,1)S(1)} %get-tuple-element.99), channel_id=1, source_target_pairs={{0,2},{1,3},{2,0},{3,1},{4,6},{5,7},{6,4},{7,5},{8,10},{9,11},{10,... | collective-permute-start | bytes 393224 | tf_op jit(solution)/shard_map/ppermute | solution.py:684
  75.9 9.5 %collective-permute-start.8 = (bf16[32,2048]{1,0:T(8,128)(2,1)S(1)}, bf16[32,2048]{1,0:T(8,128)(2,1)S(1)}, u32[]{:S(2)}, u32[]{:S(2)}) collective-permute-start(bf16[32,2048]{1,0:T(8,128)(2,1)S(1)} %get-tuple-element.100), channel_id=1, source_target_pairs={{0,3},{1,2},{2,1},{3,0},{4,7},{5,6},{6,5},{7,4},{8,11},{9,10},{10,... | collective-permute-start | bytes 393224 | tf_op jit(solution)/shard_map/ppermute | solution.py:684
  78.3 11.5 %collective-permute-start.14 = (f32[72,256]{1,0:T(8,128)S(1)}, f32[72,256]{1,0:T(8,128)S(1)}, u32[]{:S(2)}, u32[]{:S(2)}) collective-permute-start(f32[72,256]{1,0:T(8,128)S(1)} %add_add_fusion.2), channel_id=1, source_target_pairs={{0,96},{1,97},{2,98},{3,99},{4,100},{5,101},{6,102},{7,103},{8,104... | collective-permute-start | bytes 221192 | tf_op jit(solution)/shard_map/ppermute | solution.py:684
  81.0 8.9 %collective-permute-start.13 = (f32[72,256]{1,0:T(8,128)S(1)}, f32[72,256]{1,0:T(8,128)S(1)}, u32[]{:S(2)}, u32[]{:S(2)}) collective-permute-start(f32[72,256]{1,0:T(8,128)S(1)} %add_add_fusion.2), channel_id=1, source_target_pairs={{0,64},{1,65},{2,66},{3,67},{4,68},{5,69},{6,70},{7,71},{8,72},{9,... | collective-permute-start | bytes 221192 | tf_op jit(solution)/shard_map/ppermute | solution.py:684
  82.2 7.7 %collective-permute-start.12 = (f32[72,256]{1,0:T(8,128)S(1)}, f32[72,256]{1,0:T(8,128)S(1)}, u32[]{:S(2)}, u32[]{:S(2)}) collective-permute-start(f32[72,256]{1,0:T(8,128)S(1)} %add_add_fusion.2), channel_id=1, source_target_pairs={{0,32},{1,33},{2,34},{3,35},{4,36},{5,37},{6,38},{7,39},{8,40},{9,... | collective-permute-start | bytes 221192 | tf_op jit(solution)/shard_map/ppermute | solution.py:684
  83.1 6.8 %collective-permute-start.15 = (bf16[32,2048]{1,0:T(8,128)(2,1)S(1)}, bf16[32,2048]{1,0:T(8,128)(2,1)S(1)}, u32[]{:S(2)}, u32[]{:S(2)}) collective-permute-start(bf16[32,2048]{1,0:T(8,128)(2,1)S(1)} %copy-done.11), channel_id=1, source_target_pairs={{0,2},{1,3},{2,0},{3,1},{4,6},{5,7},{6,4},{7,5},{8,10},{9,11},{10,... | collective-permute-start | bytes 393224 | tf_op jit(solution)/shard_map/ppermute | solution.py:684
  85.4 7.0 %collective-permute-start.16 = (bf16[32,2048]{1,0:T(8,128)(2,1)S(1)}, bf16[32,2048]{1,0:T(8,128)(2,1)S(1)}, u32[]{:S(2)}, u32[]{:S(2)}) collective-permute-start(bf16[32,2048]{1,0:T(8,128)(2,1)S(1)} %copy-done.10), channel_id=1, source_target_pairs={{0,3},{1,2},{2,1},{3,0},{4,7},{5,6},{6,5},{7,4},{8,11},{9,10},{10,... | collective-permute-start | bytes 393224 | tf_op jit(solution)/shard_map/ppermute | solution.py:684
  89.8 31.1 %copy-start.9 = (bf16[32,2048]{1,0:T(8,128)(2,1)S(1)}, bf16[32,2048]{1,0:T(8,128)(2,1)}, u32[]{:S(2)}) copy-start(bf16[32,2048]{1,0:T(8,128)(2,1)} %get-tuple-element.126) | copy-start | bytes 393220
  89.8 31.2 %copy-start.8 = (bf16[64,2048]{1,0:T(8,128)(2,1)S(1)}, bf16[64,2048]{1,0:T(8,128)(2,1)}, u32[]{:S(2)}) copy-start(bf16[64,2048]{1,0:T(8,128)(2,1)} %get-tuple-element.122) | copy-start | bytes 786436
  89.9 36.5 %copy-start.5 = (bf16[32,2048]{1,0:T(8,128)(2,1)}, bf16[32,2048]{1,0:T(8,128)(2,1)S(1)}, u32[]{:S(2)}) copy-start(bf16[32,2048]{1,0:T(8,128)(2,1)S(1)} %collective-permute-done.15.s2) | copy-start | bytes 393220
  92.4 34.0 %copy-start.6 = (bf16[32,2048]{1,0:T(8,128)(2,1)}, bf16[32,2048]{1,0:T(8,128)(2,1)S(1)}, u32[]{:S(2)}) copy-start(bf16[32,2048]{1,0:T(8,128)(2,1)S(1)} %collective-permute-done.16.s3) | copy-start | bytes 393220
  92.4 36.0 %all-to-all-start.2 = ((bf16[32,5,32,128]{3,2,1,0:T(8,128)(2,1)}), bf16[32,5,32,128]{3,2,1,0:T(8,128)(2,1)}, u32[]{:S(2)}, u32[]{:S(2)}) async-start(bf16[32,5,32,128]{3,2,1,0:T(8,128)(2,1)} %get-tuple-element.117), calls=%async_computation.2 | async-start | bytes 2621440 | tf_op jit(solution)/shard_map/all_to_all | solution.py:690
  100.4 20.6 %collective-permute-start.19 = (f32[72,256]{1,0:T(8,128)S(1)}, f32[72,256]{1,0:T(8,128)S(1)}, u32[]{:S(2)}, u32[]{:S(2)}) collective-permute-start(f32[72,256]{1,0:T(8,128)S(1)} %add_add_fusion.1), channel_id=1, source_target_pairs={{0,24},{1,25},{2,26},{3,27},{4,28},{5,29},{6,30},{7,31},{8,16},{9,... | collective-permute-start | bytes 221192 | tf_op jit(solution)/shard_map/ppermute | solution.py:684
  103.4 17.5 %collective-permute-start.18 = (f32[72,256]{1,0:T(8,128)S(1)}, f32[72,256]{1,0:T(8,128)S(1)}, u32[]{:S(2)}, u32[]{:S(2)}) collective-permute-start(f32[72,256]{1,0:T(8,128)S(1)} %add_add_fusion.1), channel_id=1, source_target_pairs={{0,16},{1,17},{2,18},{3,19},{4,20},{5,21},{6,22},{7,23},{8,24},{9,... | collective-permute-start | bytes 221192 | tf_op jit(solution)/shard_map/ppermute | solution.py:684
  104.2 16.7 %collective-permute-start.17 = (f32[72,256]{1,0:T(8,128)S(1)}, f32[72,256]{1,0:T(8,128)S(1)}, u32[]{:S(2)}, u32[]{:S(2)}) collective-permute-start(f32[72,256]{1,0:T(8,128)S(1)} %add_add_fusion.1), channel_id=1, source_target_pairs={{0,8},{1,9},{2,10},{3,11},{4,12},{5,13},{6,14},{7,15},{8,0},{9,1},... | collective-permute-start | bytes 221192 | tf_op jit(solution)/shard_map/ppermute | solution.py:684
  104.5 21.9 %collective-permute-start.21 = (bf16[64,2048]{1,0:T(8,128)(2,1)}, bf16[64,2048]{1,0:T(8,128)(2,1)S(1)}, u32[]{:S(2)}, u32[]{:S(2)}) collective-permute-start(bf16[64,2048]{1,0:T(8,128)(2,1)} %get-tuple-element.123), channel_id=1, source_target_pairs={{0,2},{1,3},{2,0},{3,1},{4,6},{5,7},{6,4},{7,5},{8,10},{9,11},{10,... | collective-permute-start | bytes 786440 | tf_op jit(solution)/shard_map/ppermute | solution.py:684
  106.5 21.9 %collective-permute-start.22 = (bf16[64,2048]{1,0:T(8,128)(2,1)}, bf16[64,2048]{1,0:T(8,128)(2,1)S(1)}, u32[]{:S(2)}, u32[]{:S(2)}) collective-permute-start(bf16[64,2048]{1,0:T(8,128)(2,1)} %get-tuple-element.124), channel_id=1, source_target_pairs={{0,3},{1,2},{2,1},{3,0},{4,7},{5,6},{6,5},{7,4},{8,11},{9,10},{10,... | collective-permute-start | bytes 786440 | tf_op jit(solution)/shard_map/ppermute | solution.py:684
  120.9 5.5 %collective-permute-start.23 = (bf16[32,2048]{1,0:T(8,128)(2,1)S(1)}, bf16[32,2048]{1,0:T(8,128)(2,1)S(1)}, u32[]{:S(2)}, u32[]{:S(2)}) collective-permute-start(bf16[32,2048]{1,0:T(8,128)(2,1)S(1)} %copy-done.9), channel_id=1, source_target_pairs={{0,1},{1,0},{2,3},{3,2},{4,5},{5,4},{6,7},{7,6},{8,9},{9,8},{10,11... | collective-permute-start | bytes 393224 | tf_op jit(solution)/shard_map/ppermute | solution.py:684
  121.0 7.4 %collective-permute-start.20 = (bf16[64,2048]{1,0:T(8,128)(2,1)S(1)}, bf16[64,2048]{1,0:T(8,128)(2,1)S(1)}, u32[]{:S(2)}, u32[]{:S(2)}) collective-permute-start(bf16[64,2048]{1,0:T(8,128)(2,1)S(1)} %copy-done.8), channel_id=1, source_target_pairs={{0,1},{1,0},{2,3},{3,2},{4,5},{5,4},{6,7},{7,6},{8,9},{9,8},{10,11... | collective-permute-start | bytes 786440 | tf_op jit(solution)/shard_map/ppermute | solution.py:684
  121.6 11.8 %collective-permute-start.24 = (f32[72,256]{1,0:T(8,128)S(1)}, f32[72,256]{1,0:T(8,128)S(1)}, u32[]{:S(2)}, u32[]{:S(2)}) collective-permute-start(f32[72,256]{1,0:T(8,128)S(1)} %add_add_fusion.refs_0_), channel_id=1, source_target_pairs={{0,4},{1,5},{2,6},{3,7},{4,0},{5,1},{6,2},{7,3},{8,12},{9,13},{10,... | collective-permute-start | bytes 221192 | tf_op jit(solution)/shard_map/ppermute | solution.py:684
  (8 other events, 66.0 us)

commit v5 on v4

--- a/solution.py
+++ b/solution.py
@@ -637,7 +637,7 @@
     return call(
         collect_kernel,
         "collect",
-        "saah" + 8 * "h" + ">wh",
+        "saahhahhhahh>wh",
         (place, asked, band_sum, incoming, *outs),
         ((band_sum.shape, BF), ((outs[0].shape[0], rows), BF)),
         scratch=[

time: 136 us -> 137 us (level)
  no operation moved by 1% of the time
where the time goes in v5:
time: 137 us; the launch traced here: 134 us
  starting transfers between devices  52.3 us (38%)
  waiting for transfers between devices  44.7 us (33%)
  Pallas kernels  35.1 us (26%)
    pallas_call x12, Pallas kernels, call(): pl.pallas_call(kernel, in_specs=[pl.BlockSpec(memory_space=spaces[p]) for...  35.1 us
    ppermute x25, waiting for transfers between devices, swap(): return lax.ppermute(value, ('loop', 'feat'), pairs)  31.7 us
    ppermute x25, starting transfers between devices, swap(): return lax.ppermute(value, ('loop', 'feat'), pairs)  30.4 us
    all_to_all x3, starting transfers between devices, spread(): lax.all_to_all(value, 'loop', split_axis=0, concat_axis=0, tiled=True)  21.9 us
    all_to_all x3, waiting for transfers between devices, spread(): lax.all_to_all(value, 'loop', split_axis=0, concat_axis=0, tiled=True)  13 us
  transfers between devices with their start and end apart: 28, of which 11 were waited for; matrix products, arithmetic and copies ran while one was open for 0% of the time, Pallas kernels for 20%

profile of v5, /device:TPU:0, one launch (start us, length us, event | category | flops | bytes accessed | tf_op | source)
XLA Modules:
  0.0 134.0 jit_solution(7441961952977592679)
XLA Ops:
  0.7 1.8 %prepare.1 = (s32[1,64]{1,0:T(1,128)S(1)}, s32[32,1,128]{2,1,0:T(1,128)}) custom-call(s32[1,64]{1,0:T(1,128)} %bitcast.19, s32[1,64]{1,0:T(1,128)} %bitcast.20), custom_call_target="tpu_custom_call" | custom-call | flops 1 | bytes 1 | tf_op jit(solution)/shard_map/prepare/pallas_call | solution.py:43
  2.5 9.3 %all-to-all-start = ((s32[32,1,128]{2,1,0:T(1,128)}), s32[32,1,128]{2,1,0:T(1,128)S(1)}, u32[]{:S(2)}, u32[]{:S(2)}) async-start(s32[32,1,128]{2,1,0:T(1,128)} %get-tuple-element.73), calls=%async_computation | async-start | bytes 32768 | tf_op jit(solution)/shard_map/all_to_all | solution.py:690
  11.8 3.1 %by_device.1 = (bf16[96,2304]{1,0:T(8,128)(2,1)}, bf16[96,2304]{1,0:T(8,128)(2,1)}, bf16[96,2304]{1,0:T(8,128)(2,1)}, bf16[96,2304]{1,0:T(8,128)(2,1)}) custom-call(s32[2]{0:T(128)S(1)} %pad_add_fusion.place_ref.tie_ref.feat_ref, bf16[32,8192]{1,0:T(8,128)(2,1)} %bitcast.11, bf16[64,8192]{1,0:T(8,128)(2,1)} %bitcast.14, bf16[32,256]{1,0:T(8,128)(2,1)} %self_in.1, ...), custom_call_target="tpu_custom_call" | custom-call | flops 1 | bytes 1 | tf_op jit(solution)/shard_map/by_device/pallas_call | solution.py:43
  14.8 5.1 %all-to-all-done.asked_ref = s32[32,1,128]{2,1,0:T(1,128)S(1)} async-done(((s32[32,1,128]{2,1,0:T(1,128)}), s32[32,1,128]{2,1,0:T(1,128)S(1)}, u32[]{:S(2)}, u32[]{:S(2)}) %all-to-all-start) | async-done | bytes 16416 | tf_op jit(solution)/shard_map/all_to_all | solution.py:690
  19.9 2.8 %answers.1 = bf16[32,5,32,128]{3,2,1,0:T(8,128)(2,1)} custom-call(s32[2]{0:T(128)S(1)} %pad_add_fusion.place_ref.tie_ref.feat_ref, s32[32,1,128]{2,1,0:T(1,128)S(1)} %all-to-all-done.asked_ref, bf16[32,8192]{1,0:T(8,128)(2,1)} %bitcast.12), custom_call_target="tpu_custom_call" | custom-call | flops 1 | bytes 1 | tf_op jit(solution)/shard_map/answers/pallas_call | solution.py:43
  22.7 4.7 %all-to-all-start.1 = ((bf16[32,5,32,128]{3,2,1,0:T(8,128)(2,1)}), bf16[32,5,32,128]{3,2,1,0:T(8,128)(2,1)}, u32[]{:S(2)}, u32[]{:S(2)}) async-start(bf16[32,5,32,128]{3,2,1,0:T(8,128)(2,1)} %answers.1), calls=%async_computation.1 | async-start | bytes 2621440 | tf_op jit(solution)/shard_map/all_to_all | solution.py:690
  27.5 3.0 %collective-permute-start.1 = (bf16[96,2304]{1,0:T(8,128)(2,1)}, bf16[96,2304]{1,0:T(8,128)(2,1)S(1)}, u32[]{:S(2)}, u32[]{:S(2)}) collective-permute-start(bf16[96,2304]{1,0:T(8,128)(2,1)} %get-tuple-element.78), channel_id=1, source_target_pairs={{0,2},{1,3},{2,0},{3,1},{4,6},{5,7},{6,4},{7,5},{8,10},{9,11},{10,... | collective-permute-start | bytes 1327112 | tf_op jit(solution)/shard_map/ppermute | solution.py:684
  30.9 7.6 %band_forward.1 = (f32[48,8192]{1,0:T(8,128)}, bf16[64,128,128]{2,1,0:T(8,128)(2,1)S(1)}) custom-call(s32[2]{0:T(128)S(1)} %pad_add_fusion.place_ref.tie_ref.feat_ref, bf16[64,3,128,128]{3,2,1,0:T(8,128)(2,1)} %a_ref.3, bf16[64,128,128]{2,1,0:T(8,128)(2,1)} %off_ref.1, bf16[32,8192]{1,0:T(8,128)(2,1)} %bitcast.13), custom_call_target="tpu_custom_call" | custom-call | flops 1 | bytes 1 | tf_op jit(solution)/shard_map/band_forward/pallas_call | solution.py:43
  38.5 7.9 %all-to-all-done.1.panel_in = bf16[32,5,32,128]{3,2,1,0:T(8,128)(2,1)} async-done(((bf16[32,5,32,128]{3,2,1,0:T(8,128)(2,1)}), bf16[32,5,32,128]{3,2,1,0:T(8,128)(2,1)}, u32[]{:S(2)}, u32[]{:S(2)}) %all-to-all-start.1) | async-done | bytes 1310752 | tf_op jit(solution)/shard_map/all_to_all | solution.py:690
  46.4 4.1 %off_forward.1 = (bf16[32,2048]{1,0:T(8,128)(2,1)S(1)}, bf16[32,2048]{1,0:T(8,128)(2,1)S(1)}, bf16[32,2048]{1,0:T(8,128)(2,1)S(1)}, bf16[32,2048]{1,0:T(8,128)(2,1)S(1)}, f32[1,2048]{1,0:T(1,128)S(1)}) custom-call(s32[2]{0:T(128)S(1)} %pad_add_fusion.place_ref.tie_ref.feat_ref, s32[64]{0:T(128)S(1)} %copy-done.1, s32[1,64]{1,0:T(1,128)S(1)} %get-tuple-element.76.key_ref, ...), custom_call_target="tpu_custom_call" | custom-call | flops 1 | bytes 1 | tf_op jit(solution)/shard_map/off_forward/pallas_call | solution.py:43
  50.7 3.0 %collective-permute-start.4 = (bf16[32,2048]{1,0:T(8,128)(2,1)S(1)}, bf16[32,2048]{1,0:T(8,128)(2,1)S(1)}, u32[]{:S(2)}, u32[]{:S(2)}) collective-permute-start(bf16[32,2048]{1,0:T(8,128)(2,1)S(1)} %get-tuple-element.86), channel_id=1, source_target_pairs={{0,2},{1,3},{2,0},{3,1},{4,6},{5,7},{6,4},{7,5},{8,10},{9,11},{10,... | collective-permute-start | bytes 393224 | tf_op jit(solution)/shard_map/ppermute | solution.py:684
  54.8 6.2 %collective-permute-done.2.p3 = bf16[96,2304]{1,0:T(8,128)(2,1)S(1)} collective-permute-done((bf16[96,2304]{1,0:T(8,128)(2,1)}, bf16[96,2304]{1,0:T(8,128)(2,1)S(1)}, u32[]{:S(2)}, u32[]{:S(2)}) %collective-permute-start.2) | collective-permute-done | bytes 442400 | tf_op jit(solution)/shard_map/ppermute | solution.py:684
  61.7 5.0 %collective-permute-done.4.m2 = bf16[32,2048]{1,0:T(8,128)(2,1)S(1)} collective-permute-done((bf16[32,2048]{1,0:T(8,128)(2,1)S(1)}, bf16[32,2048]{1,0:T(8,128)(2,1)S(1)}, u32[]{:S(2)}, u32[]{:S(2)}) %collective-permute-start.4) | collective-permute-done | bytes 131104 | tf_op jit(solution)/shard_map/ppermute | solution.py:684
  66.8 2.4 %dense.1 = (bf16[32,2048]{1,0:T(8,128)(2,1)S(1)}, bf16[32,2048]{1,0:T(8,128)(2,1)S(1)}, bf16[32,2048]{1,0:T(8,128)(2,1)S(1)}, bf16[32,2048]{1,0:T(8,128)(2,1)S(1...) custom-call(bf16[96,2304]{1,0:T(8,128)(2,1)S(1)} %copy-done, ...), custom_call_target="tpu_custom_call" | custom-call | flops 1 | bytes 1 | tf_op jit(solution)/shard_map/dense/pallas_call | solution.py:43
  69.2 1.1 after.1
  70.3 1.3 collective-permute-start.9
  72.2 2.3 %collective-permute-start.11 = (f32[72,256]{1,0:T(8,128)S(1)}, f32[72,256]{1,0:T(8,128)S(1)}, u32[]{:S(2)}, u32[]{:S(2)}) collective-permute-start(f32[72,256]{1,0:T(8,128)S(1)} %get-tuple-element.107), channel_id=1, source_target_pairs={{0,3},{1,2},{2,1},{3,0},{4,7},{5,6},{6,5},{7,4},{8,11},{9,10},{10,... | collective-permute-start | bytes 221192 | tf_op jit(solution)/shard_map/ppermute | solution.py:684
  75.9 2.2 %collective-permute-start.8 = (bf16[32,2048]{1,0:T(8,128)(2,1)S(1)}, bf16[32,2048]{1,0:T(8,128)(2,1)S(1)}, u32[]{:S(2)}, u32[]{:S(2)}) collective-permute-start(bf16[32,2048]{1,0:T(8,128)(2,1)S(1)} %get-tuple-element.100), channel_id=1, source_target_pairs={{0,3},{1,2},{2,1},{3,0},{4,7},{5,6},{6,5},{7,4},{8,11},{9,10},{10,... | collective-permute-start | bytes 393224 | tf_op jit(solution)/shard_map/ppermute | solution.py:684
  78.3 2.7 %collective-permute-start.14 = (f32[72,256]{1,0:T(8,128)S(1)}, f32[72,256]{1,0:T(8,128)S(1)}, u32[]{:S(2)}, u32[]{:S(2)}) collective-permute-start(f32[72,256]{1,0:T(8,128)S(1)} %add_add_fusion.2), channel_id=1, source_target_pairs={{0,96},{1,97},{2,98},{3,99},{4,100},{5,101},{6,102},{7,103},{8,104... | collective-permute-start | bytes 221192 | tf_op jit(solution)/shard_map/ppermute | solution.py:684
  81.0 1.2 collective-permute-start.13
  83.1 2.3 %collective-permute-start.15 = (bf16[32,2048]{1,0:T(8,128)(2,1)S(1)}, bf16[32,2048]{1,0:T(8,128)(2,1)S(1)}, u32[]{:S(2)}, u32[]{:S(2)}) collective-permute-start(bf16[32,2048]{1,0:T(8,128)(2,1)S(1)} %copy-done.8), channel_id=1, source_target_pairs={{0,2},{1,3},{2,0},{3,1},{4,6},{5,7},{6,4},{7,5},{8,10},{9,11},{10,... | collective-permute-start | bytes 393224 | tf_op jit(solution)/shard_map/ppermute | solution.py:684
  85.4 1.1 collective-permute-start.16
  86.5 3.3 %off_backward.1 = (bf16[32,5,32,128]{3,2,1,0:T(8,128)(2,1)}, bf16[32,8192]{1,0:T(8,128)(2,1)S(1)}) custom-call(s32[2]{0:T(128)S(1)} %pad_add_fusion.place_ref.tie_ref.feat_ref, s32[64]{0:T(128)S(1)} %copy-done.1, s32[1,64]{1,0:T(1,128)S(1)} %get-tuple-element.76.key_ref, bf16[32,2048]{1,0:T(8,128)(2,1)S(1)} %get-tuple-element.97.b0, ...), custom_call_target="tpu_custom_call" | custom-call | flops 1 | bytes 1 | tf_op jit(solution)/shard_map/off_backward/pallas_call | solution.py:43
  89.9 2.5 %collective-permute-done.16.s3 = bf16[32,2048]{1,0:T(8,128)(2,1)S(1)} collective-permute-done((bf16[32,2048]{1,0:T(8,128)(2,1)S(1)}, bf16[32,2048]{1,0:T(8,128)(2,1)S(1)}, u32[]{:S(2)}, u32[]{:S(2)}) %collective-permute-start.16) | collective-permute-done | bytes 131104 | tf_op jit(solution)/shard_map/ppermute | solution.py:684
  92.4 7.9 %all-to-all-start.2 = ((bf16[32,5,32,128]{3,2,1,0:T(8,128)(2,1)}), bf16[32,5,32,128]{3,2,1,0:T(8,128)(2,1)}, u32[]{:S(2)}, u32[]{:S(2)}) async-start(bf16[32,5,32,128]{3,2,1,0:T(8,128)(2,1)} %get-tuple-element.117), calls=%async_computation.2 | async-start | bytes 2621440 | tf_op jit(solution)/shard_map/all_to_all | solution.py:690
  100.4 3.0 %collective-permute-start.19 = (f32[72,256]{1,0:T(8,128)S(1)}, f32[72,256]{1,0:T(8,128)S(1)}, u32[]{:S(2)}, u32[]{:S(2)}) collective-permute-start(f32[72,256]{1,0:T(8,128)S(1)} %add_add_fusion.1), channel_id=1, source_target_pairs={{0,24},{1,25},{2,26},{3,27},{4,28},{5,29},{6,30},{7,31},{8,16},{9,... | collective-permute-start | bytes 221192 | tf_op jit(solution)/shard_map/ppermute | solution.py:684
  104.5 1.9 %collective-permute-start.21 = (bf16[64,2048]{1,0:T(8,128)(2,1)}, bf16[64,2048]{1,0:T(8,128)(2,1)S(1)}, u32[]{:S(2)}, u32[]{:S(2)}) collective-permute-start(bf16[64,2048]{1,0:T(8,128)(2,1)} %get-tuple-element.123), channel_id=1, source_target_pairs={{0,2},{1,3},{2,0},{3,1},{4,6},{5,7},{6,4},{7,5},{8,10},{9,11},{10,... | collective-permute-start | bytes 786440 | tf_op jit(solution)/shard_map/ppermute | solution.py:684
  106.5 14.4 %collective-permute-done.19 = f32[72,256]{1,0:T(8,128)S(1)} collective-permute-done((f32[72,256]{1,0:T(8,128)S(1)}, f32[72,256]{1,0:T(8,128)S(1)}, u32[]{:S(2)}, u32[]{:S(2)}) %collective-permute-start.19) | collective-permute-done | bytes 73760 | tf_op jit(solution)/shard_map/ppermute | solution.py:684
  121.5 1.5 %collective-permute-start.24 = (f32[72,256]{1,0:T(8,128)S(1)}, f32[72,256]{1,0:T(8,128)S(1)}, u32[]{:S(2)}, u32[]{:S(2)}) collective-permute-start(f32[72,256]{1,0:T(8,128)S(1)} %add_add_fusion.refs_0_), channel_id=1, source_target_pairs={{0,4},{1,5},{2,6},{3,7},{4,0},{5,1},{6,2},{7,3},{8,12},{9,13},{10,... | collective-permute-start | bytes 221192 | tf_op jit(solution)/shard_map/ppermute | solution.py:684
  123.0 3.3 %band_backward.1.start_ref = f32[32,8192]{1,0:T(8,128)S(1)} custom-call(bf16[32,8192]{1,0:T(8,128)(2,1)S(1)} %get-tuple-element.116.back_ref, bf16[64,3,128,128]{3,2,1,0:T(8,128)(2,1)} %a_ref.3), custom_call_target="tpu_custom_call" | custom-call | flops 1 | bytes 1 | tf_op jit(solution)/shard_map/band_backward/pallas_call | solution.py:43
  126.4 2.0 %collective-permute-done.22.h3 = bf16[64,2048]{1,0:T(8,128)(2,1)S(1)} collective-permute-done((bf16[64,2048]{1,0:T(8,128)(2,1)}, bf16[64,2048]{1,0:T(8,128)(2,1)S(1)}, u32[]{:S(2)}, u32[]{:S(2)}) %collective-permute-start.22) | collective-permute-done | bytes 262176 | tf_op jit(solution)/shard_map/ppermute | solution.py:684
  129.1 4.2 %collect.1 = (bf16[32,8192]{1,0:T(8,128)(2,1)}, bf16[64,8192]{1,0:T(8,128)(2,1)}) custom-call(s32[2]{0:T(128)S(1)} %pad_add_fusion.place_ref.tie_ref.feat_ref, s32[32,1,128]{2,1,0:T(1,128)S(1)} %all-to-all-done.asked_ref, f32[32,8192]{1,0:T(8,128)S(1)} %band_backward.1.start_ref, bf16[32,5,32,128]{3,2,1,0:T(8,128)(2,1)} %all-to-all-done.2.in_ref, ...), custom_call_target="tpu_custom_call" | custom-call | flops 1 | bytes 1 | tf_op jit(solution)/shard_map/collect/pallas_call | solution.py:43
  (58 shorter events, 8.8 us)
Async XLA Ops:
  2.5 17.4 %all-to-all-start = ((s32[32,1,128]{2,1,0:T(1,128)}), s32[32,1,128]{2,1,0:T(1,128)S(1)}, u32[]{:S(2)}, u32[]{:S(2)}) async-start(s32[32,1,128]{2,1,0:T(1,128)} %get-tuple-element.73), calls=%async_computation | async-start | bytes 32768 | tf_op jit(solution)/shard_map/all_to_all | solution.py:690
  22.7 23.7 %all-to-all-start.1 = ((bf16[32,5,32,128]{3,2,1,0:T(8,128)(2,1)}), bf16[32,5,32,128]{3,2,1,0:T(8,128)(2,1)}, u32[]{:S(2)}, u32[]{:S(2)}) async-start(bf16[32,5,32,128]{3,2,1,0:T(8,128)(2,1)} %answers.1), calls=%async_computation.1 | async-start | bytes 2621440 | tf_op jit(solution)/shard_map/all_to_all | solution.py:690
  27.4 26.2 %collective-permute-start = (bf16[96,2304]{1,0:T(8,128)(2,1)}, bf16[96,2304]{1,0:T(8,128)(2,1)S(1)}, u32[]{:S(2)}, u32[]{:S(2)}) collective-permute-start(bf16[96,2304]{1,0:T(8,128)(2,1)} %get-tuple-element.77), channel_id=1, source_target_pairs={{0,1},{1,0},{2,3},{3,2},{4,5},{5,4},{6,7},{7,6},{8,9},{9,8},{10,11... | collective-permute-start | bytes 1327112 | tf_op jit(solution)/shard_map/ppermute | solution.py:684
  27.5 27.3 %collective-permute-start.1 = (bf16[96,2304]{1,0:T(8,128)(2,1)}, bf16[96,2304]{1,0:T(8,128)(2,1)S(1)}, u32[]{:S(2)}, u32[]{:S(2)}) collective-permute-start(bf16[96,2304]{1,0:T(8,128)(2,1)} %get-tuple-element.78), channel_id=1, source_target_pairs={{0,2},{1,3},{2,0},{3,1},{4,6},{5,7},{6,4},{7,5},{8,10},{9,11},{10,... | collective-permute-start | bytes 1327112 | tf_op jit(solution)/shard_map/ppermute | solution.py:684
  30.5 30.4 %collective-permute-start.2 = (bf16[96,2304]{1,0:T(8,128)(2,1)}, bf16[96,2304]{1,0:T(8,128)(2,1)S(1)}, u32[]{:S(2)}, u32[]{:S(2)}) collective-permute-start(bf16[96,2304]{1,0:T(8,128)(2,1)} %get-tuple-element.79), channel_id=1, source_target_pairs={{0,3},{1,2},{2,1},{3,0},{4,7},{5,6},{6,5},{7,4},{8,11},{9,10},{10,... | collective-permute-start | bytes 1327112 | tf_op jit(solution)/shard_map/ppermute | solution.py:684
  50.6 11.2 %collective-permute-start.3 = (bf16[32,2048]{1,0:T(8,128)(2,1)S(1)}, bf16[32,2048]{1,0:T(8,128)(2,1)S(1)}, u32[]{:S(2)}, u32[]{:S(2)}) collective-permute-start(bf16[32,2048]{1,0:T(8,128)(2,1)S(1)} %get-tuple-element.85), channel_id=1, source_target_pairs={{0,1},{1,0},{2,3},{3,2},{4,5},{5,4},{6,7},{7,6},{8,9},{9,8},{10,11... | collective-permute-start | bytes 393224 | tf_op jit(solution)/shard_map/ppermute | solution.py:684
  50.7 16.1 %collective-permute-start.4 = (bf16[32,2048]{1,0:T(8,128)(2,1)S(1)}, bf16[32,2048]{1,0:T(8,128)(2,1)S(1)}, u32[]{:S(2)}, u32[]{:S(2)}) collective-permute-start(bf16[32,2048]{1,0:T(8,128)(2,1)S(1)} %get-tuple-element.86), channel_id=1, source_target_pairs={{0,2},{1,3},{2,0},{3,1},{4,6},{5,7},{6,4},{7,5},{8,10},{9,11},{10,... | collective-permute-start | bytes 393224 | tf_op jit(solution)/shard_map/ppermute | solution.py:684
  53.6 13.1 %collective-permute-start.5 = (bf16[32,2048]{1,0:T(8,128)(2,1)S(1)}, bf16[32,2048]{1,0:T(8,128)(2,1)S(1)}, u32[]{:S(2)}, u32[]{:S(2)}) collective-permute-start(bf16[32,2048]{1,0:T(8,128)(2,1)S(1)} %get-tuple-element.87), channel_id=1, source_target_pairs={{0,3},{1,2},{2,1},{3,0},{4,7},{5,6},{6,5},{7,4},{8,11},{9,10},{10,... | collective-permute-start | bytes 393224 | tf_op jit(solution)/shard_map/ppermute | solution.py:684
  69.2 16.2 %copy-start.7 = (bf16[32,2048]{1,0:T(8,128)(2,1)S(1)}, bf16[32,2048]{1,0:T(8,128)(2,1)}, u32[]{:S(2)}) copy-start(bf16[32,2048]{1,0:T(8,128)(2,1)} %get-tuple-element.111) | copy-start | bytes 393220
  70.3 5.6 %collective-permute-start.9 = (f32[72,256]{1,0:T(8,128)S(1)}, f32[72,256]{1,0:T(8,128)S(1)}, u32[]{:S(2)}, u32[]{:S(2)}) collective-permute-start(f32[72,256]{1,0:T(8,128)S(1)} %get-tuple-element.105), channel_id=1, source_target_pairs={{0,1},{1,0},{2,3},{3,2},{4,5},{5,4},{6,7},{7,6},{8,9},{9,8},{10,11... | collective-permute-start | bytes 221192 | tf_op jit(solution)/shard_map/ppermute | solution.py:684
  71.6 6.6 %collective-permute-start.10 = (f32[72,256]{1,0:T(8,128)S(1)}, f32[72,256]{1,0:T(8,128)S(1)}, u32[]{:S(2)}, u32[]{:S(2)}) collective-permute-start(f32[72,256]{1,0:T(8,128)S(1)} %get-tuple-element.106), channel_id=1, source_target_pairs={{0,2},{1,3},{2,0},{3,1},{4,6},{5,7},{6,4},{7,5},{8,10},{9,11},{10,... | collective-permute-start | bytes 221192 | tf_op jit(solution)/shard_map/ppermute | solution.py:684
  72.2 6.1 %collective-permute-start.11 = (f32[72,256]{1,0:T(8,128)S(1)}, f32[72,256]{1,0:T(8,128)S(1)}, u32[]{:S(2)}, u32[]{:S(2)}) collective-permute-start(f32[72,256]{1,0:T(8,128)S(1)} %get-tuple-element.107), channel_id=1, source_target_pairs={{0,3},{1,2},{2,1},{3,0},{4,7},{5,6},{6,5},{7,4},{8,11},{9,10},{10,... | collective-permute-start | bytes 221192 | tf_op jit(solution)/shard_map/ppermute | solution.py:684
  74.5 7.6 %collective-permute-start.6 = (bf16[32,2048]{1,0:T(8,128)(2,1)S(1)}, bf16[32,2048]{1,0:T(8,128)(2,1)S(1)}, u32[]{:S(2)}, u32[]{:S(2)}) collective-permute-start(bf16[32,2048]{1,0:T(8,128)(2,1)S(1)} %get-tuple-element.98), channel_id=1, source_target_pairs={{0,1},{1,0},{2,3},{3,2},{4,5},{5,4},{6,7},{7,6},{8,9},{9,8},{10,11... | collective-permute-start | bytes 393224 | tf_op jit(solution)/shard_map/ppermute | solution.py:684
  75.2 7.9 %collective-permute-start.7 = (bf16[32,2048]{1,0:T(8,128)(2,1)S(1)}, bf16[32,2048]{1,0:T(8,128)(2,1)S(1)}, u32[]{:S(2)}, u32[]{:S(2)}) collective-permute-start(bf16[32,2048]{1,0:T(8,128)(2,1)S(1)} %get-tuple-element.99), channel_id=1, source_target_pairs={{0,2},{1,3},{2,0},{3,1},{4,6},{5,7},{6,4},{7,5},{8,10},{9,11},{10,... | collective-permute-start | bytes 393224 | tf_op jit(solution)/shard_map/ppermute | solution.py:684
  75.9 9.5 %collective-permute-start.8 = (bf16[32,2048]{1,0:T(8,128)(2,1)S(1)}, bf16[32,2048]{1,0:T(8,128)(2,1)S(1)}, u32[]{:S(2)}, u32[]{:S(2)}) collective-permute-start(bf16[32,2048]{1,0:T(8,128)(2,1)S(1)} %get-tuple-element.100), channel_id=1, source_target_pairs={{0,3},{1,2},{2,1},{3,0},{4,7},{5,6},{6,5},{7,4},{8,11},{9,10},{10,... | collective-permute-start | bytes 393224 | tf_op jit(solution)/shard_map/ppermute | solution.py:684
  78.3 11.5 %collective-permute-start.14 = (f32[72,256]{1,0:T(8,128)S(1)}, f32[72,256]{1,0:T(8,128)S(1)}, u32[]{:S(2)}, u32[]{:S(2)}) collective-permute-start(f32[72,256]{1,0:T(8,128)S(1)} %add_add_fusion.2), channel_id=1, source_target_pairs={{0,96},{1,97},{2,98},{3,99},{4,100},{5,101},{6,102},{7,103},{8,104... | collective-permute-start | bytes 221192 | tf_op jit(solution)/shard_map/ppermute | solution.py:684
  81.0 8.9 %collective-permute-start.13 = (f32[72,256]{1,0:T(8,128)S(1)}, f32[72,256]{1,0:T(8,128)S(1)}, u32[]{:S(2)}, u32[]{:S(2)}) collective-permute-start(f32[72,256]{1,0:T(8,128)S(1)} %add_add_fusion.2), channel_id=1, source_target_pairs={{0,64},{1,65},{2,66},{3,67},{4,68},{5,69},{6,70},{7,71},{8,72},{9,... | collective-permute-start | bytes 221192 | tf_op jit(solution)/shard_map/ppermute | solution.py:684
  82.2 7.7 %collective-permute-start.12 = (f32[72,256]{1,0:T(8,128)S(1)}, f32[72,256]{1,0:T(8,128)S(1)}, u32[]{:S(2)}, u32[]{:S(2)}) collective-permute-start(f32[72,256]{1,0:T(8,128)S(1)} %add_add_fusion.2), channel_id=1, source_target_pairs={{0,32},{1,33},{2,34},{3,35},{4,36},{5,37},{6,38},{7,39},{8,40},{9,... | collective-permute-start | bytes 221192 | tf_op jit(solution)/shard_map/ppermute | solution.py:684
  83.1 6.8 %collective-permute-start.15 = (bf16[32,2048]{1,0:T(8,128)(2,1)S(1)}, bf16[32,2048]{1,0:T(8,128)(2,1)S(1)}, u32[]{:S(2)}, u32[]{:S(2)}) collective-permute-start(bf16[32,2048]{1,0:T(8,128)(2,1)S(1)} %copy-done.8), channel_id=1, source_target_pairs={{0,2},{1,3},{2,0},{3,1},{4,6},{5,7},{6,4},{7,5},{8,10},{9,11},{10,... | collective-permute-start | bytes 393224 | tf_op jit(solution)/shard_map/ppermute | solution.py:684
  85.4 7.0 %collective-permute-start.16 = (bf16[32,2048]{1,0:T(8,128)(2,1)S(1)}, bf16[32,2048]{1,0:T(8,128)(2,1)S(1)}, u32[]{:S(2)}, u32[]{:S(2)}) collective-permute-start(bf16[32,2048]{1,0:T(8,128)(2,1)S(1)} %copy-done.7), channel_id=1, source_target_pairs={{0,3},{1,2},{2,1},{3,0},{4,7},{5,6},{6,5},{7,4},{8,11},{9,10},{10,... | collective-permute-start | bytes 393224 | tf_op jit(solution)/shard_map/ppermute | solution.py:684
  89.8 31.1 %copy-start.6 = (bf16[64,2048]{1,0:T(8,128)(2,1)S(1)}, bf16[64,2048]{1,0:T(8,128)(2,1)}, u32[]{:S(2)}) copy-start(bf16[64,2048]{1,0:T(8,128)(2,1)} %get-tuple-element.122) | copy-start | bytes 786436
  89.9 36.4 %copy-start.4 = (bf16[32,2048]{1,0:T(8,128)(2,1)}, bf16[32,2048]{1,0:T(8,128)(2,1)S(1)}, u32[]{:S(2)}) copy-start(bf16[32,2048]{1,0:T(8,128)(2,1)S(1)} %collective-permute-done.15.s2) | copy-start | bytes 393220
  92.4 33.9 %copy-start.5 = (bf16[32,2048]{1,0:T(8,128)(2,1)}, bf16[32,2048]{1,0:T(8,128)(2,1)S(1)}, u32[]{:S(2)}) copy-start(bf16[32,2048]{1,0:T(8,128)(2,1)S(1)} %collective-permute-done.16.s3) | copy-start | bytes 393220
  92.4 36.0 %all-to-all-start.2 = ((bf16[32,5,32,128]{3,2,1,0:T(8,128)(2,1)}), bf16[32,5,32,128]{3,2,1,0:T(8,128)(2,1)}, u32[]{:S(2)}, u32[]{:S(2)}) async-start(bf16[32,5,32,128]{3,2,1,0:T(8,128)(2,1)} %get-tuple-element.117), calls=%async_computation.2 | async-start | bytes 2621440 | tf_op jit(solution)/shard_map/all_to_all | solution.py:690
  100.4 20.6 %collective-permute-start.19 = (f32[72,256]{1,0:T(8,128)S(1)}, f32[72,256]{1,0:T(8,128)S(1)}, u32[]{:S(2)}, u32[]{:S(2)}) collective-permute-start(f32[72,256]{1,0:T(8,128)S(1)} %add_add_fusion.1), channel_id=1, source_target_pairs={{0,24},{1,25},{2,26},{3,27},{4,28},{5,29},{6,30},{7,31},{8,16},{9,... | collective-permute-start | bytes 221192 | tf_op jit(solution)/shard_map/ppermute | solution.py:684
  103.4 17.5 %collective-permute-start.18 = (f32[72,256]{1,0:T(8,128)S(1)}, f32[72,256]{1,0:T(8,128)S(1)}, u32[]{:S(2)}, u32[]{:S(2)}) collective-permute-start(f32[72,256]{1,0:T(8,128)S(1)} %add_add_fusion.1), channel_id=1, source_target_pairs={{0,16},{1,17},{2,18},{3,19},{4,20},{5,21},{6,22},{7,23},{8,24},{9,... | collective-permute-start | bytes 221192 | tf_op jit(solution)/shard_map/ppermute | solution.py:684
  104.2 16.7 %collective-permute-start.17 = (f32[72,256]{1,0:T(8,128)S(1)}, f32[72,256]{1,0:T(8,128)S(1)}, u32[]{:S(2)}, u32[]{:S(2)}) collective-permute-start(f32[72,256]{1,0:T(8,128)S(1)} %add_add_fusion.1), channel_id=1, source_target_pairs={{0,8},{1,9},{2,10},{3,11},{4,12},{5,13},{6,14},{7,15},{8,0},{9,1},... | collective-permute-start | bytes 221192 | tf_op jit(solution)/shard_map/ppermute | solution.py:684
  104.5 21.8 %collective-permute-start.21 = (bf16[64,2048]{1,0:T(8,128)(2,1)}, bf16[64,2048]{1,0:T(8,128)(2,1)S(1)}, u32[]{:S(2)}, u32[]{:S(2)}) collective-permute-start(bf16[64,2048]{1,0:T(8,128)(2,1)} %get-tuple-element.123), channel_id=1, source_target_pairs={{0,2},{1,3},{2,0},{3,1},{4,6},{5,7},{6,4},{7,5},{8,10},{9,11},{10,... | collective-permute-start | bytes 786440 | tf_op jit(solution)/shard_map/ppermute | solution.py:684
  106.5 21.9 %collective-permute-start.22 = (bf16[64,2048]{1,0:T(8,128)(2,1)}, bf16[64,2048]{1,0:T(8,128)(2,1)S(1)}, u32[]{:S(2)}, u32[]{:S(2)}) collective-permute-start(bf16[64,2048]{1,0:T(8,128)(2,1)} %get-tuple-element.124), channel_id=1, source_target_pairs={{0,3},{1,2},{2,1},{3,0},{4,7},{5,6},{6,5},{7,4},{8,11},{9,10},{10,... | collective-permute-start | bytes 786440 | tf_op jit(solution)/shard_map/ppermute | solution.py:684
  120.9 5.4 %collective-permute-start.23 = (bf16[32,2048]{1,0:T(8,128)(2,1)}, bf16[32,2048]{1,0:T(8,128)(2,1)S(1)}, u32[]{:S(2)}, u32[]{:S(2)}) collective-permute-start(bf16[32,2048]{1,0:T(8,128)(2,1)} %get-tuple-element.126), channel_id=1, source_target_pairs={{0,1},{1,0},{2,3},{3,2},{4,5},{5,4},{6,7},{7,6},{8,9},{9,8},{10,11... | collective-permute-start | bytes 393224 | tf_op jit(solution)/shard_map/ppermute | solution.py:684
  120.9 7.4 %collective-permute-start.20 = (bf16[64,2048]{1,0:T(8,128)(2,1)S(1)}, bf16[64,2048]{1,0:T(8,128)(2,1)S(1)}, u32[]{:S(2)}, u32[]{:S(2)}) collective-permute-start(bf16[64,2048]{1,0:T(8,128)(2,1)S(1)} %copy-done.6), channel_id=1, source_target_pairs={{0,1},{1,0},{2,3},{3,2},{4,5},{5,4},{6,7},{7,6},{8,9},{9,8},{10,11... | collective-permute-start | bytes 786440 | tf_op jit(solution)/shard_map/ppermute | solution.py:684
  121.5 11.9 %collective-permute-start.24 = (f32[72,256]{1,0:T(8,128)S(1)}, f32[72,256]{1,0:T(8,128)S(1)}, u32[]{:S(2)}, u32[]{:S(2)}) collective-permute-start(f32[72,256]{1,0:T(8,128)S(1)} %add_add_fusion.refs_0_), channel_id=1, source_target_pairs={{0,4},{1,5},{2,6},{3,7},{4,0},{5,1},{6,2},{7,3},{8,12},{9,13},{10,... | collective-permute-start | bytes 221192 | tf_op jit(solution)/shard_map/ppermute | solution.py:684
  (5 other events, 47.1 us)
